TPU v7x, 32 devices: a whole 2x2x4 slice. The times are simulated.
32 devices in a mesh: dp: 8 (over y, x, core), leaf: 4 (over z).
Axes of the slice: x: 2, y: 2, z: 4, core: 2. Of those that a mesh axis runs over, the one named last changes fastest.
Arguments:
- predict: float32 [100, 262144], P(None, ('dp', 'leaf')), may hold values from -6 to 256
- labels: int32 [262144], P(('dp', 'leaf')), may hold values from 0 to 99
- leaf_ids: int32 [32, 262144], P(None, ('dp', 'leaf')), may hold values from 0 to 63
Outputs:
- new_predict: float32 [100, 262144], P(None, ('dp', 'leaf'))
- leaf_values: float32 [100, 2048], P(None, 'leaf')
All inputs are finite; a program needn't handle non-finite values.
Results may differ from a plain program's by a relative error of at most 0.0044.
Values sent between devices are 32-bit elements; how exact they have to be, the bound alone decides.
No kernel may reach another device: no remote copies, remote signals or barrier semaphores. Data moves between devices by JAX's collectives and lax.ppermute only.
A program may use at most 64 MiB of HBM per device.

v0:
```python
import jax
import jax.numpy as jnp
from jax import lax
from jax.sharding import PartitionSpec as P

LEAVES = 64


step_size = 0.5
ridge_term = 1.0


def gradients(predict, labels):
    row_max = jnp.max(predict, axis=0, keepdims=True)
    exponent = jnp.exp(predict - row_max)
    probability = exponent / jnp.sum(exponent, axis=0, keepdims=True)
    classes = lax.broadcasted_iota(jnp.int32, predict.shape, 0)
    targets = (classes == labels[None, :]).astype(jnp.float32)
    gradient = (probability - targets).astype(jnp.bfloat16)
    hessian = (probability * (1.0 - probability)).astype(jnp.bfloat16)
    return jnp.concatenate([gradient, hessian], axis=0)


def block_rows(row_count):
    return min(row_count, 1024)


def leaf_table(tree_ids, first_row, width):
    id_block = lax.dynamic_slice_in_dim(tree_ids, first_row, width, 1)
    leaf_slot = lax.broadcasted_iota(jnp.int32, (id_block.shape[0], LEAVES, width), 1)
    matches = id_block[:, None, :] == leaf_slot
    return matches.astype(jnp.bfloat16).reshape(id_block.shape[0] * LEAVES, width)


def local_sums(stacked, leaf_ids):
    row_count = stacked.shape[1]
    width = block_rows(row_count)
    initial = jnp.zeros((stacked.shape[0], leaf_ids.shape[0] * LEAVES), jnp.float32)

    def local_advance(counter, running):
        first_row = counter * width
        partial_value = lax.dynamic_slice_in_dim(stacked, first_row, width, 1)
        one_hot = leaf_table(leaf_ids, first_row, width)
        return running + lax.dot_general(
            partial_value, one_hot, (((1,), (1,)), ((), ())), preferred_element_type=jnp.float32
        )

    return lax.fori_loop(0, row_count // width, local_advance, initial)


def newton(totals):
    classes = totals.shape[0] // 2
    return -step_size * totals[:classes] / (totals[classes:] + ridge_term)


def apply_values(carried, values, tree_ids):
    row_count = tree_ids.shape[1]
    width = block_rows(row_count)
    high_part = values.astype(jnp.bfloat16)
    low_part = (values - high_part.astype(jnp.float32)).astype(jnp.bfloat16)

    def apply_advance(counter, running):
        first_row = counter * width
        one_hot = leaf_table(tree_ids, first_row, width)
        partial_value = jnp.dot(high_part, one_hot, preferred_element_type=jnp.float32)
        partial_value = partial_value + jnp.dot(
            low_part, one_hot, preferred_element_type=jnp.float32
        )
        previous = lax.dynamic_slice_in_dim(running, first_row, width, 1)
        return lax.dynamic_update_slice_in_dim(running, previous + partial_value, first_row, 1)

    return lax.fori_loop(0, row_count // width, apply_advance, carried)


def shards(predict, labels, leaf_ids):
    stacked = gradients(predict, labels)
    leaf_sums = local_sums(stacked, leaf_ids)
    initial = jnp.zeros(predict.shape, jnp.float32)
    own_sums = lax.psum_scatter(leaf_sums, "leaf", scatter_dimension=1, tiled=True)
    totals = lax.psum(own_sums, "dp")
    own_values = newton(totals)
    update = apply_values(initial, lax.all_gather(own_values, "leaf", axis=1, tiled=True), leaf_ids)
    return (predict + update, own_values)


def solution(mesh):
    return jax.shard_map(
        shards,
        mesh=mesh,
        in_specs=(P(None, ("dp", "leaf")), P(("dp", "leaf")), P(None, ("dp", "leaf"))),
        out_specs=(P(None, ("dp", "leaf")), P(None, "leaf")),
        check_vma=False,
    )
```

profile of v0, /device:TPU:1, one launch (start us, length us, event | category | flops | bytes accessed | tf_op | source)
XLA Modules:
  0.0 245.6 jit_solution(5277954720077888716)
XLA Ops:
  7.2 2.3 reduce_max.9
  10.9 1.3 subtract_convert_fusion
  12.2 2.2 pad_maximum_fusion
  14.4 51.0 %while.28 = (s32[]{:T(128)}, f32[200,2048]{1,0:T(8,128)}, bf16[200,8192]{1,0:T(8,128)(2,1)}, s32[32,8192]{1,0:T(8,128)}, s32[]{:T(128)}, /*index=5*/s32[]{:T(128)}, s32[]{:T(128)}, s32[]{:T(128)}) while((s32[]{:T(128)}, f32[200,2048]{1,0:T(8,128)}, bf16[200,8192]{1,0:T(8,128)(2,1)}, s32[32,8192]{1,0:T(8,128)}, s32[]{:T(128)}, ...), condition=%wide.region_3.0_spmd.clone, body=%wide.region_2.0_spmd.clone.sunk | while | flops 841777152 | bytes 21414100 | solution.py:48
  15.5 1.3 bitcast_compare_fusion.5
  16.9 2.7 %convolution_add_fusion.3 = f32[200,2048]{1,0:T(8,128)S(1)} fusion(pred[2048,1024]{1,0:T(32,128)(4,1)S(1)} %bitcast_compare_fusion.5, f32[200,2048]{1,0:T(8,128)S(1)} %copy-done.1, pred[]{:T(512)S(6)} %compare.3, bf16[200,8192]{1,0:T(8,128)(2,1)} %get-tuple-element.288, s32[]{:T(128)S(6)} %select_n.21), kind=kOutput, calls=%fused_computation.7.clone.1 | convolution fusion | flops 839680000 | bytes 5783557 | tf_op jit(solution)/shard_map/while/body/eval_jaxpr/dot_general | solution.py:44
  19.6 1.2 copy-done.2
  21.9 1.3 bitcast_compare_fusion.5
  23.2 2.7 %convolution_add_fusion.3 = f32[200,2048]{1,0:T(8,128)S(1)} fusion(pred[2048,1024]{1,0:T(32,128)(4,1)S(1)} %bitcast_compare_fusion.5, f32[200,2048]{1,0:T(8,128)S(1)} %copy-done.1, pred[]{:T(512)S(6)} %compare.3, bf16[200,8192]{1,0:T(8,128)(2,1)} %get-tuple-element.288, s32[]{:T(128)S(6)} %select_n.21), kind=kOutput, calls=%fused_computation.7.clone.1 | convolution fusion | flops 839680000 | bytes 5783557 | tf_op jit(solution)/shard_map/while/body/eval_jaxpr/dot_general | solution.py:44
  28.3 1.3 bitcast_compare_fusion.5
  29.6 2.7 %convolution_add_fusion.3 = f32[200,2048]{1,0:T(8,128)S(1)} fusion(pred[2048,1024]{1,0:T(32,128)(4,1)S(1)} %bitcast_compare_fusion.5, f32[200,2048]{1,0:T(8,128)S(1)} %copy-done.1, pred[]{:T(512)S(6)} %compare.3, bf16[200,8192]{1,0:T(8,128)(2,1)} %get-tuple-element.288, s32[]{:T(128)S(6)} %select_n.21), kind=kOutput, calls=%fused_computation.7.clone.1 | convolution fusion | flops 839680000 | bytes 5783557 | tf_op jit(solution)/shard_map/while/body/eval_jaxpr/dot_general | solution.py:44
  32.3 1.2 copy-done.2
  34.6 1.3 bitcast_compare_fusion.5
  36.0 2.7 %convolution_add_fusion.3 = f32[200,2048]{1,0:T(8,128)S(1)} fusion(pred[2048,1024]{1,0:T(32,128)(4,1)S(1)} %bitcast_compare_fusion.5, f32[200,2048]{1,0:T(8,128)S(1)} %copy-done.1, pred[]{:T(512)S(6)} %compare.3, bf16[200,8192]{1,0:T(8,128)(2,1)} %get-tuple-element.288, s32[]{:T(128)S(6)} %select_n.21), kind=kOutput, calls=%fused_computation.7.clone.1 | convolution fusion | flops 839680000 | bytes 5783557 | tf_op jit(solution)/shard_map/while/body/eval_jaxpr/dot_general | solution.py:44
  38.7 1.2 copy-done.2
  41.0 1.3 bitcast_compare_fusion.5
  42.4 2.7 %convolution_add_fusion.3 = f32[200,2048]{1,0:T(8,128)S(1)} fusion(pred[2048,1024]{1,0:T(32,128)(4,1)S(1)} %bitcast_compare_fusion.5, f32[200,2048]{1,0:T(8,128)S(1)} %copy-done.1, pred[]{:T(512)S(6)} %compare.3, bf16[200,8192]{1,0:T(8,128)(2,1)} %get-tuple-element.288, s32[]{:T(128)S(6)} %select_n.21), kind=kOutput, calls=%fused_computation.7.clone.1 | convolution fusion | flops 839680000 | bytes 5783557 | tf_op jit(solution)/shard_map/while/body/eval_jaxpr/dot_general | solution.py:44
  45.1 1.2 copy-done.2
  47.4 1.3 bitcast_compare_fusion.5
  48.7 2.7 %convolution_add_fusion.3 = f32[200,2048]{1,0:T(8,128)S(1)} fusion(pred[2048,1024]{1,0:T(32,128)(4,1)S(1)} %bitcast_compare_fusion.5, f32[200,2048]{1,0:T(8,128)S(1)} %copy-done.1, pred[]{:T(512)S(6)} %compare.3, bf16[200,8192]{1,0:T(8,128)(2,1)} %get-tuple-element.288, s32[]{:T(128)S(6)} %select_n.21), kind=kOutput, calls=%fused_computation.7.clone.1 | convolution fusion | flops 839680000 | bytes 5783557 | tf_op jit(solution)/shard_map/while/body/eval_jaxpr/dot_general | solution.py:44
  51.5 1.2 copy-done.2
  53.8 1.3 bitcast_compare_fusion.5
  55.1 2.7 %convolution_add_fusion.3 = f32[200,2048]{1,0:T(8,128)S(1)} fusion(pred[2048,1024]{1,0:T(32,128)(4,1)S(1)} %bitcast_compare_fusion.5, f32[200,2048]{1,0:T(8,128)S(1)} %copy-done.1, pred[]{:T(512)S(6)} %compare.3, bf16[200,8192]{1,0:T(8,128)(2,1)} %get-tuple-element.288, s32[]{:T(128)S(6)} %select_n.21), kind=kOutput, calls=%fused_computation.7.clone.1 | convolution fusion | flops 839680000 | bytes 5783557 | tf_op jit(solution)/shard_map/while/body/eval_jaxpr/dot_general | solution.py:44
  57.8 1.2 copy-done.2
  60.1 1.3 bitcast_compare_fusion.5
  61.5 2.7 %convolution_add_fusion.3 = f32[200,2048]{1,0:T(8,128)S(1)} fusion(pred[2048,1024]{1,0:T(32,128)(4,1)S(1)} %bitcast_compare_fusion.5, f32[200,2048]{1,0:T(8,128)S(1)} %copy-done.1, pred[]{:T(512)S(6)} %compare.3, bf16[200,8192]{1,0:T(8,128)(2,1)} %get-tuple-element.288, s32[]{:T(128)S(6)} %select_n.21), kind=kOutput, calls=%fused_computation.7.clone.1 | convolution fusion | flops 839680000 | bytes 5783557 | tf_op jit(solution)/shard_map/while/body/eval_jaxpr/dot_general | solution.py:44
  65.5 38.3 %reduce-scatter.2.cloned.1.call-done = f32[200,512]{1,0:T(8,128)} async-done(((f32[200,2048]{1,0:T(8,128)}), f32[200,512]{1,0:T(8,128)}) %reduce-scatter.2.cloned.1.call-update) | async-done | bytes 409616 | tf_op jit(solution)/shard_map/reduce_scatter | solution.py:79
  103.8 56.1 %all-reduce.2.cloned.1.call-done = f32[200,512]{1,0:T(8,128)} async-done(((f32[200,512]{1,0:T(8,128)}), f32[200,512]{1,0:T(8,128)}) %all-reduce.2.cloned.1.call-update) | async-done | bytes 409616 | tf_op jit(solution)/shard_map/psum | solution.py:80
  161.7 17.6 %all_gather.3 = f32[100,2048]{1,0:T(8,128)S(1)} all-gather(f32[100,512]{1,0:T(8,128)S(1)} %fusion.8), channel_id=1, replica_groups=mesh['dp'=8,'leaf'=4] {'leaf'}, dimensions={1}, use_global_device_ids=true | all-gather | bytes 1024000 | tf_op jit(solution)/shard_map/all_gather | solution.py:82
  180.3 2.1 broadcast_in_dim.15
  182.4 52.3 %while.27 = (s32[]{:T(128)}, f32[100,8192]{1,0:T(8,128)}, s32[32,8192]{1,0:T(8,128)}, bf16[100,2048]{1,0:T(8,128)(2,1)}, bf16[100,2048]{1,0:T(8,128)(2,1)}, /*index=5*/s32[]{:T(128)}, s32[]{:T(128)}, s32[]{:T(128)}, s32[]{:T(128)}) while((s32[]{:T(128)}, f32[100,8192]{1,0:T(8,128)}, s32[32,8192]{1,0:T(8,128)}, bf16[100,2048]{1,0:T(8,128)(2,1)}, ...), condition=%wide.region_7.0_spmd, body=%wide.region_6.0_spmd.sunk | while | flops 841162752 | bytes 12484811 | solution.py:72
  183.4 1.3 bitcast_compare_fusion.4
  185.9 2.9 %fusion.28 = f32[100,8192]{1,0:T(8,128)} fusion(f32[100,8192]{1,0:T(8,128)} %get-tuple-element.304, s32[]{:T(128)S(6)} %select_n.20, f32[1024,100]{0,1:T(8,128)S(1)} %fusion.27, pred[2048,1024]{1,0:T(32,128)(4,1)S(1)} %bitcast_compare_fusion.4, bf16[100,2048]{1,0:T(8,128)(2,1)S(1)} %copy-done.4), kind=kOutput, calls=%fused_computation.4.clone.1 | convolution fusion | flops 419635200 | bytes 3768324 | tf_op jit(solution)/shard_map/while/body/eval_jaxpr/dot_general | solution.py:66
  189.9 1.3 bitcast_compare_fusion.4
  192.5 2.9 %fusion.28 = f32[100,8192]{1,0:T(8,128)} fusion(f32[100,8192]{1,0:T(8,128)} %get-tuple-element.304, s32[]{:T(128)S(6)} %select_n.20, f32[1024,100]{0,1:T(8,128)S(1)} %fusion.27, pred[2048,1024]{1,0:T(32,128)(4,1)S(1)} %bitcast_compare_fusion.4, bf16[100,2048]{1,0:T(8,128)(2,1)S(1)} %copy-done.4), kind=kOutput, calls=%fused_computation.4.clone.1 | convolution fusion | flops 419635200 | bytes 3768324 | tf_op jit(solution)/shard_map/while/body/eval_jaxpr/dot_general | solution.py:66
  196.5 1.3 bitcast_compare_fusion.4
  199.0 2.9 %fusion.28 = f32[100,8192]{1,0:T(8,128)} fusion(f32[100,8192]{1,0:T(8,128)} %get-tuple-element.304, s32[]{:T(128)S(6)} %select_n.20, f32[1024,100]{0,1:T(8,128)S(1)} %fusion.27, pred[2048,1024]{1,0:T(32,128)(4,1)S(1)} %bitcast_compare_fusion.4, bf16[100,2048]{1,0:T(8,128)(2,1)S(1)} %copy-done.4), kind=kOutput, calls=%fused_computation.4.clone.1 | convolution fusion | flops 419635200 | bytes 3768324 | tf_op jit(solution)/shard_map/while/body/eval_jaxpr/dot_general | solution.py:66
  203.0 1.3 bitcast_compare_fusion.4
  205.6 2.9 %fusion.28 = f32[100,8192]{1,0:T(8,128)} fusion(f32[100,8192]{1,0:T(8,128)} %get-tuple-element.304, s32[]{:T(128)S(6)} %select_n.20, f32[1024,100]{0,1:T(8,128)S(1)} %fusion.27, pred[2048,1024]{1,0:T(32,128)(4,1)S(1)} %bitcast_compare_fusion.4, bf16[100,2048]{1,0:T(8,128)(2,1)S(1)} %copy-done.4), kind=kOutput, calls=%fused_computation.4.clone.1 | convolution fusion | flops 419635200 | bytes 3768324 | tf_op jit(solution)/shard_map/while/body/eval_jaxpr/dot_general | solution.py:66
  209.5 1.3 bitcast_compare_fusion.4
  212.1 2.9 %fusion.28 = f32[100,8192]{1,0:T(8,128)} fusion(f32[100,8192]{1,0:T(8,128)} %get-tuple-element.304, s32[]{:T(128)S(6)} %select_n.20, f32[1024,100]{0,1:T(8,128)S(1)} %fusion.27, pred[2048,1024]{1,0:T(32,128)(4,1)S(1)} %bitcast_compare_fusion.4, bf16[100,2048]{1,0:T(8,128)(2,1)S(1)} %copy-done.4), kind=kOutput, calls=%fused_computation.4.clone.1 | convolution fusion | flops 419635200 | bytes 3768324 | tf_op jit(solution)/shard_map/while/body/eval_jaxpr/dot_general | solution.py:66
  216.1 1.3 bitcast_compare_fusion.4
  218.6 2.9 %fusion.28 = f32[100,8192]{1,0:T(8,128)} fusion(f32[100,8192]{1,0:T(8,128)} %get-tuple-element.304, s32[]{:T(128)S(6)} %select_n.20, f32[1024,100]{0,1:T(8,128)S(1)} %fusion.27, pred[2048,1024]{1,0:T(32,128)(4,1)S(1)} %bitcast_compare_fusion.4, bf16[100,2048]{1,0:T(8,128)(2,1)S(1)} %copy-done.4), kind=kOutput, calls=%fused_computation.4.clone.1 | convolution fusion | flops 419635200 | bytes 3768324 | tf_op jit(solution)/shard_map/while/body/eval_jaxpr/dot_general | solution.py:66
  222.6 1.3 bitcast_compare_fusion.4
  225.2 2.9 %fusion.28 = f32[100,8192]{1,0:T(8,128)} fusion(f32[100,8192]{1,0:T(8,128)} %get-tuple-element.304, s32[]{:T(128)S(6)} %select_n.20, f32[1024,100]{0,1:T(8,128)S(1)} %fusion.27, pred[2048,1024]{1,0:T(32,128)(4,1)S(1)} %bitcast_compare_fusion.4, bf16[100,2048]{1,0:T(8,128)(2,1)S(1)} %copy-done.4), kind=kOutput, calls=%fused_computation.4.clone.1 | convolution fusion | flops 419635200 | bytes 3768324 | tf_op jit(solution)/shard_map/while/body/eval_jaxpr/dot_general | solution.py:66
  229.1 1.3 bitcast_compare_fusion.4
  231.7 2.9 %fusion.28 = f32[100,8192]{1,0:T(8,128)} fusion(f32[100,8192]{1,0:T(8,128)} %get-tuple-element.304, s32[]{:T(128)S(6)} %select_n.20, f32[1024,100]{0,1:T(8,128)S(1)} %fusion.27, pred[2048,1024]{1,0:T(32,128)(4,1)S(1)} %bitcast_compare_fusion.4, bf16[100,2048]{1,0:T(8,128)(2,1)S(1)} %copy-done.4), kind=kOutput, calls=%fused_computation.4.clone.1 | convolution fusion | flops 419635200 | bytes 3768324 | tf_op jit(solution)/shard_map/while/body/eval_jaxpr/dot_general | solution.py:66
  234.6 4.1 %add.88 = f32[100,8192]{1,0:T(8,128)} add(f32[100,8192]{1,0:T(8,128)S(1)} %copy-done, f32[100,8192]{1,0:T(8,128)} %get-tuple-element.176) | non-fusion elementwise | flops 819200 | bytes 9830400 | tf_op jit(solution)/shard_map/add | solution.py:83
  (128 shorter events, 33.2 us)
Async XLA Ops:
  7.2 3.0 %copy-start = (f32[100,8192]{1,0:T(8,128)S(1)}, f32[100,8192]{1,0:T(8,128)}, u32[]{:S(2)}) copy-start(f32[100,8192]{1,0:T(8,128)} %param.7) | copy-start | bytes 9830404
  7.2 96.6 %reduce-scatter.2.cloned.1.call-start = ((), (), s32[]{:S(2)}) async-start(), calls=%async_computation.1 | async-start | bytes 2048000 | tf_op jit(solution)/shard_map/reduce_scatter | solution.py:79
  10.2 0.8 copy-start.6
  14.5 2.4 copy-start.1
  19.6 1.2 copy-start.2
  20.8 2.4 copy-start.1
  26.0 1.2 copy-start.2
  27.2 2.4 copy-start.1
  32.3 1.2 copy-start.2
  33.6 2.4 copy-start.1
  38.7 1.2 copy-start.2
  40.0 2.4 copy-start.1
  45.1 1.2 copy-start.2
  46.3 2.4 copy-start.1
  51.5 1.2 copy-start.2
  52.7 2.4 copy-start.1
  57.8 1.2 copy-start.2
  59.1 2.4 copy-start.1
  64.2 1.2 copy-start.2
  65.4 94.5 %all-reduce.2.cloned.1.call-start = ((), (), s32[]{:S(2)}) async-start(), calls=%async_computation.2 | async-start | bytes 819200 | tf_op jit(solution)/shard_map/psum | solution.py:80
  161.0 0.7 copy-start.3
  182.4 2.3 copy-start.5
  184.8 1.2 copy-start.4
  189.0 2.3 copy-start.5
  191.3 1.2 copy-start.4
  195.5 2.3 copy-start.5
  197.8 1.2 copy-start.4
  202.0 2.3 copy-start.5
  204.4 1.2 copy-start.4
  208.6 2.3 copy-start.5
  210.9 1.2 copy-start.4
  215.1 2.3 copy-start.5
  217.4 1.2 copy-start.4
  221.6 2.3 copy-start.5
  224.0 1.2 copy-start.4
  228.2 2.3 copy-start.5
  230.5 1.2 copy-start.4
Sparse Core Ops, SparseCore 0:
  65.5 38.2 reduce-scatter.1
  107.2 52.6 all-reduce.1
where the time goes:
time: 250 us; the launch traced here: 246 us
  waiting for transfers between devices  94.5 us (38%)
  matrix products  54.5 us (22%)
  other arithmetic  34 us (14%)
  local copies, waits for them, and re-layouts  30.3 us (12%)
  blocking collectives  17.6 us (7%)
  between operations  14.1 us (6%)
    psum x1, waiting for transfers between devices, shards(): totals = lax.psum(own_sums, 'dp')  56.1 us
    reduce_scatter x1, waiting for transfers between devices, shards(): lax.psum_scatter(leaf_sums, 'leaf', scatter_dimension=1, tiled=True)  38.3 us
    dot_general x8, matrix products, apply_advance(): jnp.dot(low_part, one_hot, preferred_element_type=jnp.float32)  23.5 us
    dot_general x8, matrix products, local_advance(): lax.dot_general(partial_value, one_hot, (((1,), (1,)), ((), ())), preferr...  21.7 us
    eq x16, other arithmetic, leaf_table(): matches = id_block[:, None, :] == leaf_slot  21.5 us
    all_gather x1, blocking collectives, shards(): lax.all_gather(own_values, 'leaf', axis=1, tiled=True)  17.6 us
    dynamic_slice x16, local copies, waits for them, and re-layouts, leaf_table(): id_block = lax.dynamic_slice_in_dim(tree_ids, first_row, width, 1)  16 us
    while x64, local copies, waits for them, and re-layouts  9.39 us
  transfers between devices with their start and end apart: 2, of which 2 were waited for; matrix products, arithmetic and copies ran while one was open for 0% of the time, Pallas kernels for 0%

commit v1 on v0

v1 whole, which is shorter than its diff:
```python
import functools

import jax
import jax.numpy as jnp
import numpy as np
from jax import lax
from jax.experimental import pallas as pl
from jax.experimental.pallas import tpu as pltpu
from jax.sharding import PartitionSpec as P

LEAVES = 64
PAIR = 2 * LEAVES
STEP_SIZE = 0.5
RIDGE_TERM = 1.0
VMEM_LIMIT = 40 * 1024 * 1024
AXES = ("dp", "leaf")


def round_up(value, multiple):
    return -(-value // multiple) * multiple


class Plan:
    def __init__(self, mesh, pairs):
        dp, leaf = mesh.shape["dp"], mesh.shape["leaf"]
        self.devices = dp * leaf
        core = [leaf] if dp > 1 else []
        chip_bits = (dp - 1).bit_length() - len(core)
        low = (chip_bits + 1) // 2
        x_bits = [leaf << (len(core) + b) for b in range(low)]
        y_bits = [leaf << (len(core) + b) for b in range(low, chip_bits)]
        z_bits = [1 << b for b in range((leaf - 1).bit_length())]
        even, odd = [], []
        for b in range(low):
            step = [x_bits[b]] + y_bits[b : b + 1]
            even += step
            odd += step[::-1]
        even += z_bits
        odd += z_bits[::-1]
        self.masks = [core + even, core + odd]
        self.core = core[0] if core else 0
        self.steps = len(self.masks[0])
        self.halvings = 0
        while self.halvings < self.steps and pairs >> (self.halvings + 1) << (self.halvings + 1) == pairs:
            self.halvings += 1
        self.pairs = pairs
        self.final = pairs >> self.halvings

    def mask(self, device, step):
        return self.masks[1 if device & self.core else 0][step]

    def permutation(self, step):
        return [(d, d ^ self.mask(d, step)) for d in range(self.devices)]

    def owned(self, device, slot):
        half = self.pairs
        pair = slot
        for step in range(self.halvings):
            half //= 2
            if device & self.mask(device, step):
                pair ^= half
        return pair


def one_hot(ids_ref, rows, width):
    slot = lax.broadcasted_iota(jnp.int32, (LEAVES, width), 0).astype(jnp.float32).astype(jnp.bfloat16)
    one, zero = jnp.bfloat16(1), jnp.bfloat16(0)
    blocks = []
    for row in rows:
        ids = ids_ref[pl.ds(row, 1), :].astype(jnp.float32).astype(jnp.bfloat16)
        blocks.append(jnp.where(ids == slot, one, zero))
    return jnp.concatenate(blocks, axis=0)


def pair_rows(table_ref, slots):
    rows = []
    for slot in slots:
        first = table_ref[slot] * 2
        rows += [first, first + 1]
    return rows


def groups(slots):
    return [slots[i : i + 2] for i in range(0, len(slots), 2)]


def accumulate(slots, table_ref, ids_ref, stacked, acc):
    width = ids_ref.shape[1]
    done = 0
    for group in groups(slots):
        hot = one_hot(ids_ref, pair_rows(table_ref, group), width)
        acc[pl.ds(done, hot.shape[0]), :] += lax.dot_general(
            hot, stacked, (((1,), (1,)), ((), ())), preferred_element_type=jnp.float32
        )
        done += hot.shape[0]


def write_sums(count, classes, half, acc, out_ref):
    for i in range(count):
        block = acc[pl.ds(i * PAIR, PAIR), :].T
        out_ref[:, pl.ds(2 * i * PAIR, PAIR)] = block[:classes]
        out_ref[:, pl.ds((2 * i + 1) * PAIR, PAIR)] = block[half : half + classes]


def first_kernel(slots, half, table_ref, predict_ref, labels_ref, ids_ref, stacked_ref, out_ref, acc):
    step = pl.program_id(0)

    @pl.when(step == 0)
    def _():
        acc[...] = jnp.zeros_like(acc)

    predict = predict_ref[...]
    classes, width = predict.shape
    row_max = jnp.max(predict, axis=0, keepdims=True)
    exponent = jnp.exp(predict - row_max)
    probability = exponent / jnp.sum(exponent, axis=0, keepdims=True)
    index = lax.broadcasted_iota(jnp.int32, predict.shape, 0)
    targets = jnp.where(index == labels_ref[...], 1.0, 0.0)
    filler = jnp.zeros((half - classes, width), jnp.float32)
    stacked = jnp.concatenate(
        [probability - targets, filler, probability * (1.0 - probability), filler], axis=0
    ).astype(jnp.bfloat16)
    stacked_ref[...] = stacked
    accumulate(slots, table_ref, ids_ref, stacked, acc)

    @pl.when(step == pl.num_programs(0) - 1)
    def _():
        write_sums(len(slots), classes, half, acc, out_ref)


def sums_kernel(slots, half, table_ref, stacked_ref, ids_ref, out_ref, acc):
    step = pl.program_id(0)

    @pl.when(step == 0)
    def _():
        acc[...] = jnp.zeros_like(acc)

    accumulate(slots, table_ref, ids_ref, stacked_ref[...], acc)

    @pl.when(step == pl.num_programs(0) - 1)
    def _():
        write_sums(len(slots), out_ref.shape[0], half, acc, out_ref)


def block_width(rows):
    width = rows
    while width > 2048 and width % 2 == 0:
        width //= 2
    return width


def sums_cost(slots, half, rows):
    return pl.CostEstimate(
        flops=2 * len(slots) * PAIR * rows * 2 * half, bytes_accessed=2 * half * rows * 2, transcendentals=0
    )


def first_sums(table, predict, labels, leaf_ids, slots, half):
    classes, rows = predict.shape
    trees = leaf_ids.shape[0]
    width = block_width(rows)
    return pl.pallas_call(
        functools.partial(first_kernel, slots, half),
        grid_spec=pltpu.PrefetchScalarGridSpec(
            num_scalar_prefetch=1,
            grid=(rows // width,),
            in_specs=[
                pl.BlockSpec((classes, width), lambda i, t: (0, i)),
                pl.BlockSpec((1, width), lambda i, t: (0, i)),
                pl.BlockSpec((trees, width), lambda i, t: (0, i)),
            ],
            out_specs=[
                pl.BlockSpec((2 * half, width), lambda i, t: (0, i)),
                pl.BlockSpec((classes, 2 * PAIR * len(slots)), lambda i, t: (0, 0)),
            ],
            scratch_shapes=[pltpu.VMEM((PAIR * len(slots), 2 * half), jnp.float32)],
        ),
        out_shape=[
            jax.ShapeDtypeStruct((2 * half, rows), jnp.bfloat16),
            jax.ShapeDtypeStruct((classes, 2 * PAIR * len(slots)), jnp.float32),
        ],
        compiler_params=pltpu.CompilerParams(vmem_limit_bytes=VMEM_LIMIT),
        cost_estimate=sums_cost(slots, half, rows),
        name="gradients_and_sums",
    )(table, predict, labels.reshape(1, rows), leaf_ids)


def more_sums(table, stacked, leaf_ids, classes, slots):
    height, rows = stacked.shape
    trees = leaf_ids.shape[0]
    width = block_width(rows)
    return pl.pallas_call(
        functools.partial(sums_kernel, slots, height // 2),
        grid_spec=pltpu.PrefetchScalarGridSpec(
            num_scalar_prefetch=1,
            grid=(rows // width,),
            in_specs=[
                pl.BlockSpec((height, width), lambda i, t: (0, i)),
                pl.BlockSpec((trees, width), lambda i, t: (0, i)),
            ],
            out_specs=pl.BlockSpec((classes, 2 * PAIR * len(slots)), lambda i, t: (0, 0)),
            scratch_shapes=[pltpu.VMEM((PAIR * len(slots), height), jnp.float32)],
        ),
        out_shape=jax.ShapeDtypeStruct((classes, 2 * PAIR * len(slots)), jnp.float32),
        compiler_params=pltpu.CompilerParams(vmem_limit_bytes=VMEM_LIMIT),
        cost_estimate=sums_cost(slots, height // 2, rows),
        name="leaf_sums",
    )(table, stacked, leaf_ids)


def apply_kernel(slots, table_ref, ids_ref, values_ref, carried_ref, out_ref):
    width = ids_ref.shape[1]
    total = carried_ref[...]
    done = 0
    for group in groups(slots):
        hot = one_hot(ids_ref, pair_rows(table_ref, group), width)
        values = values_ref[:, pl.ds(done, hot.shape[0])].astype(jnp.bfloat16)
        total = total + jnp.dot(values, hot, preferred_element_type=jnp.float32)
        done += hot.shape[0]
    out_ref[...] = total


def apply_values(table, leaf_ids, values, carried, slots):
    classes, rows = carried.shape
    trees = leaf_ids.shape[0]
    width = block_width(rows)
    return pl.pallas_call(
        functools.partial(apply_kernel, slots),
        grid_spec=pltpu.PrefetchScalarGridSpec(
            num_scalar_prefetch=1,
            grid=(rows // width,),
            in_specs=[
                pl.BlockSpec((trees, width), lambda i, t: (0, i)),
                pl.BlockSpec(values.shape, lambda i, t: (0, 0)),
                pl.BlockSpec((classes, width), lambda i, t: (0, i)),
            ],
            out_specs=pl.BlockSpec((classes, width), lambda i, t: (0, i)),
        ),
        out_shape=jax.ShapeDtypeStruct((classes, rows), jnp.float32),
        compiler_params=pltpu.CompilerParams(vmem_limit_bytes=VMEM_LIMIT),
        cost_estimate=pl.CostEstimate(
            flops=2 * len(slots) * PAIR * rows * 2 * classes, bytes_accessed=8 * classes * rows, transcendentals=0
        ),
        name="apply_values",
    )(table, leaf_ids, values, carried)


def newton(sums):
    values = []
    for i in range(sums.shape[1] // (2 * PAIR)):
        gradient = sums[:, 2 * i * PAIR : (2 * i + 1) * PAIR]
        hessian = sums[:, (2 * i + 1) * PAIR : (2 * i + 2) * PAIR]
        values.append(-STEP_SIZE * gradient / (hessian + RIDGE_TERM))
    return values[0] if len(values) == 1 else jnp.concatenate(values, axis=1)


def solution(mesh):
    leaf_count = mesh.shape["leaf"]

    def shards(predict, labels, leaf_ids):
        classes = predict.shape[0]
        pairs = leaf_ids.shape[0] // 2
        plan = Plan(mesh, pairs)
        half = round_up(classes, 16)

        rows = []
        for device in range(plan.devices):
            mine = [plan.owned(device, slot) for slot in range(pairs // 2)]
            other = [plan.owned(device ^ plan.core, slot) for slot in range(pairs // 2)]
            row = mine + other
            place = {pair: slot for slot, pair in enumerate(row)}
            per_leaf = pairs // leaf_count
            leaf = device % leaf_count
            rows.append(row + [place[leaf * per_leaf + i] for i in range(per_leaf)])
        table = jnp.asarray(np.array(rows, np.int32))[lax.axis_index(AXES)]

        def exchange(step, value):
            return lax.ppermute(value, AXES, plan.permutation(step))

        def sums(slots):
            return more_sums(table, stacked, leaf_ids, classes, slots)

        h = pairs // 2
        q = h // 2
        stacked, far_other = first_sums(table, predict, labels, leaf_ids, list(range(h + q, 2 * h)), half)
        far_other = exchange(0, far_other)
        far_mine = sums(list(range(q, h)))
        far = exchange(1, far_mine + far_other)
        near_other = exchange(0, sums(list(range(h, h + q))))
        near_mine = sums(list(range(q)))
        held = near_mine + near_other + far
        for step in range(2, plan.steps):
            if step < plan.halvings:
                keep = held.shape[1] // 2
                held = held[:, :keep] + exchange(step, held[:, keep:])
            else:
                held = held + exchange(step, held)
        values = newton(held)
        for step in reversed(range(2, plan.halvings)):
            values = jnp.concatenate([values, exchange(step, values)], axis=1)
        near_values = values
        far_values = exchange(1, near_values)
        mine_values = jnp.concatenate([near_values, far_values], axis=1)
        all_values = jnp.concatenate([mine_values, exchange(0, mine_values)], axis=1)
        new_predict = apply_values(table, leaf_ids, all_values, predict, list(range(pairs)))
        own = [
            lax.dynamic_slice_in_dim(all_values, table[pairs + i] * PAIR, PAIR, 1) for i in range(pairs // leaf_count)
        ]
        return new_predict, jnp.concatenate(own, axis=1)

    return jax.shard_map(
        shards,
        mesh=mesh,
        in_specs=(P(None, AXES), P(AXES), P(None, AXES)),
        out_specs=(P(None, AXES), P(None, "leaf")),
        check_vma=False,
    )
```

time: 250 us -> 76.8 us (0.31); the launches traced: 246 us -> 76 us
  waiting for transfers between devices: 94.5 us -> 18.4 us
  matrix products: 54.5 us -> 0 us
  other arithmetic: 34 us -> 0.96 us
  Pallas kernels: 0 us -> 24.7 us
  local copies, waits for them, and re-layouts: 30.3 us -> 7.39 us
  starting transfers between devices: 0.08 us -> 21.1 us
  blocking collectives: 17.6 us -> 0 us
  between operations: 14.1 us -> 3.44 us
    psum x1 -> x0, waiting for transfers between devices: 56.1 us -> none  [shards(): totals = lax.psum(own_sums, 'dp')]
    dot_general x24 -> x0, matrix products: 54.5 us -> none  [the longest x8 23.5 us: apply_advance(): jnp.dot(low_part, one_hot, preferred_element_type=jnp.float32)]
    reduce_scatter x1 -> x0, waiting for transfers between devices: 38.3 us -> none  [shards(): lax.psum_scatter(leaf_sums, 'leaf', scatter_dimension=1, tiled=True)]
    pallas_call x0 -> x5, Pallas kernels: none -> 24.7 us  [the longest x3 12.4 us: more_sums(): pl.pallas_call(functools.partial(sums_kernel, slots, height // 2), grid_s...]
    eq x16 -> x0, other arithmetic: 21.5 us -> none  [leaf_table(): matches = id_block[:, None, :] == leaf_slot]
    ppermute x0 -> x10, starting transfers between devices: none -> 21.1 us  [exchange(): return lax.ppermute(value, AXES, plan.permutation(step))]
    ppermute x0 -> x10, waiting for transfers between devices: none -> 18.4 us  [exchange(): return lax.ppermute(value, AXES, plan.permutation(step))]
    all_gather x1 -> x0, blocking collectives: 17.6 us -> none  [shards(): lax.all_gather(own_values, 'leaf', axis=1, tiled=True)]
  transfers between devices with their start and end apart: 2 -> 10, of which waited for: 2 -> 7; matrix products, arithmetic and copies ran while one was open for 0% -> 1% of each run, Pallas kernels for 0% -> 16%
where the time goes in v1:
time: 76.8 us; the launch traced here: 76 us
  Pallas kernels  24.7 us (32%)
  starting transfers between devices  21.1 us (27%)
  waiting for transfers between devices  18.4 us (24%)
  local copies, waits for them, and re-layouts  7.39 us (10%)
  between operations  3.44 us (4%)
  other arithmetic  0.96 us (1%)
    ppermute x10, starting transfers between devices, exchange(): return lax.ppermute(value, AXES, plan.permutation(step))  21.1 us
    ppermute x10, waiting for transfers between devices, exchange(): return lax.ppermute(value, AXES, plan.permutation(step))  18.4 us
    pallas_call x3, Pallas kernels, more_sums(): pl.pallas_call(functools.partial(sums_kernel, slots, height // 2), grid_s...  12.4 us
    pallas_call x1, Pallas kernels, apply_values(): pl.pallas_call(functools.partial(apply_kernel, slots), grid_spec=pltpu.Pr...  7.3 us
    unnamed x13, local copies, waits for them, and re-layouts  5.94 us
    pallas_call x1, Pallas kernels, first_sums(): pl.pallas_call(functools.partial(first_kernel, slots, half), grid_spec=pl...  5.01 us
  transfers between devices with their start and end apart: 10, of which 7 were waited for; matrix products, arithmetic and copies ran while one was open for 1% of the time, Pallas kernels for 16%

profile of v1, /device:TPU:1, one launch (start us, length us, event | category | flops | bytes accessed | tf_op | source)
XLA Modules:
  0.0 76.0 jit_solution(6941559987917781309)
XLA Ops:
  0.6 0.7 constant_dynamic-slice_fusion.4
  1.3 0.0 copy-start
  1.3 2.0 %copy-done = f32[100,8192]{1,0:T(8,128)S(1)} copy-done((f32[100,8192]{1,0:T(8,128)S(1)}, f32[100,8192]{1,0:T(8,128)}, u32[]{:S(2)}) %copy-start) | copy-done | bytes 3276824
  3.3 0.0 copy-start.2
  3.3 1.2 %copy-done.2 = s32[32,8192]{1,0:T(8,128)S(1)} copy-done((s32[32,8192]{1,0:T(8,128)S(1)}, s32[32,8192]{1,0:T(8,128)}, u32[]{:S(2)}) %copy-start.2) | copy-done | bytes 1048600
  4.5 0.0 copy-start.4
  4.5 0.8 copy-done.4
  5.3 0.0 copy-start.3
  5.3 5.0 %gradients_and_sums.1 = (bf16[224,8192]{1,0:T(8,128)(2,1)S(1)}, f32[100,1024]{1,0:T(8,128)S(1)}) custom-call(s32[20]{0:T(128)S(1)} %get-tuple-element.13.table_ref, f32[100,8192]{1,0:T(8,128)S(1)} %copy-done, s32[1,8192]{1,0:T(1,128)S(1)} %bitcast.7, s32[32,8192]{1,0:T(8,128)S(1)} %copy-done.2), custom_call_target="tpu_custom_call" | custom-call | flops 1879048192 | bytes 3670016 | tf_op jit(solution)/shard_map/gradients_and_sums/pallas_call | solution.py:162
  10.3 0.1 collective-permute-start.1
  10.5 0.0 copy-done.3
  10.5 4.1 %leaf_sums.4 = f32[100,1024]{1,0:T(8,128)S(1)} custom-call(s32[20]{0:T(128)S(1)} %get-tuple-element.13.table_ref, bf16[224,8192]{1,0:T(8,128)(2,1)S(1)} %get-tuple-element.4.stacked_ref, s32[32,8192]{1,0:T(8,128)S(1)} %copy-done.3), custom_call_target="tpu_custom_call" | custom-call | flops 1879048192 | bytes 3670016 | tf_op jit(solution)/shard_map/leaf_sums/pallas_call | solution.py:192
  14.6 0.5 collective-permute-start
  15.1 4.2 %leaf_sums.5 = f32[100,1024]{1,0:T(8,128)S(1)} custom-call(s32[20]{0:T(128)S(1)} %get-tuple-element.13.table_ref, bf16[224,8192]{1,0:T(8,128)(2,1)S(1)} %get-tuple-element.4.stacked_ref, s32[32,8192]{1,0:T(8,128)S(1)} %copy-done.3), custom_call_target="tpu_custom_call" | custom-call | flops 1879048192 | bytes 3670016 | tf_op jit(solution)/shard_map/leaf_sums/pallas_call | solution.py:192
  19.3 0.0 collective-permute-done.1
  19.3 2.3 %collective-permute-start.2 = (f32[100,1024]{1,0:T(8,128)S(1)}, f32[100,1024]{1,0:T(8,128)S(1)}, u32[]{:S(2)}, u32[]{:S(2)}) collective-permute-start(f32[100,1024]{1,0:T(8,128)S(1)} %add.45), channel_id=1, source_target_pairs={{0,8},{1,9},{2,10},{3,11},{4,20},{5,21},{6,22},{7,23},{8,0},{9,1},... | collective-permute-start | bytes 1228808 | tf_op jit(solution)/shard_map/ppermute | solution.py:278
  21.7 4.2 %leaf_sums.3 = f32[100,1024]{1,0:T(8,128)S(1)} custom-call(s32[20]{0:T(128)S(1)} %get-tuple-element.13.table_ref, bf16[224,8192]{1,0:T(8,128)(2,1)S(1)} %get-tuple-element.4.stacked_ref, s32[32,8192]{1,0:T(8,128)S(1)} %copy-done.3), custom_call_target="tpu_custom_call" | custom-call | flops 1879048192 | bytes 3670016 | tf_op jit(solution)/shard_map/leaf_sums/pallas_call | solution.py:192
  25.8 0.0 collective-permute-done
  25.8 1.6 %collective-permute-done.2 = f32[100,1024]{1,0:T(8,128)S(1)} collective-permute-done((f32[100,1024]{1,0:T(8,128)S(1)}, f32[100,1024]{1,0:T(8,128)S(1)}, u32[]{:S(2)}, u32[]{:S(2)}) %collective-permute-start.2) | collective-permute-done | bytes 409632 | tf_op jit(solution)/shard_map/ppermute | solution.py:278
  27.5 0.1 add_add_fusion
  27.6 1.5 %collective-permute-start.3 = (f32[100,512]{1,0:T(8,128)S(1)}, f32[100,512]{1,0:T(8,128)S(1)}, u32[]{:S(2)}, u32[]{:S(2)}) collective-permute-start(f32[100,512]{1,0:T(8,128)S(1)} %slice.45), channel_id=1, source_target_pairs={{0,16},{1,17},{2,18},{3,19},{4,12},{5,13},{6,14},{7,15},{8,24},{9,... | collective-permute-start | bytes 614408 | tf_op jit(solution)/shard_map/ppermute | solution.py:278
  29.0 3.6 %collective-permute-done.3 = f32[100,512]{1,0:T(8,128)S(1)} collective-permute-done((f32[100,512]{1,0:T(8,128)S(1)}, f32[100,512]{1,0:T(8,128)S(1)}, u32[]{:S(2)}, u32[]{:S(2)}) %collective-permute-start.3) | collective-permute-done | bytes 204832 | tf_op jit(solution)/shard_map/ppermute | solution.py:278
  32.7 2.6 %collective-permute-start.4 = (f32[100,256]{1,0:T(8,128)S(1)}, f32[100,256]{1,0:T(8,128)S(1)}, u32[]{:S(2)}, u32[]{:S(2)}) collective-permute-start(f32[100,256]{1,0:T(8,128)S(1)} %slice.47), channel_id=1, source_target_pairs={{0,1},{1,0},{2,3},{3,2},{4,6},{5,7},{6,4},{7,5},{8,9},{9,8},{10,11... | collective-permute-start | bytes 307208 | tf_op jit(solution)/shard_map/ppermute | solution.py:278
  35.2 2.1 %collective-permute-done.4 = f32[100,256]{1,0:T(8,128)S(1)} collective-permute-done((f32[100,256]{1,0:T(8,128)S(1)}, f32[100,256]{1,0:T(8,128)S(1)}, u32[]{:S(2)}, u32[]{:S(2)}) %collective-permute-start.4) | collective-permute-done | bytes 102432 | tf_op jit(solution)/shard_map/ppermute | solution.py:278
  37.4 1.9 %collective-permute-start.5 = (f32[100,256]{1,0:T(8,128)S(1)}, f32[100,256]{1,0:T(8,128)S(1)}, u32[]{:S(2)}, u32[]{:S(2)}) collective-permute-start(f32[100,256]{1,0:T(8,128)S(1)} %slice_add_fusion.1), channel_id=1, source_target_pairs={{0,2},{1,3},{2,0},{3,1},{4,5},{5,4},{6,7},{7,6},{8,10},{9,11},{10,... | collective-permute-start | bytes 307208 | tf_op jit(solution)/shard_map/ppermute | solution.py:278
  39.3 2.1 %collective-permute-done.5 = f32[100,256]{1,0:T(8,128)S(1)} collective-permute-done((f32[100,256]{1,0:T(8,128)S(1)}, f32[100,256]{1,0:T(8,128)S(1)}, u32[]{:S(2)}, u32[]{:S(2)}) %collective-permute-start.5) | collective-permute-done | bytes 102432 | tf_op jit(solution)/shard_map/ppermute | solution.py:278
  41.4 2.9 %collective-permute-start.6 = (f32[100,128]{1,0:T(8,128)S(1)}, f32[100,128]{1,0:T(8,128)S(1)}, u32[]{:S(2)}, u32[]{:S(2)}) collective-permute-start(f32[100,128]{1,0:T(8,128)S(1)} %get-tuple-element.7), channel_id=1, source_target_pairs={{0,1},{1,0},{2,3},{3,2},{4,6},{5,7},{6,4},{7,5},{8,9},{9,8},{10,11... | collective-permute-start | bytes 153608 | tf_op jit(solution)/shard_map/ppermute | solution.py:278
  44.4 2.2 %collective-permute-done.6 = f32[100,128]{1,0:T(8,128)S(1)} collective-permute-done((f32[100,128]{1,0:T(8,128)S(1)}, f32[100,128]{1,0:T(8,128)S(1)}, u32[]{:S(2)}, u32[]{:S(2)}) %collective-permute-start.6) | collective-permute-done | bytes 51232 | tf_op jit(solution)/shard_map/ppermute | solution.py:278
  46.5 1.3 %collective-permute-start.7 = (f32[100,256]{1,0:T(8,128)S(1)}, f32[100,256]{1,0:T(8,128)S(1)}, u32[]{:S(2)}, u32[]{:S(2)}) collective-permute-start(f32[100,256]{1,0:T(8,128)S(1)} %pad_maximum_fusion.3), channel_id=1, source_target_pairs={{0,16},{1,17},{2,18},{3,19},{4,12},{5,13},{6,14},{7,15},{8,24},{9,... | collective-permute-start | bytes 307208 | tf_op jit(solution)/shard_map/ppermute | solution.py:278
  47.9 2.5 %collective-permute-done.7 = f32[100,256]{1,0:T(8,128)S(1)} collective-permute-done((f32[100,256]{1,0:T(8,128)S(1)}, f32[100,256]{1,0:T(8,128)S(1)}, u32[]{:S(2)}, u32[]{:S(2)}) %collective-permute-start.7) | collective-permute-done | bytes 102432 | tf_op jit(solution)/shard_map/ppermute | solution.py:278
  50.3 1.8 %collective-permute-start.8 = (f32[100,512]{1,0:T(8,128)S(1)}, f32[100,512]{1,0:T(8,128)S(1)}, u32[]{:S(2)}, u32[]{:S(2)}) collective-permute-start(f32[100,512]{1,0:T(8,128)S(1)} %pad_maximum_fusion.1), channel_id=1, source_target_pairs={{0,8},{1,9},{2,10},{3,11},{4,20},{5,21},{6,22},{7,23},{8,0},{9,1},... | collective-permute-start | bytes 614408 | tf_op jit(solution)/shard_map/ppermute | solution.py:278
  52.2 4.4 %collective-permute-done.8 = f32[100,512]{1,0:T(8,128)S(1)} collective-permute-done((f32[100,512]{1,0:T(8,128)S(1)}, f32[100,512]{1,0:T(8,128)S(1)}, u32[]{:S(2)}, u32[]{:S(2)}) %collective-permute-start.8) | collective-permute-done | bytes 204832 | tf_op jit(solution)/shard_map/ppermute | solution.py:278
  56.6 6.0 %collective-permute-start.9 = (f32[100,1024]{1,0:T(8,128)S(1)}, f32[100,1024]{1,0:T(8,128)S(1)}, u32[]{:S(2)}, u32[]{:S(2)}) collective-permute-start(f32[100,1024]{1,0:T(8,128)S(1)} %pad_maximum_fusion), channel_id=1, source_target_pairs={{0,4},{1,5},{2,6},{3,7},{4,0},{5,1},{6,2},{7,3},{8,12},{9,13},{10,... | collective-permute-start | bytes 1228808 | tf_op jit(solution)/shard_map/ppermute | solution.py:278
  62.6 0.7 fusion.3
  66.0 0.0 collective-permute-done.9
  66.0 0.0 copy-start.1
  66.0 2.0 %copy-done.1 = f32[100,8192]{1,0:T(8,128)S(1)} copy-done((f32[100,8192]{1,0:T(8,128)S(1)}, f32[100,8192]{1,0:T(8,128)}, u32[]{:S(2)}) %copy-start.1) | copy-done | bytes 3276824
  68.0 7.3 %apply_values.1 = f32[100,8192]{1,0:T(8,128)} custom-call(s32[20]{0:T(128)S(1)} %get-tuple-element.13.table_ref, s32[32,8192]{1,0:T(8,128)S(1)} %copy-done.3, f32[100,2048]{1,0:T(8,128)S(1)} %constant_dynamic-update-slice_fusion.values_ref, f32[100,8192]{1,0:T(8,128)S(1)} %copy-done.1), custom_call_target="tpu_custom_call" | custom-call | flops 6710886400 | bytes 6553600 | tf_op jit(solution)/shard_map/apply_values/pallas_call | solution.py:227
  75.3 0.7 pad_maximum_fusion.2
  (15 shorter events, 0.3 us)
Async XLA Ops:
  1.3 2.0 %copy-start = (f32[100,8192]{1,0:T(8,128)S(1)}, f32[100,8192]{1,0:T(8,128)}, u32[]{:S(2)}) copy-start(f32[100,8192]{1,0:T(8,128)} %carried_ref.1) | copy-start | bytes 9830404
  3.3 1.2 %copy-start.2 = (s32[32,8192]{1,0:T(8,128)S(1)}, s32[32,8192]{1,0:T(8,128)}, u32[]{:S(2)}) copy-start(s32[32,8192]{1,0:T(8,128)} %ids_ref.9) | copy-start | bytes 3145732
  4.5 0.8 copy-start.4
  5.3 5.2 %copy-start.3 = (s32[32,8192]{1,0:T(8,128)S(1)}, s32[32,8192]{1,0:T(8,128)}, u32[]{:S(2)}) copy-start(s32[32,8192]{1,0:T(8,128)} %ids_ref.9) | copy-start | bytes 3145732
  10.3 9.0 %collective-permute-start.1 = (f32[100,1024]{1,0:T(8,128)S(1)}, f32[100,1024]{1,0:T(8,128)S(1)}, u32[]{:S(2)}, u32[]{:S(2)}) collective-permute-start(f32[100,1024]{1,0:T(8,128)S(1)} %get-tuple-element.5), channel_id=1, source_target_pairs={{0,4},{1,5},{2,6},{3,7},{4,0},{5,1},{6,2},{7,3},{8,12},{9,13},{10,... | collective-permute-start | bytes 1228808 | tf_op jit(solution)/shard_map/ppermute | solution.py:278
  14.6 11.2 %collective-permute-start = (f32[100,1024]{1,0:T(8,128)S(1)}, f32[100,1024]{1,0:T(8,128)S(1)}, u32[]{:S(2)}, u32[]{:S(2)}) collective-permute-start(f32[100,1024]{1,0:T(8,128)S(1)} %leaf_sums.4), channel_id=1, source_target_pairs={{0,4},{1,5},{2,6},{3,7},{4,0},{5,1},{6,2},{7,3},{8,12},{9,13},{10,... | collective-permute-start | bytes 1228808 | tf_op jit(solution)/shard_map/ppermute | solution.py:278
  19.3 8.1 %collective-permute-start.2 = (f32[100,1024]{1,0:T(8,128)S(1)}, f32[100,1024]{1,0:T(8,128)S(1)}, u32[]{:S(2)}, u32[]{:S(2)}) collective-permute-start(f32[100,1024]{1,0:T(8,128)S(1)} %add.45), channel_id=1, source_target_pairs={{0,8},{1,9},{2,10},{3,11},{4,20},{5,21},{6,22},{7,23},{8,0},{9,1},... | collective-permute-start | bytes 1228808 | tf_op jit(solution)/shard_map/ppermute | solution.py:278
  27.6 5.1 %collective-permute-start.3 = (f32[100,512]{1,0:T(8,128)S(1)}, f32[100,512]{1,0:T(8,128)S(1)}, u32[]{:S(2)}, u32[]{:S(2)}) collective-permute-start(f32[100,512]{1,0:T(8,128)S(1)} %slice.45), channel_id=1, source_target_pairs={{0,16},{1,17},{2,18},{3,19},{4,12},{5,13},{6,14},{7,15},{8,24},{9,... | collective-permute-start | bytes 614408 | tf_op jit(solution)/shard_map/ppermute | solution.py:278
  32.7 4.7 %collective-permute-start.4 = (f32[100,256]{1,0:T(8,128)S(1)}, f32[100,256]{1,0:T(8,128)S(1)}, u32[]{:S(2)}, u32[]{:S(2)}) collective-permute-start(f32[100,256]{1,0:T(8,128)S(1)} %slice.47), channel_id=1, source_target_pairs={{0,1},{1,0},{2,3},{3,2},{4,6},{5,7},{6,4},{7,5},{8,9},{9,8},{10,11... | collective-permute-start | bytes 307208 | tf_op jit(solution)/shard_map/ppermute | solution.py:278
  37.4 4.0 %collective-permute-start.5 = (f32[100,256]{1,0:T(8,128)S(1)}, f32[100,256]{1,0:T(8,128)S(1)}, u32[]{:S(2)}, u32[]{:S(2)}) collective-permute-start(f32[100,256]{1,0:T(8,128)S(1)} %slice_add_fusion.1), channel_id=1, source_target_pairs={{0,2},{1,3},{2,0},{3,1},{4,5},{5,4},{6,7},{7,6},{8,10},{9,11},{10,... | collective-permute-start | bytes 307208 | tf_op jit(solution)/shard_map/ppermute | solution.py:278
  41.4 5.1 %collective-permute-start.6 = (f32[100,128]{1,0:T(8,128)S(1)}, f32[100,128]{1,0:T(8,128)S(1)}, u32[]{:S(2)}, u32[]{:S(2)}) collective-permute-start(f32[100,128]{1,0:T(8,128)S(1)} %get-tuple-element.7), channel_id=1, source_target_pairs={{0,1},{1,0},{2,3},{3,2},{4,6},{5,7},{6,4},{7,5},{8,9},{9,8},{10,11... | collective-permute-start | bytes 153608 | tf_op jit(solution)/shard_map/ppermute | solution.py:278
  46.5 3.8 %collective-permute-start.7 = (f32[100,256]{1,0:T(8,128)S(1)}, f32[100,256]{1,0:T(8,128)S(1)}, u32[]{:S(2)}, u32[]{:S(2)}) collective-permute-start(f32[100,256]{1,0:T(8,128)S(1)} %pad_maximum_fusion.3), channel_id=1, source_target_pairs={{0,16},{1,17},{2,18},{3,19},{4,12},{5,13},{6,14},{7,15},{8,24},{9,... | collective-permute-start | bytes 307208 | tf_op jit(solution)/shard_map/ppermute | solution.py:278
  50.3 6.2 %collective-permute-start.8 = (f32[100,512]{1,0:T(8,128)S(1)}, f32[100,512]{1,0:T(8,128)S(1)}, u32[]{:S(2)}, u32[]{:S(2)}) collective-permute-start(f32[100,512]{1,0:T(8,128)S(1)} %pad_maximum_fusion.1), channel_id=1, source_target_pairs={{0,8},{1,9},{2,10},{3,11},{4,20},{5,21},{6,22},{7,23},{8,0},{9,1},... | collective-permute-start | bytes 614408 | tf_op jit(solution)/shard_map/ppermute | solution.py:278
  56.6 9.4 %collective-permute-start.9 = (f32[100,1024]{1,0:T(8,128)S(1)}, f32[100,1024]{1,0:T(8,128)S(1)}, u32[]{:S(2)}, u32[]{:S(2)}) collective-permute-start(f32[100,1024]{1,0:T(8,128)S(1)} %pad_maximum_fusion), channel_id=1, source_target_pairs={{0,4},{1,5},{2,6},{3,7},{4,0},{5,1},{6,2},{7,3},{8,12},{9,13},{10,... | collective-permute-start | bytes 1228808 | tf_op jit(solution)/shard_map/ppermute | solution.py:278
  66.0 2.0 %copy-start.1 = (f32[100,8192]{1,0:T(8,128)S(1)}, f32[100,8192]{1,0:T(8,128)}, u32[]{:S(2)}) copy-start(f32[100,8192]{1,0:T(8,128)} %carried_ref.1) | copy-start | bytes 9830404

commit v2 on v0

v2 whole, which is shorter than its diff:
```python
import functools

import jax
import jax.numpy as jnp
from jax import lax
from jax.experimental import pallas as pl
from jax.experimental.pallas import tpu as pltpu
from jax.sharding import PartitionSpec as P

LEAVES = 64
PAIR = 2 * LEAVES
STEP_SIZE = 0.5
RIDGE_TERM = 1.0
VMEM_LIMIT = 24 * 1024 * 1024
FIRST_VMEM_LIMIT = 57 * 1024 * 1024
AXES = ("dp", "leaf")
IN_VMEM = pl.BlockSpec(memory_space=pltpu.VMEM)
IN_HBM = pl.BlockSpec(memory_space=pltpu.HBM)


def round_up(value, multiple):
    return -(-value // multiple) * multiple


class Plan:
    def __init__(self, mesh, pairs):
        dp, leaf = mesh.shape["dp"], mesh.shape["leaf"]
        self.leaf = leaf
        self.devices = dp * leaf
        chip_bits = (dp - 1).bit_length() - 1
        low = (chip_bits + 1) // 2
        x_bits = [leaf << (1 + b) for b in range(low)]
        y_bits = [leaf << (1 + b) for b in range(low, chip_bits)]
        z_bits = [1 << b for b in range((leaf - 1).bit_length())]
        even, odd = [], []
        for b in range(low):
            step = [x_bits[b]] + y_bits[b : b + 1]
            even += step
            odd += step[::-1]
        self.core = leaf
        self.masks = [[leaf] + even + z_bits, [leaf] + odd + z_bits[::-1]]
        self.steps = len(self.masks[0])
        self.halvings = 0
        while self.halvings < self.steps and pairs >> (self.halvings + 1) << (self.halvings + 1) == pairs:
            self.halvings += 1
        self.pairs = pairs

    def permutation(self, step):
        return [(d, d ^ self.masks[1 if d & self.core else 0][step]) for d in range(self.devices)]

    def code(self, device, other):
        odd = (device & self.core) != 0
        codes = []
        for masks in self.masks:
            total = jnp.int32(0)
            for step in range(1, self.halvings):
                half = self.pairs >> (step + 1)
                total = total | jnp.where((device & masks[step]) != 0, half, 0)
            codes.append(total)
        top = self.pairs >> 1
        if other:
            return jnp.where(odd, codes[0], codes[1] | top)
        return jnp.where(odd, codes[1] | top, codes[0])


def own_device(plan):
    return lax.axis_index("dp").astype(jnp.int32) * plan.leaf + lax.axis_index("leaf").astype(jnp.int32)


def one_hot(ids_ref, rows, first, width):
    slot = lax.broadcasted_iota(jnp.int32, (LEAVES, width), 0).astype(jnp.float32).astype(jnp.bfloat16)
    one, zero = jnp.bfloat16(1), jnp.bfloat16(0)
    blocks = []
    for row in rows:
        ids = ids_ref[pl.ds(row, 1), pl.ds(first, width)].astype(jnp.float32).astype(jnp.bfloat16)
        blocks.append(jnp.where(ids == slot, one, zero))
    return jnp.concatenate(blocks, axis=0)


def tree_rows(code, slots):
    rows = []
    for slot in slots:
        first = (slot ^ code) * 2
        rows += [first, first + 1]
    return rows


def groups(slots, size):
    return [slots[i : i + size] for i in range(0, len(slots), size)]


def chunk(rows, limit):
    width = rows
    while width > limit and width % 256 == 0:
        width //= 2
    return width


def pair_sums(hot, stacked):
    return lax.dot_general(hot, stacked, (((1,), (1,)), ((), ())), preferred_element_type=jnp.float32)


def write_sums(sums, half, out_ref, first):
    classes = out_ref.shape[0]
    turned = sums.T
    for i in range(turned.shape[1] // PAIR):
        block = turned[:, i * PAIR : (i + 1) * PAIR]
        out_ref[:, pl.ds(2 * (first + i) * PAIR, PAIR)] = block[:classes]
        out_ref[:, pl.ds((2 * (first + i) + 1) * PAIR, PAIR)] = block[half : half + classes]


def first_kernel(plan, slots, half, width, predict_hbm, labels_hbm, ids_hbm, stacked_hbm, out_ref,
                 predict_ref, labels_ref, ids_ref, stacked_ref, sems, out_sems):
    rows = predict_ref.shape[1]
    classes = predict_ref.shape[0]
    count = rows // width
    copies = [
        pltpu.make_async_copy(labels_hbm, labels_ref, sems.at[0]),
        pltpu.make_async_copy(ids_hbm, ids_ref, sems.at[1]),
    ]
    for i in range(count):
        part = pl.ds(i * width, width)
        copies.append(pltpu.make_async_copy(predict_hbm.at[:, part], predict_ref.at[:, part], sems.at[2 + i]))
    copies[0].start()
    copies[2].start()
    copies[1].start()
    for copy in copies[3:]:
        copy.start()
    tree = tree_rows(plan.code(own_device(plan), True), slots)
    copies[0].wait()
    total = None
    writes = []
    for i in range(count):
        copies[2 + i].wait()
        predict = predict_ref[:, i * width : (i + 1) * width]
        row_max = jnp.max(predict, axis=0, keepdims=True)
        exponent = jnp.exp(predict - row_max)
        probability = exponent * (1.0 / jnp.sum(exponent, axis=0, keepdims=True))
        index = lax.broadcasted_iota(jnp.int32, predict.shape, 0)
        targets = jnp.where(index == labels_ref[:, i * width : (i + 1) * width], 1.0, 0.0)
        filler = jnp.zeros((half - classes, width), jnp.float32)
        stacked = jnp.concatenate(
            [probability - targets, filler, probability * (1.0 - probability), filler], axis=0
        ).astype(jnp.bfloat16)
        stacked_ref[:, i * width : (i + 1) * width] = stacked
        part = pl.ds(i * width, width)
        writes.append(pltpu.make_async_copy(stacked_ref.at[:, part], stacked_hbm.at[:, part], out_sems.at[i]))
        writes[-1].start()
        if i == 0:
            copies[1].wait()
        part = pair_sums(one_hot(ids_ref, tree, i * width, width), stacked)
        total = part if total is None else total + part
    write_sums(total, half, out_ref, 0)
    for write in writes:
        write.wait()


def sums_kernel(plan, parts, half, width, stacked_ref, ids_ref, *out_refs):
    device = own_device(plan)
    rows = stacked_ref.shape[1]
    todo = []
    for (slots, other), out_ref in zip(parts, out_refs):
        tree = tree_rows(plan.code(device, other), slots)
        todo += [(tree[2 * i : 2 * i + 2], out_ref, i) for i in range(len(slots))]
    for group in groups(todo, 4):
        tree = [row for item in group for row in item[0]]
        total = None
        for first in range(0, rows, width):
            part = pair_sums(one_hot(ids_ref, tree, first, width), stacked_ref[:, first : first + width])
            total = part if total is None else total + part
        for i, (_, out_ref, place) in enumerate(group):
            write_sums(total[i * PAIR : (i + 1) * PAIR], half, out_ref, place)


def sums_cost(count, half, rows):
    return pl.CostEstimate(
        flops=2 * count * PAIR * rows * 2 * half, bytes_accessed=2 * half * rows * 2, transcendentals=0
    )


def first_sums(plan, predict, labels, leaf_ids, slots, half):
    classes, rows = predict.shape
    width = chunk(rows, 1024)
    return pl.pallas_call(
        functools.partial(first_kernel, plan, slots, half, width),
        in_specs=[IN_HBM, IN_HBM, IN_HBM],
        out_specs=[IN_HBM, IN_VMEM],
        out_shape=[
            jax.ShapeDtypeStruct((2 * half, rows), jnp.bfloat16),
            jax.ShapeDtypeStruct((classes, 2 * PAIR * len(slots)), jnp.float32),
        ],
        scratch_shapes=[
            pltpu.VMEM((classes, rows), jnp.float32),
            pltpu.VMEM((1, rows), jnp.int32),
            pltpu.VMEM(leaf_ids.shape, jnp.int32),
            pltpu.VMEM((2 * half, rows), jnp.bfloat16),
            pltpu.SemaphoreType.DMA((2 + rows // width,)),
            pltpu.SemaphoreType.DMA((rows // width,)),
        ],
        compiler_params=pltpu.CompilerParams(vmem_limit_bytes=FIRST_VMEM_LIMIT),
        cost_estimate=sums_cost(len(slots), half, rows),
        name="gradients_and_sums",
    )(predict, labels.reshape(1, rows), leaf_ids)


def more_sums(plan, stacked, leaf_ids, classes, parts):
    height, rows = stacked.shape
    return pl.pallas_call(
        functools.partial(sums_kernel, plan, parts, height // 2, chunk(rows, 1024)),
        in_specs=[IN_VMEM, IN_VMEM],
        out_specs=[IN_VMEM] * len(parts),
        out_shape=[jax.ShapeDtypeStruct((classes, 2 * PAIR * len(slots)), jnp.float32) for slots, _ in parts],
        compiler_params=pltpu.CompilerParams(vmem_limit_bytes=VMEM_LIMIT),
        cost_estimate=sums_cost(sum(len(slots) for slots, _ in parts), height // 2, rows),
        name="leaf_sums",
    )(stacked, leaf_ids)


def looked_up(plan, parts, value_refs, ids_ref, first, width):
    device = own_device(plan)
    todo = []
    for (slots, other), value_ref in zip(parts, value_refs):
        tree = tree_rows(plan.code(device, other), slots)
        todo += [(tree[2 * i : 2 * i + 2], value_ref, i) for i in range(len(slots))]
    total = None
    for group in groups(todo, 2):
        tree = [row for item in group for row in item[0]]
        hot = one_hot(ids_ref, tree, first, width)
        values = [ref[:, pl.ds(i * PAIR, PAIR)].astype(jnp.bfloat16) for _, ref, i in group]
        values = values[0] if len(values) == 1 else jnp.concatenate(values, axis=1)
        part = jnp.dot(values, hot, preferred_element_type=jnp.float32)
        total = part if total is None else total + part
    return total


def apply_kernel(plan, parts, width, carried, *refs):
    ids_ref, refs = refs[0], refs[1:]
    value_refs, out_ref = refs[: len(parts)], refs[-1]
    for first in range(0, out_ref.shape[1], width):
        part = pl.ds(first, width)
        total = looked_up(plan, parts, value_refs, ids_ref, first, width)
        out_ref[:, part] = refs[len(parts)][:, part] + total if carried else total


def apply_cost(count, classes, rows):
    return pl.CostEstimate(
        flops=2 * count * PAIR * rows * 2 * classes, bytes_accessed=4 * classes * rows, transcendentals=0
    )


def apply_values(plan, leaf_ids, parts, values, update):
    classes, rows = values[0].shape[0], leaf_ids.shape[1]
    carried = update is not None
    operands = (leaf_ids, *values) + ((update,) if carried else ())
    return pl.pallas_call(
        functools.partial(apply_kernel, plan, parts, chunk(rows, 2048), carried),
        in_specs=[IN_VMEM] * len(operands),
        out_specs=IN_VMEM,
        out_shape=jax.ShapeDtypeStruct((classes, rows), jnp.float32),
        input_output_aliases={len(operands) - 1: 0} if carried else {},
        compiler_params=pltpu.CompilerParams(vmem_limit_bytes=VMEM_LIMIT),
        cost_estimate=apply_cost(sum(len(slots) for slots, _ in parts), classes, rows),
        name="apply_values",
    )(*operands)


def last_kernel(plan, parts, pieces, width, *refs):
    ids_ref, update_ref, predict_hbm = refs[:3]
    value_refs = refs[3 : 3 + len(pieces)]
    out_hbm, own_ref, predict_ref, out_ref, table_ref, in_sems, out_sems = refs[3 + len(pieces) :]
    rows = ids_ref.shape[1]
    count = rows // width
    reads, writes = [], []
    for i in range(count):
        part = pl.ds(i * width, width)
        reads.append(pltpu.make_async_copy(predict_hbm.at[:, part], predict_ref.at[:, part], in_sems.at[i]))
        writes.append(pltpu.make_async_copy(out_ref.at[:, part], out_hbm.at[:, part], out_sems.at[i]))
    for read in reads:
        read.start()
    last = [value_refs[pieces.index(piece)] for piece in parts]
    for i in range(count):
        part = pl.ds(i * width, width)
        total = looked_up(plan, parts, last, ids_ref, i * width, width) + update_ref[:, part]
        reads[i].wait()
        out_ref[:, part] = predict_ref[:, part] + total
        writes[i].start()
    device = own_device(plan)
    half = plan.pairs // 2
    for (slots, other), value_ref in zip(pieces, value_refs):
        first = slots[0] + (half if other else 0)
        table_ref[:, pl.ds(first * PAIR, len(slots) * PAIR)] = value_ref[...]
    mine, theirs = plan.code(device, False), plan.code(device, True)
    per_leaf = plan.pairs // plan.leaf
    for i in range(per_leaf):
        pair = lax.axis_index("leaf").astype(jnp.int32) * per_leaf + i
        place = pair ^ mine
        place = jnp.where(place < half, place, (pair ^ theirs) + half)
        own_ref[:, pl.ds(i * PAIR, PAIR)] = table_ref[:, pl.ds(pl.multiple_of(place * PAIR, PAIR), PAIR)]
    for write in writes:
        write.wait()


def finish(plan, leaf_ids, update, predict, parts, pieces, values):
    classes, rows = predict.shape
    width = chunk(rows, 2048)
    return pl.pallas_call(
        functools.partial(last_kernel, plan, parts, pieces, width),
        in_specs=[IN_VMEM, IN_VMEM, IN_HBM] + [IN_VMEM] * len(values),
        out_specs=[IN_HBM, IN_VMEM],
        out_shape=[
            jax.ShapeDtypeStruct((classes, rows), jnp.float32),
            jax.ShapeDtypeStruct((classes, plan.pairs // plan.leaf * PAIR), jnp.float32),
        ],
        scratch_shapes=[
            pltpu.VMEM((classes, rows), jnp.float32),
            pltpu.VMEM((classes, rows), jnp.float32),
            pltpu.VMEM((classes, plan.pairs * PAIR), jnp.float32),
            pltpu.SemaphoreType.DMA((rows // width,)),
            pltpu.SemaphoreType.DMA((rows // width,)),
        ],
        compiler_params=pltpu.CompilerParams(vmem_limit_bytes=VMEM_LIMIT),
        cost_estimate=apply_cost(sum(len(slots) for slots, _ in parts), classes, rows),
        name="apply_last_values",
    )(leaf_ids, update, predict, *values)


def newton(sums):
    values = []
    for i in range(sums.shape[1] // (2 * PAIR)):
        gradient = sums[:, 2 * i * PAIR : (2 * i + 1) * PAIR]
        hessian = sums[:, (2 * i + 1) * PAIR : (2 * i + 2) * PAIR]
        values.append(-STEP_SIZE * gradient / (hessian + RIDGE_TERM))
    return values[0] if len(values) == 1 else jnp.concatenate(values, axis=1)


def after(value, *earlier):
    return lax.optimization_barrier((value, *earlier))[0]


def solution(mesh):
    def shards(predict, labels, leaf_ids):
        classes = predict.shape[0]
        plan = Plan(mesh, leaf_ids.shape[0] // 2)
        half = round_up(classes, 16)

        def exchange(step, value):
            return lax.ppermute(value, AXES, plan.permutation(step))

        h = plan.pairs // 2
        far = list(range(h // 2, h))
        middle = list(range(h // 4, h // 2))
        near = list(range(h // 4))

        stacked, far_other = first_sums(plan, predict, labels, leaf_ids, far, half)
        far_core = exchange(0, far_other)
        (far_own,) = more_sums(plan, stacked, leaf_ids, classes, [(far, False)])
        far_sums = far_own + far_core
        far_moved = exchange(1, far_sums)
        other, middle_own = more_sums(
            plan, after(stacked, far_sums), leaf_ids, classes, [(near + middle, True), (middle, False)]
        )
        rest = exchange(0, other)
        cut = 2 * PAIR * len(near)
        middle_sums = middle_own + rest[:, cut:] + far_moved[:, cut:]
        middle_moved = exchange(2, middle_sums)
        (near_own,) = more_sums(plan, after(stacked, middle_sums), leaf_ids, classes, [(near, False)])
        held = near_own + rest[:, :cut] + far_moved[:, :cut] + middle_moved
        for step in range(3, plan.steps):
            if step < plan.halvings:
                keep = held.shape[1] // 2
                held = held[:, :keep] + exchange(step, held[:, keep:])
            else:
                held = held + exchange(step, held)
        near_values = newton(held)
        for step in reversed(range(3, plan.halvings)):
            near_values = jnp.concatenate([near_values, exchange(step, near_values)], axis=1)

        near_theirs = exchange(0, near_values)
        middle_values = exchange(2, near_values)
        update = apply_values(
            plan, leaf_ids, [(near, False), (near, True)], [near_values, near_theirs], None
        )
        middle_theirs = exchange(0, after(middle_values, update))
        far_values = exchange(1, after(jnp.concatenate([near_values, middle_values], axis=1), update))
        update = apply_values(
            plan, leaf_ids, [(middle, False), (middle, True)], [middle_values, middle_theirs], update
        )
        far_theirs = exchange(0, after(far_values, update))
        update = apply_values(plan, leaf_ids, [(far, False)], [far_values], update)
        pieces = [(near, False), (middle, False), (far, False), (near, True), (middle, True), (far, True)]
        values = [near_values, middle_values, far_values, near_theirs, middle_theirs, far_theirs]
        return tuple(finish(plan, leaf_ids, update, predict, [(far, True)], pieces, values))

    return jax.shard_map(
        shards,
        mesh=mesh,
        in_specs=(P(None, AXES), P(AXES), P(None, AXES)),
        out_specs=(P(None, AXES), P(None, "leaf")),
        check_vma=False,
    )
```

time: 250 us -> 62.2 us (0.25); the launches traced: 246 us -> 61.4 us
  waiting for transfers between devices: 94.5 us -> 13.5 us
  matrix products: 54.5 us -> 0 us
  other arithmetic: 34 us -> 0.24 us
  local copies, waits for them, and re-layouts: 30.3 us -> 2.06 us
  Pallas kernels: 0 us -> 25.3 us
  starting transfers between devices: 0.08 us -> 19.4 us
  blocking collectives: 17.6 us -> 0 us
  between operations: 14.1 us -> 0.92 us
    psum x1 -> x0, waiting for transfers between devices: 56.1 us -> none  [shards(): totals = lax.psum(own_sums, 'dp')]
    dot_general x24 -> x0, matrix products: 54.5 us -> none  [the longest x8 23.5 us: apply_advance(): jnp.dot(low_part, one_hot, preferred_element_type=jnp.float32)]
    reduce_scatter x1 -> x0, waiting for transfers between devices: 38.3 us -> none  [shards(): lax.psum_scatter(leaf_sums, 'leaf', scatter_dimension=1, tiled=True)]
    pallas_call x0 -> x8, Pallas kernels: none -> 25.3 us  [the longest x1 8.57 us: first_sums(): pl.pallas_call(functools.partial(first_kernel, plan, slots, half, width),...]
    eq x16 -> x0, other arithmetic: 21.5 us -> none  [leaf_table(): matches = id_block[:, None, :] == leaf_slot]
    ppermute x0 -> x12, starting transfers between devices: none -> 19.4 us  [exchange(): return lax.ppermute(value, AXES, plan.permutation(step))]
    all_gather x1 -> x0, blocking collectives: 17.6 us -> none  [shards(): lax.all_gather(own_values, 'leaf', axis=1, tiled=True)]
    dynamic_slice x16 -> x0, local copies, waits for them, and re-layouts: 16 us -> none  [leaf_table(): id_block = lax.dynamic_slice_in_dim(tree_ids, first_row, width, 1)]
  transfers between devices with their start and end apart: 2 -> 12, of which waited for: 2 -> 7; matrix products, arithmetic and copies ran while one was open for 0% -> 0% of each run, Pallas kernels for 0% -> 20%
where the time goes in v2:
time: 62.2 us; the launch traced here: 61.4 us
  Pallas kernels  25.3 us (41%)
  starting transfers between devices  19.4 us (31%)
  waiting for transfers between devices  13.5 us (22%)
  local copies, waits for them, and re-layouts  2.06 us (3%)
  between operations  0.92 us (1%)
    ppermute x12, starting transfers between devices, exchange(): return lax.ppermute(value, AXES, plan.permutation(step))  19.4 us
    ppermute x12, waiting for transfers between devices, exchange(): return lax.ppermute(value, AXES, plan.permutation(step))  13.5 us
    pallas_call x1, Pallas kernels, first_sums(): pl.pallas_call(functools.partial(first_kernel, plan, slots, half, width),...  8.57 us
    pallas_call x3, Pallas kernels, more_sums(): pl.pallas_call(functools.partial(sums_kernel, plan, parts, height // 2, c...  7.33 us
    pallas_call x3, Pallas kernels, apply_values(): pl.pallas_call(functools.partial(apply_kernel, plan, parts, chunk(rows, 2...  5.23 us
    pallas_call x1, Pallas kernels, finish(): pl.pallas_call(functools.partial(last_kernel, plan, parts, pieces, width)...  4.13 us
    unnamed x6, local copies, waits for them, and re-layouts  2.05 us
  transfers between devices with their start and end apart: 12, of which 7 were waited for; matrix products, arithmetic and copies ran while one was open for 0% of the time, Pallas kernels for 20%

profile of v2, /device:TPU:1, one launch (start us, length us, event | category | flops | bytes accessed | tf_op | source)
XLA Modules:
  0.0 61.4 jit_solution(5761447641745311915)
XLA Ops:
  0.6 0.0 copy-start
  0.6 8.6 %gradients_and_sums.1 = (bf16[224,8192]{1,0:T(8,128)(2,1)}, f32[100,1024]{1,0:T(8,128)}) custom-call(f32[100,8192]{1,0:T(8,128)} %refs_2_.1, s32[1,8192]{1,0:T(1,128)} %bitcast.1, s32[32,8192]{1,0:T(8,128)} %refs_0_.7), custom_call_target="tpu_custom_call" | custom-call | flops 1879048192 | bytes 3670016 | tf_op jit(solution)/shard_map/gradients_and_sums/pallas_call | solution.py:184
  9.2 0.1 collective-permute-start
  9.3 0.0 copy-done
  9.3 0.0 copy-start.1
  9.3 2.0 %copy-done.1 = bf16[224,8192]{1,0:T(8,128)(2,1)S(1)} copy-done((bf16[224,8192]{1,0:T(8,128)(2,1)S(1)}, bf16[224,8192]{1,0:T(8,128)(2,1)}, u32[]{:S(2)}) %copy-start.1) | copy-done | bytes 3670040
  11.4 2.4 %leaf_sums.3 = f32[100,1024]{1,0:T(8,128)S(1)} custom-call(bf16[224,8192]{1,0:T(8,128)(2,1)S(1)} %copy-done.1, s32[32,8192]{1,0:T(8,128)S(1)} %copy-done), custom_call_target="tpu_custom_call" | custom-call | flops 1879048192 | bytes 3670016 | tf_op jit(solution)/shard_map/leaf_sums/pallas_call | solution.py:208
  13.8 0.0 collective-permute-done
  13.9 2.8 %collective-permute-start.2 = (f32[100,1024]{1,0:T(8,128)S(1)}, f32[100,1024]{1,0:T(8,128)S(1)}, u32[]{:S(2)}, u32[]{:S(2)}) collective-permute-start(f32[100,1024]{1,0:T(8,128)S(1)} %add.30), channel_id=1, source_target_pairs={{0,8},{1,9},{2,10},{3,11},{4,20},{5,21},{6,22},{7,23},{8,0},{9,1},... | collective-permute-start | bytes 1228808 | tf_op jit(solution)/shard_map/ppermute | solution.py:347
  16.6 3.6 %leaf_sums.4 = (f32[100,1024]{1,0:T(8,128)S(1)}, f32[100,512]{1,0:T(8,128)S(1)}) custom-call(bf16[224,8192]{1,0:T(8,128)(2,1)S(1)} %copy-done.1, s32[32,8192]{1,0:T(8,128)S(1)} %copy-done), custom_call_target="tpu_custom_call" | custom-call | flops 2818572288 | bytes 3670016 | tf_op jit(solution)/shard_map/leaf_sums/pallas_call | solution.py:208
  20.2 0.3 collective-permute-start.1
  20.5 1.9 %collective-permute-done.2 = f32[100,1024]{1,0:T(8,128)S(1)} collective-permute-done((f32[100,1024]{1,0:T(8,128)S(1)}, f32[100,1024]{1,0:T(8,128)S(1)}, u32[]{:S(2)}, u32[]{:S(2)}) %collective-permute-start.2) | collective-permute-done | bytes 409632 | tf_op jit(solution)/shard_map/ppermute | solution.py:347
  22.4 0.0 collective-permute-done.1
  22.5 1.5 %collective-permute-start.3 = (f32[100,512]{1,0:T(8,128)S(1)}, f32[100,512]{1,0:T(8,128)S(1)}, u32[]{:S(2)}, u32[]{:S(2)}) collective-permute-start(f32[100,512]{1,0:T(8,128)S(1)} %slice_add_fusion.2), channel_id=1, source_target_pairs={{0,16},{1,17},{2,18},{3,19},{4,12},{5,13},{6,14},{7,15},{8,24},{9,... | collective-permute-start | bytes 614408 | tf_op jit(solution)/shard_map/ppermute | solution.py:347
  24.0 1.3 %leaf_sums.5 = f32[100,512]{1,0:T(8,128)S(1)} custom-call(bf16[224,8192]{1,0:T(8,128)(2,1)S(1)} %copy-done.1, s32[32,8192]{1,0:T(8,128)S(1)} %copy-done), custom_call_target="tpu_custom_call" | custom-call | flops 939524096 | bytes 3670016 | tf_op jit(solution)/shard_map/leaf_sums/pallas_call | solution.py:208
  25.3 2.2 %collective-permute-done.3 = f32[100,512]{1,0:T(8,128)S(1)} collective-permute-done((f32[100,512]{1,0:T(8,128)S(1)}, f32[100,512]{1,0:T(8,128)S(1)}, u32[]{:S(2)}, u32[]{:S(2)}) %collective-permute-start.3) | collective-permute-done | bytes 204832 | tf_op jit(solution)/shard_map/ppermute | solution.py:347
  27.6 0.1 fusion
  27.6 2.6 %collective-permute-start.4 = (f32[100,256]{1,0:T(8,128)S(1)}, f32[100,256]{1,0:T(8,128)S(1)}, u32[]{:S(2)}, u32[]{:S(2)}) collective-permute-start(f32[100,256]{1,0:T(8,128)S(1)} %slice.37), channel_id=1, source_target_pairs={{0,1},{1,0},{2,3},{3,2},{4,6},{5,7},{6,4},{7,5},{8,9},{9,8},{10,11... | collective-permute-start | bytes 307208 | tf_op jit(solution)/shard_map/ppermute | solution.py:347
  30.2 2.1 %collective-permute-done.4 = f32[100,256]{1,0:T(8,128)S(1)} collective-permute-done((f32[100,256]{1,0:T(8,128)S(1)}, f32[100,256]{1,0:T(8,128)S(1)}, u32[]{:S(2)}, u32[]{:S(2)}) %collective-permute-start.4) | collective-permute-done | bytes 102432 | tf_op jit(solution)/shard_map/ppermute | solution.py:347
  32.4 1.9 %collective-permute-start.5 = (f32[100,256]{1,0:T(8,128)S(1)}, f32[100,256]{1,0:T(8,128)S(1)}, u32[]{:S(2)}, u32[]{:S(2)}) collective-permute-start(f32[100,256]{1,0:T(8,128)S(1)} %slice_add_fusion.4), channel_id=1, source_target_pairs={{0,2},{1,3},{2,0},{3,1},{4,5},{5,4},{6,7},{7,6},{8,10},{9,11},{10,... | collective-permute-start | bytes 307208 | tf_op jit(solution)/shard_map/ppermute | solution.py:347
  34.3 2.1 %collective-permute-done.5 = f32[100,256]{1,0:T(8,128)S(1)} collective-permute-done((f32[100,256]{1,0:T(8,128)S(1)}, f32[100,256]{1,0:T(8,128)S(1)}, u32[]{:S(2)}, u32[]{:S(2)}) %collective-permute-start.5) | collective-permute-done | bytes 102432 | tf_op jit(solution)/shard_map/ppermute | solution.py:347
  36.4 3.0 %collective-permute-start.6 = (f32[100,128]{1,0:T(8,128)S(1)}, f32[100,128]{1,0:T(8,128)S(1)}, u32[]{:S(2)}, u32[]{:S(2)}) collective-permute-start(f32[100,128]{1,0:T(8,128)S(1)} %fusion.1), channel_id=1, source_target_pairs={{0,1},{1,0},{2,3},{3,2},{4,6},{5,7},{6,4},{7,5},{8,9},{9,8},{10,11... | collective-permute-start | bytes 153608 | tf_op jit(solution)/shard_map/ppermute | solution.py:347
  39.4 2.1 %collective-permute-done.6 = f32[100,128]{1,0:T(8,128)S(1)} collective-permute-done((f32[100,128]{1,0:T(8,128)S(1)}, f32[100,128]{1,0:T(8,128)S(1)}, u32[]{:S(2)}, u32[]{:S(2)}) %collective-permute-start.6) | collective-permute-done | bytes 51232 | tf_op jit(solution)/shard_map/ppermute | solution.py:347
  41.5 3.0 %collective-permute-start.8 = (f32[100,256]{1,0:T(8,128)S(1)}, f32[100,256]{1,0:T(8,128)S(1)}, u32[]{:S(2)}, u32[]{:S(2)}) collective-permute-start(f32[100,256]{1,0:T(8,128)S(1)} %pad_maximum_fusion.1.refs_1_.refs_3_), channel_id=1, source_target_pairs={{0,4},{1,5},{2,6},{3,7},{4,0},{5,1},{6,2},{7,3},{8,12},{9,13},{10,... | collective-permute-start | bytes 307208 | tf_op jit(solution)/shard_map/ppermute | solution.py:347
  44.5 1.2 %collective-permute-start.7 = (f32[100,256]{1,0:T(8,128)S(1)}, f32[100,256]{1,0:T(8,128)S(1)}, u32[]{:S(2)}, u32[]{:S(2)}) collective-permute-start(f32[100,256]{1,0:T(8,128)S(1)} %pad_maximum_fusion.1.refs_1_.refs_3_), channel_id=1, source_target_pairs={{0,16},{1,17},{2,18},{3,19},{4,12},{5,13},{6,14},{7,15},{8,24},{9,... | collective-permute-start | bytes 307208 | tf_op jit(solution)/shard_map/ppermute | solution.py:347
  45.7 0.0 collective-permute-done.8.refs_2_.refs_6_
  45.7 1.6 %apply_values.3.refs_3_ = f32[100,8192]{1,0:T(8,128)S(1)} custom-call(s32[32,8192]{1,0:T(8,128)S(1)} %copy-done, f32[100,256]{1,0:T(8,128)S(1)} %pad_maximum_fusion.1.refs_1_.refs_3_, f32[100,256]{1,0:T(8,128)S(1)} %collective-permute-done.8.refs_2_.refs_6_), custom_call_target="tpu_custom_call" | custom-call | flops 1677721600 | bytes 3276800 | tf_op jit(solution)/shard_map/apply_values/pallas_call | solution.py:255
  47.3 1.1 %collective-permute-done.7.refs_1_.refs_4_ = f32[100,256]{1,0:T(8,128)S(1)} collective-permute-done((f32[100,256]{1,0:T(8,128)S(1)}, f32[100,256]{1,0:T(8,128)S(1)}, u32[]{:S(2)}, u32[]{:S(2)}) %collective-permute-start.7) | collective-permute-done | bytes 102432 | tf_op jit(solution)/shard_map/ppermute | solution.py:347
  48.4 0.9 %collective-permute-start.10 = (f32[100,256]{1,0:T(8,128)S(1)}, f32[100,256]{1,0:T(8,128)S(1)}, u32[]{:S(2)}, u32[]{:S(2)}) collective-permute-start(f32[100,256]{1,0:T(8,128)S(1)} %collective-permute-done.7.refs_1_.refs_4_), channel_id=1, source_target_pairs={{0,4},{1,5},{2,6},{3,7},{4,0},{5,1},{6,2},{7,3},{8,12},{9,13},{10,... | collective-permute-start | bytes 307208 | tf_op jit(solution)/shard_map/ppermute | solution.py:347
  49.3 1.3 %collective-permute-start.9 = (f32[100,512]{1,0:T(8,128)S(1)}, f32[100,512]{1,0:T(8,128)S(1)}, u32[]{:S(2)}, u32[]{:S(2)}) collective-permute-start(f32[100,512]{1,0:T(8,128)S(1)} %pad_maximum_fusion), channel_id=1, source_target_pairs={{0,8},{1,9},{2,10},{3,11},{4,20},{5,21},{6,22},{7,23},{8,0},{9,1},... | collective-permute-start | bytes 614408 | tf_op jit(solution)/shard_map/ppermute | solution.py:347
  50.6 0.0 collective-permute-done.10.refs_2_.refs_7_
  50.6 1.8 %apply_values.4.refs_2_ = f32[100,8192]{1,0:T(8,128)S(1)} custom-call(s32[32,8192]{1,0:T(8,128)S(1)} %copy-done, f32[100,256]{1,0:T(8,128)S(1)} %collective-permute-done.7.refs_1_.refs_4_, f32[100,256]{1,0:T(8,128)S(1)} %collective-permute-done.10.refs_2_.refs_7_, f32[100,8192]{1,0:T(8,128)S(1)} %apply_values.3.refs_3_), custom_call_target="tpu_custom_call", output_to_operand_aliasing={{}: (3, {})} | custom-call | flops 1677721600 | bytes 3276800 | tf_op jit(solution)/shard_map/apply_values/pallas_call | solution.py:255
  52.4 0.0 copy-start.2
  52.4 1.9 %collective-permute-done.9.refs_1_.refs_5_ = f32[100,512]{1,0:T(8,128)S(1)} collective-permute-done((f32[100,512]{1,0:T(8,128)S(1)}, f32[100,512]{1,0:T(8,128)S(1)}, u32[]{:S(2)}, u32[]{:S(2)}) %collective-permute-start.9) | collective-permute-done | bytes 204832 | tf_op jit(solution)/shard_map/ppermute | solution.py:347
  54.4 0.9 %collective-permute-start.11 = (f32[100,512]{1,0:T(8,128)S(1)}, f32[100,512]{1,0:T(8,128)S(1)}, u32[]{:S(2)}, u32[]{:S(2)}) collective-permute-start(f32[100,512]{1,0:T(8,128)S(1)} %collective-permute-done.9.refs_1_.refs_5_), channel_id=1, source_target_pairs={{0,4},{1,5},{2,6},{3,7},{4,0},{5,1},{6,2},{7,3},{8,12},{9,13},{10,... | collective-permute-start | bytes 614408 | tf_op jit(solution)/shard_map/ppermute | solution.py:347
  55.2 1.8 %apply_values.5.refs_1_ = f32[100,8192]{1,0:T(8,128)S(1)} custom-call(s32[32,8192]{1,0:T(8,128)S(1)} %copy-done, f32[100,512]{1,0:T(8,128)S(1)} %collective-permute-done.9.refs_1_.refs_5_, f32[100,8192]{1,0:T(8,128)S(1)} %apply_values.4.refs_2_), custom_call_target="tpu_custom_call", output_to_operand_aliasing={{}: (2, {})} | custom-call | flops 1677721600 | bytes 3276800 | tf_op jit(solution)/shard_map/apply_values/pallas_call | solution.py:255
  57.1 0.0 collective-permute-done.11.refs_8_
  57.1 0.0 copy-done.2
  57.1 4.1 %apply_last_values.1 = (f32[100,8192]{1,0:T(8,128)}, f32[100,512]{1,0:T(8,128)}) custom-call(s32[32,8192]{1,0:T(8,128)S(1)} %copy-done, f32[100,8192]{1,0:T(8,128)S(1)} %apply_values.5.refs_1_, f32[100,8192]{1,0:T(8,128)S(1)} %copy-done.2, f32[100,256]{1,0:T(8,128)S(1)} %pad_maximum_fusion.1.refs_1_.refs_3_, ...), custom_call_target="tpu_custom_call" | custom-call | flops 1677721600 | bytes 3276800 | tf_op jit(solution)/shard_map/apply_last_values/pallas_call | solution.py:306
  (8 shorter events, 0.2 us)
Async XLA Ops:
  0.6 8.7 %copy-start = (s32[32,8192]{1,0:T(8,128)S(1)}, s32[32,8192]{1,0:T(8,128)}, u32[]{:S(2)}) copy-start(s32[32,8192]{1,0:T(8,128)} %refs_0_.7) | copy-start | bytes 3145732
  9.2 4.6 %collective-permute-start = (f32[100,1024]{1,0:T(8,128)}, f32[100,1024]{1,0:T(8,128)S(1)}, u32[]{:S(2)}, u32[]{:S(2)}) collective-permute-start(f32[100,1024]{1,0:T(8,128)} %get-tuple-element.12), channel_id=1, source_target_pairs={{0,4},{1,5},{2,6},{3,7},{4,0},{5,1},{6,2},{7,3},{8,12},{9,13},{10,... | collective-permute-start | bytes 1228808 | tf_op jit(solution)/shard_map/ppermute | solution.py:347
  9.3 2.0 %copy-start.1 = (bf16[224,8192]{1,0:T(8,128)(2,1)S(1)}, bf16[224,8192]{1,0:T(8,128)(2,1)}, u32[]{:S(2)}) copy-start(bf16[224,8192]{1,0:T(8,128)(2,1)} %get-tuple-element.16.stacked_ref) | copy-start | bytes 11010052
  13.9 8.6 %collective-permute-start.2 = (f32[100,1024]{1,0:T(8,128)S(1)}, f32[100,1024]{1,0:T(8,128)S(1)}, u32[]{:S(2)}, u32[]{:S(2)}) collective-permute-start(f32[100,1024]{1,0:T(8,128)S(1)} %add.30), channel_id=1, source_target_pairs={{0,8},{1,9},{2,10},{3,11},{4,20},{5,21},{6,22},{7,23},{8,0},{9,1},... | collective-permute-start | bytes 1228808 | tf_op jit(solution)/shard_map/ppermute | solution.py:347
  20.2 2.2 %collective-permute-start.1 = (f32[100,1024]{1,0:T(8,128)S(1)}, f32[100,1024]{1,0:T(8,128)S(1)}, u32[]{:S(2)}, u32[]{:S(2)}) collective-permute-start(f32[100,1024]{1,0:T(8,128)S(1)} %get-tuple-element.15), channel_id=1, source_target_pairs={{0,4},{1,5},{2,6},{3,7},{4,0},{5,1},{6,2},{7,3},{8,12},{9,13},{10,... | collective-permute-start | bytes 1228808 | tf_op jit(solution)/shard_map/ppermute | solution.py:347
  22.5 5.1 %collective-permute-start.3 = (f32[100,512]{1,0:T(8,128)S(1)}, f32[100,512]{1,0:T(8,128)S(1)}, u32[]{:S(2)}, u32[]{:S(2)}) collective-permute-start(f32[100,512]{1,0:T(8,128)S(1)} %slice_add_fusion.2), channel_id=1, source_target_pairs={{0,16},{1,17},{2,18},{3,19},{4,12},{5,13},{6,14},{7,15},{8,24},{9,... | collective-permute-start | bytes 614408 | tf_op jit(solution)/shard_map/ppermute | solution.py:347
  27.6 4.7 %collective-permute-start.4 = (f32[100,256]{1,0:T(8,128)S(1)}, f32[100,256]{1,0:T(8,128)S(1)}, u32[]{:S(2)}, u32[]{:S(2)}) collective-permute-start(f32[100,256]{1,0:T(8,128)S(1)} %slice.37), channel_id=1, source_target_pairs={{0,1},{1,0},{2,3},{3,2},{4,6},{5,7},{6,4},{7,5},{8,9},{9,8},{10,11... | collective-permute-start | bytes 307208 | tf_op jit(solution)/shard_map/ppermute | solution.py:347
  32.4 4.0 %collective-permute-start.5 = (f32[100,256]{1,0:T(8,128)S(1)}, f32[100,256]{1,0:T(8,128)S(1)}, u32[]{:S(2)}, u32[]{:S(2)}) collective-permute-start(f32[100,256]{1,0:T(8,128)S(1)} %slice_add_fusion.4), channel_id=1, source_target_pairs={{0,2},{1,3},{2,0},{3,1},{4,5},{5,4},{6,7},{7,6},{8,10},{9,11},{10,... | collective-permute-start | bytes 307208 | tf_op jit(solution)/shard_map/ppermute | solution.py:347
  36.4 5.1 %collective-permute-start.6 = (f32[100,128]{1,0:T(8,128)S(1)}, f32[100,128]{1,0:T(8,128)S(1)}, u32[]{:S(2)}, u32[]{:S(2)}) collective-permute-start(f32[100,128]{1,0:T(8,128)S(1)} %fusion.1), channel_id=1, source_target_pairs={{0,1},{1,0},{2,3},{3,2},{4,6},{5,7},{6,4},{7,5},{8,9},{9,8},{10,11... | collective-permute-start | bytes 153608 | tf_op jit(solution)/shard_map/ppermute | solution.py:347
  41.5 4.2 %collective-permute-start.8 = (f32[100,256]{1,0:T(8,128)S(1)}, f32[100,256]{1,0:T(8,128)S(1)}, u32[]{:S(2)}, u32[]{:S(2)}) collective-permute-start(f32[100,256]{1,0:T(8,128)S(1)} %pad_maximum_fusion.1.refs_1_.refs_3_), channel_id=1, source_target_pairs={{0,4},{1,5},{2,6},{3,7},{4,0},{5,1},{6,2},{7,3},{8,12},{9,13},{10,... | collective-permute-start | bytes 307208 | tf_op jit(solution)/shard_map/ppermute | solution.py:347
  44.5 3.9 %collective-permute-start.7 = (f32[100,256]{1,0:T(8,128)S(1)}, f32[100,256]{1,0:T(8,128)S(1)}, u32[]{:S(2)}, u32[]{:S(2)}) collective-permute-start(f32[100,256]{1,0:T(8,128)S(1)} %pad_maximum_fusion.1.refs_1_.refs_3_), channel_id=1, source_target_pairs={{0,16},{1,17},{2,18},{3,19},{4,12},{5,13},{6,14},{7,15},{8,24},{9,... | collective-permute-start | bytes 307208 | tf_op jit(solution)/shard_map/ppermute | solution.py:347
  48.4 2.2 %collective-permute-start.10 = (f32[100,256]{1,0:T(8,128)S(1)}, f32[100,256]{1,0:T(8,128)S(1)}, u32[]{:S(2)}, u32[]{:S(2)}) collective-permute-start(f32[100,256]{1,0:T(8,128)S(1)} %collective-permute-done.7.refs_1_.refs_4_), channel_id=1, source_target_pairs={{0,4},{1,5},{2,6},{3,7},{4,0},{5,1},{6,2},{7,3},{8,12},{9,13},{10,... | collective-permute-start | bytes 307208 | tf_op jit(solution)/shard_map/ppermute | solution.py:347
  49.3 5.1 %collective-permute-start.9 = (f32[100,512]{1,0:T(8,128)S(1)}, f32[100,512]{1,0:T(8,128)S(1)}, u32[]{:S(2)}, u32[]{:S(2)}) collective-permute-start(f32[100,512]{1,0:T(8,128)S(1)} %pad_maximum_fusion), channel_id=1, source_target_pairs={{0,8},{1,9},{2,10},{3,11},{4,20},{5,21},{6,22},{7,23},{8,0},{9,1},... | collective-permute-start | bytes 614408 | tf_op jit(solution)/shard_map/ppermute | solution.py:347
  52.4 4.7 %copy-start.2 = (f32[100,8192]{1,0:T(8,128)S(1)}, f32[100,8192]{1,0:T(8,128)}, u32[]{:S(2)}) copy-start(f32[100,8192]{1,0:T(8,128)} %refs_2_.1) | copy-start | bytes 9830404
  54.4 2.7 %collective-permute-start.11 = (f32[100,512]{1,0:T(8,128)S(1)}, f32[100,512]{1,0:T(8,128)S(1)}, u32[]{:S(2)}, u32[]{:S(2)}) collective-permute-start(f32[100,512]{1,0:T(8,128)S(1)} %collective-permute-done.9.refs_1_.refs_5_), channel_id=1, source_target_pairs={{0,4},{1,5},{2,6},{3,7},{4,0},{5,1},{6,2},{7,3},{8,12},{9,13},{10,... | collective-permute-start | bytes 614408 | tf_op jit(solution)/shard_map/ppermute | solution.py:347

commit v3 on v2

--- a/solution.py
+++ b/solution.py
@@ -45,8 +45,14 @@
             self.halvings += 1
         self.pairs = pairs
 
-    def permutation(self, step):
-        return [(d, d ^ self.masks[1 if d & self.core else 0][step]) for d in range(self.devices)]
+    def permutation(self, *steps):
+        pairs = []
+        for device in range(self.devices):
+            partner = device
+            for step in steps:
+                partner ^= self.masks[1 if device & self.core else 0][step]
+            pairs.append((device, partner))
+        return pairs
 
     def code(self, device, other):
         odd = (device & self.core) != 0
@@ -121,14 +127,13 @@
     for i in range(count):
         part = pl.ds(i * width, width)
         copies.append(pltpu.make_async_copy(predict_hbm.at[:, part], predict_ref.at[:, part], sems.at[2 + i]))
+    copies[2].start()
     copies[0].start()
-    copies[2].start()
-    copies[1].start()
     for copy in copies[3:]:
         copy.start()
+    copies[1].start()
     tree = tree_rows(plan.code(own_device(plan), True), slots)
     copies[0].wait()
-    total = None
     writes = []
     for i in range(count):
         copies[2 + i].wait()
@@ -137,22 +142,41 @@
         exponent = jnp.exp(predict - row_max)
         probability = exponent * (1.0 / jnp.sum(exponent, axis=0, keepdims=True))
         index = lax.broadcasted_iota(jnp.int32, predict.shape, 0)
-        targets = jnp.where(index == labels_ref[:, i * width : (i + 1) * width], 1.0, 0.0)
+        gradient = jnp.where(index == labels_ref[:, i * width : (i + 1) * width], probability - 1.0, probability)
         filler = jnp.zeros((half - classes, width), jnp.float32)
-        stacked = jnp.concatenate(
-            [probability - targets, filler, probability * (1.0 - probability), filler], axis=0
+        stacked_ref[:, i * width : (i + 1) * width] = jnp.concatenate(
+            [gradient, filler, probability * (1.0 - probability), filler], axis=0
         ).astype(jnp.bfloat16)
-        stacked_ref[:, i * width : (i + 1) * width] = stacked
         part = pl.ds(i * width, width)
         writes.append(pltpu.make_async_copy(stacked_ref.at[:, part], stacked_hbm.at[:, part], out_sems.at[i]))
         writes[-1].start()
-        if i == 0:
-            copies[1].wait()
-        part = pair_sums(one_hot(ids_ref, tree, i * width, width), stacked)
+    copies[1].wait()
+    total = None
+    for i in range(count):
+        part = pair_sums(one_hot(ids_ref, tree, i * width, width), stacked_ref[:, i * width : (i + 1) * width])
         total = part if total is None else total + part
     write_sums(total, half, out_ref, 0)
     for write in writes:
         write.wait()
+
+
+def second_kernel(plan, slots, half, width, stacked_hbm, ids_hbm, out_ref, stacked_ref, ids_ref, sems):
+    rows = stacked_ref.shape[1]
+    count = rows // width
+    copies = [pltpu.make_async_copy(ids_hbm, ids_ref, sems.at[0])]
+    for i in range(count):
+        part = pl.ds(i * width, width)
+        copies.append(pltpu.make_async_copy(stacked_hbm.at[:, part], stacked_ref.at[:, part], sems.at[1 + i]))
+    for copy in copies:
+        copy.start()
+    tree = tree_rows(plan.code(own_device(plan), False), slots)
+    copies[0].wait()
+    total = None
+    for i in range(count):
+        copies[1 + i].wait()
+        part = pair_sums(one_hot(ids_ref, tree, i * width, width), stacked_ref[:, i * width : (i + 1) * width])
+        total = part if total is None else total + part
+    write_sums(total, half, out_ref, 0)
 
 
 def sums_kernel(plan, parts, half, width, stacked_ref, ids_ref, *out_refs):
@@ -203,6 +227,25 @@
     )(predict, labels.reshape(1, rows), leaf_ids)
 
 
+def second_sums(plan, stacked, leaf_ids, classes, slots):
+    height, rows = stacked.shape
+    width = chunk(rows, 2048)
+    return pl.pallas_call(
+        functools.partial(second_kernel, plan, slots, height // 2, width),
+        in_specs=[IN_HBM, IN_HBM],
+        out_specs=IN_VMEM,
+        out_shape=jax.ShapeDtypeStruct((classes, 2 * PAIR * len(slots)), jnp.float32),
+        scratch_shapes=[
+            pltpu.VMEM(stacked.shape, stacked.dtype),
+            pltpu.VMEM(leaf_ids.shape, jnp.int32),
+            pltpu.SemaphoreType.DMA((1 + rows // width,)),
+        ],
+        compiler_params=pltpu.CompilerParams(vmem_limit_bytes=FIRST_VMEM_LIMIT),
+        cost_estimate=sums_cost(len(slots), height // 2, rows),
+        name="second_sums",
+    )(stacked, leaf_ids)
+
+
 def more_sums(plan, stacked, leaf_ids, classes, parts):
     height, rows = stacked.shape
     return pl.pallas_call(
@@ -265,25 +308,11 @@
 
 
 def last_kernel(plan, parts, pieces, width, *refs):
-    ids_ref, update_ref, predict_hbm = refs[:3]
+    ids_ref, update_ref, predict_ref = refs[:3]
     value_refs = refs[3 : 3 + len(pieces)]
-    out_hbm, own_ref, predict_ref, out_ref, table_ref, in_sems, out_sems = refs[3 + len(pieces) :]
+    out_hbm, own_hbm, out_ref, own_ref, table_ref, sems = refs[3 + len(pieces) :]
     rows = ids_ref.shape[1]
     count = rows // width
-    reads, writes = [], []
-    for i in range(count):
-        part = pl.ds(i * width, width)
-        reads.append(pltpu.make_async_copy(predict_hbm.at[:, part], predict_ref.at[:, part], in_sems.at[i]))
-        writes.append(pltpu.make_async_copy(out_ref.at[:, part], out_hbm.at[:, part], out_sems.at[i]))
-    for read in reads:
-        read.start()
-    last = [value_refs[pieces.index(piece)] for piece in parts]
-    for i in range(count):
-        part = pl.ds(i * width, width)
-        total = looked_up(plan, parts, last, ids_ref, i * width, width) + update_ref[:, part]
-        reads[i].wait()
-        out_ref[:, part] = predict_ref[:, part] + total
-        writes[i].start()
     device = own_device(plan)
     half = plan.pairs // 2
     for (slots, other), value_ref in zip(pieces, value_refs):
@@ -296,6 +325,15 @@
         place = pair ^ mine
         place = jnp.where(place < half, place, (pair ^ theirs) + half)
         own_ref[:, pl.ds(i * PAIR, PAIR)] = table_ref[:, pl.ds(pl.multiple_of(place * PAIR, PAIR), PAIR)]
+    writes = [pltpu.make_async_copy(own_ref, own_hbm, sems.at[count])]
+    writes[0].start()
+    last = [value_refs[pieces.index(piece)] for piece in parts]
+    for i in range(count):
+        part = pl.ds(i * width, width)
+        total = looked_up(plan, parts, last, ids_ref, i * width, width) + update_ref[:, part]
+        out_ref[:, part] = predict_ref[:, part] + total
+        writes.append(pltpu.make_async_copy(out_ref.at[:, part], out_hbm.at[:, part], sems.at[i]))
+        writes[-1].start()
     for write in writes:
         write.wait()
 
@@ -303,20 +341,17 @@
 def finish(plan, leaf_ids, update, predict, parts, pieces, values):
     classes, rows = predict.shape
     width = chunk(rows, 2048)
+    own = (classes, plan.pairs // plan.leaf * PAIR)
     return pl.pallas_call(
         functools.partial(last_kernel, plan, parts, pieces, width),
-        in_specs=[IN_VMEM, IN_VMEM, IN_HBM] + [IN_VMEM] * len(values),
-        out_specs=[IN_HBM, IN_VMEM],
-        out_shape=[
-            jax.ShapeDtypeStruct((classes, rows), jnp.float32),
-            jax.ShapeDtypeStruct((classes, plan.pairs // plan.leaf * PAIR), jnp.float32),
-        ],
+        in_specs=[IN_VMEM] * (3 + len(values)),
+        out_specs=[IN_HBM, IN_HBM],
+        out_shape=[jax.ShapeDtypeStruct((classes, rows), jnp.float32), jax.ShapeDtypeStruct(own, jnp.float32)],
         scratch_shapes=[
             pltpu.VMEM((classes, rows), jnp.float32),
-            pltpu.VMEM((classes, rows), jnp.float32),
+            pltpu.VMEM(own, jnp.float32),
             pltpu.VMEM((classes, plan.pairs * PAIR), jnp.float32),
-            pltpu.SemaphoreType.DMA((rows // width,)),
-            pltpu.SemaphoreType.DMA((rows // width,)),
+            pltpu.SemaphoreType.DMA((rows // width + 1,)),
         ],
         compiler_params=pltpu.CompilerParams(vmem_limit_bytes=VMEM_LIMIT),
         cost_estimate=apply_cost(sum(len(slots) for slots, _ in parts), classes, rows),
@@ -343,8 +378,8 @@
         plan = Plan(mesh, leaf_ids.shape[0] // 2)
         half = round_up(classes, 16)
 
-        def exchange(step, value):
-            return lax.ppermute(value, AXES, plan.permutation(step))
+        def exchange(value, *steps):
+            return lax.ppermute(value, AXES, plan.permutation(*steps))
 
         h = plan.pairs // 2
         far = list(range(h // 2, h))
@@ -352,44 +387,50 @@
         near = list(range(h // 4))
 
         stacked, far_other = first_sums(plan, predict, labels, leaf_ids, far, half)
-        far_core = exchange(0, far_other)
-        (far_own,) = more_sums(plan, stacked, leaf_ids, classes, [(far, False)])
+        far_core = exchange(far_other, 0)
+        far_own = second_sums(plan, stacked, leaf_ids, classes, far)
         far_sums = far_own + far_core
-        far_moved = exchange(1, far_sums)
+        far_moved = exchange(far_sums, 1)
         other, middle_own = more_sums(
             plan, after(stacked, far_sums), leaf_ids, classes, [(near + middle, True), (middle, False)]
         )
-        rest = exchange(0, other)
+        rest = exchange(other, 0)
         cut = 2 * PAIR * len(near)
         middle_sums = middle_own + rest[:, cut:] + far_moved[:, cut:]
-        middle_moved = exchange(2, middle_sums)
+        middle_moved = exchange(middle_sums, 2)
         (near_own,) = more_sums(plan, after(stacked, middle_sums), leaf_ids, classes, [(near, False)])
         held = near_own + rest[:, :cut] + far_moved[:, :cut] + middle_moved
         for step in range(3, plan.steps):
             if step < plan.halvings:
                 keep = held.shape[1] // 2
-                held = held[:, :keep] + exchange(step, held[:, keep:])
+                held = held[:, :keep] + exchange(held[:, keep:], step)
             else:
-                held = held + exchange(step, held)
+                held = held + exchange(held, step)
         near_values = newton(held)
         for step in reversed(range(3, plan.halvings)):
-            near_values = jnp.concatenate([near_values, exchange(step, near_values)], axis=1)
-
-        near_theirs = exchange(0, near_values)
-        middle_values = exchange(2, near_values)
-        update = apply_values(
-            plan, leaf_ids, [(near, False), (near, True)], [near_values, near_theirs], None
-        )
-        middle_theirs = exchange(0, after(middle_values, update))
-        far_values = exchange(1, after(jnp.concatenate([near_values, middle_values], axis=1), update))
-        update = apply_values(
-            plan, leaf_ids, [(middle, False), (middle, True)], [middle_values, middle_theirs], update
-        )
-        far_theirs = exchange(0, after(far_values, update))
-        update = apply_values(plan, leaf_ids, [(far, False)], [far_values], update)
-        pieces = [(near, False), (middle, False), (far, False), (near, True), (middle, True), (far, True)]
-        values = [near_values, middle_values, far_values, near_theirs, middle_theirs, far_theirs]
-        return tuple(finish(plan, leaf_ids, update, predict, [(far, True)], pieces, values))
+            near_values = jnp.concatenate([near_values, exchange(near_values, step)], axis=1)
+
+        near_theirs = exchange(near_values, 0)
+        both_values = exchange(near_values, 1, 2)
+        first_values = exchange(near_values, 1)
+        second_values = exchange(near_values, 2)
+
+        def apply(parts, values, update):
+            return apply_values(plan, leaf_ids, parts, values, update)
+
+        first = list(range(h // 2, h // 2 + len(near)))
+        both = list(range(h // 2 + len(near), h))
+        update = apply([(near, False), (near, True)], [near_values, near_theirs], None)
+        both_theirs = exchange(after(both_values, update), 0)
+        first_theirs = exchange(after(first_values, update), 0)
+        update = apply([(both, False), (both, True)], [both_values, both_theirs], update)
+        second_theirs = exchange(after(second_values, update), 0)
+        update = apply([(first, False), (first, True)], [first_values, first_theirs], update)
+        pieces = [(slots, other) for other in (False, True) for slots in (near, middle, first, both)]
+        values = [near_values, second_values, first_values, both_values]
+        values += [near_theirs, second_theirs, first_theirs, both_theirs]
+        last = [(middle, False), (middle, True)]
+        return tuple(finish(plan, leaf_ids, update, predict, last, pieces, values))
 
     return jax.shard_map(
         shards,

time: 62.2 us -> 62.5 us (level)
  local copies, waits for them, and re-layouts: 2.06 us -> 0.02 us
  starting transfers between devices: 19.4 us -> 20.9 us
  waiting for transfers between devices: 13.5 us -> 12.4 us
  Pallas kernels: 25.3 us -> 26.3 us
  other arithmetic: 0.24 us -> 1.22 us
    pallas_call x0 -> x1, Pallas kernels: none -> 7.52 us  [second_sums(): pl.pallas_call(functools.partial(second_kernel, plan, slots, height // 2,...]
    pallas_call x1, Pallas kernels: 8.57 us -> 6.01 us  [first_sums(): pl.pallas_call(functools.partial(first_kernel, plan, slots, half, width),...]
    pallas_call x3 -> x2, Pallas kernels: 7.33 us -> 4.9 us  [more_sums(): pl.pallas_call(functools.partial(sums_kernel, plan, parts, height // 2, c...]
    unnamed x6, local copies, waits for them, and re-layouts: 2.05 us -> 0.01 us
    pallas_call x1, Pallas kernels: 4.13 us -> 2.59 us  [finish(): pl.pallas_call(functools.partial(last_kernel, plan, parts, pieces, width)...]
    ppermute x12 -> x14, starting transfers between devices: 19.4 us -> 20.9 us  [exchange(): return lax.ppermute(value, AXES, plan.permutation(*steps))]
    ppermute x12 -> x14, waiting for transfers between devices: 13.5 us -> 12.4 us  [exchange(): return lax.ppermute(value, AXES, plan.permutation(*steps))]
    add x1, other arithmetic: 0.05 us -> 1.06 us  [shards(): far_sums = far_own + far_core]
  transfers between devices with their start and end apart: 12 -> 14, of which waited for: 7 -> 7; matrix products, arithmetic and copies ran while one was open for 0% -> 0% of each run, Pallas kernels for 20% -> 29%
where the time goes in v3:
time: 62.5 us; the launch traced here: 61.8 us
  Pallas kernels  26.3 us (42%)
  starting transfers between devices  20.9 us (33%)
  waiting for transfers between devices  12.4 us (20%)
  other arithmetic  1.22 us (2%)
  between operations  0.91 us (1%)
    ppermute x14, starting transfers between devices, exchange(): return lax.ppermute(value, AXES, plan.permutation(*steps))  20.9 us
    ppermute x14, waiting for transfers between devices, exchange(): return lax.ppermute(value, AXES, plan.permutation(*steps))  12.4 us
    pallas_call x1, Pallas kernels, second_sums(): pl.pallas_call(functools.partial(second_kernel, plan, slots, height // 2,...  7.52 us
    pallas_call x1, Pallas kernels, first_sums(): pl.pallas_call(functools.partial(first_kernel, plan, slots, half, width),...  6.01 us
    pallas_call x3, Pallas kernels, apply_values(): pl.pallas_call(functools.partial(apply_kernel, plan, parts, chunk(rows, 2...  5.26 us
    pallas_call x2, Pallas kernels, more_sums(): pl.pallas_call(functools.partial(sums_kernel, plan, parts, height // 2, c...  4.9 us
    pallas_call x1, Pallas kernels, finish(): pl.pallas_call(functools.partial(last_kernel, plan, parts, pieces, width)...  2.59 us
  transfers between devices with their start and end apart: 14, of which 7 were waited for; matrix products, arithmetic and copies ran while one was open for 0% of the time, Pallas kernels for 29%

profile of v3, /device:TPU:1, one launch (start us, length us, event | category | flops | bytes accessed | tf_op | source)
XLA Modules:
  0.0 61.8 jit_solution(11143444778992739674)
XLA Ops:
  0.6 6.0 %gradients_and_sums.1 = (bf16[224,8192]{1,0:T(8,128)(2,1)}, f32[100,1024]{1,0:T(8,128)}) custom-call(f32[100,8192]{1,0:T(8,128)} %refs_2_.1, s32[1,8192]{1,0:T(1,128)} %bitcast.1, s32[32,8192]{1,0:T(8,128)} %refs_0_.7), custom_call_target="tpu_custom_call" | custom-call | flops 1879048192 | bytes 3670016 | tf_op jit(solution)/shard_map/gradients_and_sums/pallas_call | solution.py:208
  6.6 0.1 collective-permute-start
  6.8 0.0 copy-start
  6.8 0.0 copy-start.1
  6.8 7.5 %second_sums.1 = f32[100,1024]{1,0:T(8,128)} custom-call(bf16[224,8192]{1,0:T(8,128)(2,1)} %get-tuple-element.16.stacked_hbm.stacked_ref, s32[32,8192]{1,0:T(8,128)} %refs_0_.7), custom_call_target="tpu_custom_call" | custom-call | flops 1879048192 | bytes 3670016 | tf_op jit(solution)/shard_map/second_sums/pallas_call | solution.py:233
  14.3 0.0 collective-permute-done
  14.3 1.1 %add.30 = f32[100,1024]{1,0:T(8,128)S(1)} add(f32[100,1024]{1,0:T(8,128)} %second_sums.1, f32[100,1024]{1,0:T(8,128)S(1)} %collective-permute-done) | non-fusion elementwise | flops 102400 | bytes 1228800 | tf_op jit(solution)/shard_map/add | solution.py:392
  15.4 2.8 %collective-permute-start.2 = (f32[100,1024]{1,0:T(8,128)S(1)}, f32[100,1024]{1,0:T(8,128)S(1)}, u32[]{:S(2)}, u32[]{:S(2)}) collective-permute-start(f32[100,1024]{1,0:T(8,128)S(1)} %add.30), channel_id=1, source_target_pairs={{0,8},{1,9},{2,10},{3,11},{4,20},{5,21},{6,22},{7,23},{8,0},{9,1},... | collective-permute-start | bytes 1228808 | tf_op jit(solution)/shard_map/ppermute | solution.py:382
  18.1 0.0 copy-done
  18.1 0.0 copy-done.1
  18.1 3.6 %leaf_sums.2 = (f32[100,1024]{1,0:T(8,128)S(1)}, f32[100,512]{1,0:T(8,128)S(1)}) custom-call(bf16[224,8192]{1,0:T(8,128)(2,1)S(1)} %copy-done.1, s32[32,8192]{1,0:T(8,128)S(1)} %copy-done), custom_call_target="tpu_custom_call" | custom-call | flops 2818572288 | bytes 3670016 | tf_op jit(solution)/shard_map/leaf_sums/pallas_call | solution.py:251
  21.7 0.4 collective-permute-start.1
  22.1 1.9 %collective-permute-done.2 = f32[100,1024]{1,0:T(8,128)S(1)} collective-permute-done((f32[100,1024]{1,0:T(8,128)S(1)}, f32[100,1024]{1,0:T(8,128)S(1)}, u32[]{:S(2)}, u32[]{:S(2)}) %collective-permute-start.2) | collective-permute-done | bytes 409632 | tf_op jit(solution)/shard_map/ppermute | solution.py:382
  23.9 0.0 collective-permute-done.1
  24.0 1.5 %collective-permute-start.3 = (f32[100,512]{1,0:T(8,128)S(1)}, f32[100,512]{1,0:T(8,128)S(1)}, u32[]{:S(2)}, u32[]{:S(2)}) collective-permute-start(f32[100,512]{1,0:T(8,128)S(1)} %slice_add_fusion.2), channel_id=1, source_target_pairs={{0,16},{1,17},{2,18},{3,19},{4,12},{5,13},{6,14},{7,15},{8,24},{9,... | collective-permute-start | bytes 614408 | tf_op jit(solution)/shard_map/ppermute | solution.py:382
  25.5 1.3 %leaf_sums.3 = f32[100,512]{1,0:T(8,128)S(1)} custom-call(bf16[224,8192]{1,0:T(8,128)(2,1)S(1)} %copy-done.1, s32[32,8192]{1,0:T(8,128)S(1)} %copy-done), custom_call_target="tpu_custom_call" | custom-call | flops 939524096 | bytes 3670016 | tf_op jit(solution)/shard_map/leaf_sums/pallas_call | solution.py:251
  26.8 2.2 %collective-permute-done.3 = f32[100,512]{1,0:T(8,128)S(1)} collective-permute-done((f32[100,512]{1,0:T(8,128)S(1)}, f32[100,512]{1,0:T(8,128)S(1)}, u32[]{:S(2)}, u32[]{:S(2)}) %collective-permute-start.3) | collective-permute-done | bytes 204832 | tf_op jit(solution)/shard_map/ppermute | solution.py:382
  29.0 0.1 fusion
  29.1 2.6 %collective-permute-start.4 = (f32[100,256]{1,0:T(8,128)S(1)}, f32[100,256]{1,0:T(8,128)S(1)}, u32[]{:S(2)}, u32[]{:S(2)}) collective-permute-start(f32[100,256]{1,0:T(8,128)S(1)} %slice.37), channel_id=1, source_target_pairs={{0,1},{1,0},{2,3},{3,2},{4,6},{5,7},{6,4},{7,5},{8,9},{9,8},{10,11... | collective-permute-start | bytes 307208 | tf_op jit(solution)/shard_map/ppermute | solution.py:382
  31.7 2.1 %collective-permute-done.4 = f32[100,256]{1,0:T(8,128)S(1)} collective-permute-done((f32[100,256]{1,0:T(8,128)S(1)}, f32[100,256]{1,0:T(8,128)S(1)}, u32[]{:S(2)}, u32[]{:S(2)}) %collective-permute-start.4) | collective-permute-done | bytes 102432 | tf_op jit(solution)/shard_map/ppermute | solution.py:382
  33.9 1.9 %collective-permute-start.5 = (f32[100,256]{1,0:T(8,128)S(1)}, f32[100,256]{1,0:T(8,128)S(1)}, u32[]{:S(2)}, u32[]{:S(2)}) collective-permute-start(f32[100,256]{1,0:T(8,128)S(1)} %slice_add_fusion.4), channel_id=1, source_target_pairs={{0,2},{1,3},{2,0},{3,1},{4,5},{5,4},{6,7},{7,6},{8,10},{9,11},{10,... | collective-permute-start | bytes 307208 | tf_op jit(solution)/shard_map/ppermute | solution.py:382
  35.8 2.1 %collective-permute-done.5 = f32[100,256]{1,0:T(8,128)S(1)} collective-permute-done((f32[100,256]{1,0:T(8,128)S(1)}, f32[100,256]{1,0:T(8,128)S(1)}, u32[]{:S(2)}, u32[]{:S(2)}) %collective-permute-start.5) | collective-permute-done | bytes 102432 | tf_op jit(solution)/shard_map/ppermute | solution.py:382
  37.9 3.0 %collective-permute-start.6 = (f32[100,128]{1,0:T(8,128)S(1)}, f32[100,128]{1,0:T(8,128)S(1)}, u32[]{:S(2)}, u32[]{:S(2)}) collective-permute-start(f32[100,128]{1,0:T(8,128)S(1)} %fusion.1), channel_id=1, source_target_pairs={{0,1},{1,0},{2,3},{3,2},{4,6},{5,7},{6,4},{7,5},{8,9},{9,8},{10,11... | collective-permute-start | bytes 153608 | tf_op jit(solution)/shard_map/ppermute | solution.py:382
  40.9 2.1 %collective-permute-done.6 = f32[100,128]{1,0:T(8,128)S(1)} collective-permute-done((f32[100,128]{1,0:T(8,128)S(1)}, f32[100,128]{1,0:T(8,128)S(1)}, u32[]{:S(2)}, u32[]{:S(2)}) %collective-permute-start.6) | collective-permute-done | bytes 51232 | tf_op jit(solution)/shard_map/ppermute | solution.py:382
  43.0 3.0 %collective-permute-start.8 = (f32[100,256]{1,0:T(8,128)S(1)}, f32[100,256]{1,0:T(8,128)S(1)}, u32[]{:S(2)}, u32[]{:S(2)}) collective-permute-start(f32[100,256]{1,0:T(8,128)S(1)} %pad_maximum_fusion.refs_1_.refs_3_), channel_id=1, source_target_pairs={{0,4},{1,5},{2,6},{3,7},{4,0},{5,1},{6,2},{7,3},{8,12},{9,13},{10,... | collective-permute-start | bytes 307208 | tf_op jit(solution)/shard_map/ppermute | solution.py:382
  46.0 2.1 %collective-permute-start.10 = (f32[100,256]{1,0:T(8,128)S(1)}, f32[100,256]{1,0:T(8,128)S(1)}, u32[]{:S(2)}, u32[]{:S(2)}) collective-permute-start(f32[100,256]{1,0:T(8,128)S(1)} %pad_maximum_fusion.refs_1_.refs_3_), channel_id=1, source_target_pairs={{0,24},{1,25},{2,26},{3,27},{4,28},{5,29},{6,30},{7,31},{8,16},{9,... | collective-permute-start | bytes 307208 | tf_op jit(solution)/shard_map/ppermute | solution.py:382
  48.2 0.2 collective-permute-start.7
  48.4 0.0 collective-permute-done.8.refs_2_.refs_7_
  48.4 1.6 %apply_values.3.refs_3_ = f32[100,8192]{1,0:T(8,128)S(1)} custom-call(s32[32,8192]{1,0:T(8,128)S(1)} %copy-done, f32[100,256]{1,0:T(8,128)S(1)} %pad_maximum_fusion.refs_1_.refs_3_, f32[100,256]{1,0:T(8,128)S(1)} %collective-permute-done.8.refs_2_.refs_7_), custom_call_target="tpu_custom_call" | custom-call | flops 1677721600 | bytes 3276800 | tf_op jit(solution)/shard_map/apply_values/pallas_call | solution.py:298
  50.0 1.5 %collective-permute-done.10.refs_1_.refs_6_ = f32[100,256]{1,0:T(8,128)S(1)} collective-permute-done((f32[100,256]{1,0:T(8,128)S(1)}, f32[100,256]{1,0:T(8,128)S(1)}, u32[]{:S(2)}, u32[]{:S(2)}) %collective-permute-start.10) | collective-permute-done | bytes 102432 | tf_op jit(solution)/shard_map/ppermute | solution.py:382
  51.5 1.0 %collective-permute-start.11 = (f32[100,256]{1,0:T(8,128)S(1)}, f32[100,256]{1,0:T(8,128)S(1)}, u32[]{:S(2)}, u32[]{:S(2)}) collective-permute-start(f32[100,256]{1,0:T(8,128)S(1)} %collective-permute-done.10.refs_1_.refs_6_), channel_id=1, source_target_pairs={{0,4},{1,5},{2,6},{3,7},{4,0},{5,1},{6,2},{7,3},{8,12},{9,13},{10,... | collective-permute-start | bytes 307208 | tf_op jit(solution)/shard_map/ppermute | solution.py:382
  52.4 1.2 %collective-permute-start.12 = (f32[100,256]{1,0:T(8,128)S(1)}, f32[100,256]{1,0:T(8,128)S(1)}, u32[]{:S(2)}, u32[]{:S(2)}) collective-permute-start(f32[100,256]{1,0:T(8,128)S(1)} %pad_maximum_fusion.refs_1_.refs_3_), channel_id=1, source_target_pairs={{0,16},{1,17},{2,18},{3,19},{4,12},{5,13},{6,14},{7,15},{8,24},{9,... | collective-permute-start | bytes 307208 | tf_op jit(solution)/shard_map/ppermute | solution.py:382
  53.6 0.0 collective-permute-done.7.refs_1_.refs_5_
  53.6 0.3 collective-permute-start.9
  53.9 0.0 collective-permute-done.11.refs_2_.refs_10_
  53.9 1.8 %apply_values.4.refs_3_ = f32[100,8192]{1,0:T(8,128)S(1)} custom-call(s32[32,8192]{1,0:T(8,128)S(1)} %copy-done, f32[100,256]{1,0:T(8,128)S(1)} %collective-permute-done.10.refs_1_.refs_6_, f32[100,256]{1,0:T(8,128)S(1)} %collective-permute-done.11.refs_2_.refs_10_, f32[100,8192]{1,0:T(8,128)S(1)} %apply_values.3.refs_3_), custom_call_target="tpu_custom_call", output_to_operand_aliasing={{}: (3, {})} | custom-call | flops 1677721600 | bytes 3276800 | tf_op jit(solution)/shard_map/apply_values/pallas_call | solution.py:298
  55.8 0.0 copy-start.2
  55.8 0.5 collective-permute-done.12.refs_4_
  56.3 0.9 %collective-permute-start.13 = (f32[100,256]{1,0:T(8,128)S(1)}, f32[100,256]{1,0:T(8,128)S(1)}, u32[]{:S(2)}, u32[]{:S(2)}) collective-permute-start(f32[100,256]{1,0:T(8,128)S(1)} %collective-permute-done.12.refs_4_), channel_id=1, source_target_pairs={{0,4},{1,5},{2,6},{3,7},{4,0},{5,1},{6,2},{7,3},{8,12},{9,13},{10,... | collective-permute-start | bytes 307208 | tf_op jit(solution)/shard_map/ppermute | solution.py:382
  57.1 0.0 collective-permute-done.9.refs_2_.refs_9_
  57.1 1.8 %apply_values.5.refs_1_ = f32[100,8192]{1,0:T(8,128)S(1)} custom-call(s32[32,8192]{1,0:T(8,128)S(1)} %copy-done, f32[100,256]{1,0:T(8,128)S(1)} %collective-permute-done.7.refs_1_.refs_5_, f32[100,256]{1,0:T(8,128)S(1)} %collective-permute-done.9.refs_2_.refs_9_, f32[100,8192]{1,0:T(8,128)S(1)} %apply_values.4.refs_3_), custom_call_target="tpu_custom_call", output_to_operand_aliasing={{}: (3, {})} | custom-call | flops 1677721600 | bytes 3276800 | tf_op jit(solution)/shard_map/apply_values/pallas_call | solution.py:298
  59.0 0.0 collective-permute-done.13.refs_8_
  59.0 0.0 copy-done.2
  59.0 2.6 %apply_last_values.1 = (f32[100,8192]{1,0:T(8,128)}, f32[100,512]{1,0:T(8,128)}) custom-call(s32[32,8192]{1,0:T(8,128)S(1)} %copy-done, f32[100,8192]{1,0:T(8,128)S(1)} %apply_values.5.refs_1_, f32[100,8192]{1,0:T(8,128)S(1)} %copy-done.2, f32[100,256]{1,0:T(8,128)S(1)} %pad_maximum_fusion.refs_1_.refs_3_, f32[100,256]{1,0:T(8,128)S(1)} %collective-permute-done.12.refs_4_, ...), custom_call_target="tpu_custom_call" | custom-call | flops 1677721600 | bytes 3276800 | tf_op jit(solution)/shard_map/apply_last_values/pallas_call | solution.py:345
  (6 shorter events, 0.1 us)
Async XLA Ops:
  6.6 7.7 %collective-permute-start = (f32[100,1024]{1,0:T(8,128)}, f32[100,1024]{1,0:T(8,128)S(1)}, u32[]{:S(2)}, u32[]{:S(2)}) collective-permute-start(f32[100,1024]{1,0:T(8,128)} %get-tuple-element.12), channel_id=1, source_target_pairs={{0,4},{1,5},{2,6},{3,7},{4,0},{5,1},{6,2},{7,3},{8,12},{9,13},{10,... | collective-permute-start | bytes 1228808 | tf_op jit(solution)/shard_map/ppermute | solution.py:382
  6.8 11.4 %copy-start = (s32[32,8192]{1,0:T(8,128)S(1)}, s32[32,8192]{1,0:T(8,128)}, u32[]{:S(2)}) copy-start(s32[32,8192]{1,0:T(8,128)} %refs_0_.7) | copy-start | bytes 3145732
  6.8 11.4 %copy-start.1 = (bf16[224,8192]{1,0:T(8,128)(2,1)S(1)}, bf16[224,8192]{1,0:T(8,128)(2,1)}, u32[]{:S(2)}) copy-start(bf16[224,8192]{1,0:T(8,128)(2,1)} %get-tuple-element.16.stacked_hbm.stacked_ref) | copy-start | bytes 11010052
  15.4 8.6 %collective-permute-start.2 = (f32[100,1024]{1,0:T(8,128)S(1)}, f32[100,1024]{1,0:T(8,128)S(1)}, u32[]{:S(2)}, u32[]{:S(2)}) collective-permute-start(f32[100,1024]{1,0:T(8,128)S(1)} %add.30), channel_id=1, source_target_pairs={{0,8},{1,9},{2,10},{3,11},{4,20},{5,21},{6,22},{7,23},{8,0},{9,1},... | collective-permute-start | bytes 1228808 | tf_op jit(solution)/shard_map/ppermute | solution.py:382
  21.7 2.2 %collective-permute-start.1 = (f32[100,1024]{1,0:T(8,128)S(1)}, f32[100,1024]{1,0:T(8,128)S(1)}, u32[]{:S(2)}, u32[]{:S(2)}) collective-permute-start(f32[100,1024]{1,0:T(8,128)S(1)} %get-tuple-element.15), channel_id=1, source_target_pairs={{0,4},{1,5},{2,6},{3,7},{4,0},{5,1},{6,2},{7,3},{8,12},{9,13},{10,... | collective-permute-start | bytes 1228808 | tf_op jit(solution)/shard_map/ppermute | solution.py:382
  24.0 5.1 %collective-permute-start.3 = (f32[100,512]{1,0:T(8,128)S(1)}, f32[100,512]{1,0:T(8,128)S(1)}, u32[]{:S(2)}, u32[]{:S(2)}) collective-permute-start(f32[100,512]{1,0:T(8,128)S(1)} %slice_add_fusion.2), channel_id=1, source_target_pairs={{0,16},{1,17},{2,18},{3,19},{4,12},{5,13},{6,14},{7,15},{8,24},{9,... | collective-permute-start | bytes 614408 | tf_op jit(solution)/shard_map/ppermute | solution.py:382
  29.1 4.7 %collective-permute-start.4 = (f32[100,256]{1,0:T(8,128)S(1)}, f32[100,256]{1,0:T(8,128)S(1)}, u32[]{:S(2)}, u32[]{:S(2)}) collective-permute-start(f32[100,256]{1,0:T(8,128)S(1)} %slice.37), channel_id=1, source_target_pairs={{0,1},{1,0},{2,3},{3,2},{4,6},{5,7},{6,4},{7,5},{8,9},{9,8},{10,11... | collective-permute-start | bytes 307208 | tf_op jit(solution)/shard_map/ppermute | solution.py:382
  33.9 4.0 %collective-permute-start.5 = (f32[100,256]{1,0:T(8,128)S(1)}, f32[100,256]{1,0:T(8,128)S(1)}, u32[]{:S(2)}, u32[]{:S(2)}) collective-permute-start(f32[100,256]{1,0:T(8,128)S(1)} %slice_add_fusion.4), channel_id=1, source_target_pairs={{0,2},{1,3},{2,0},{3,1},{4,5},{5,4},{6,7},{7,6},{8,10},{9,11},{10,... | collective-permute-start | bytes 307208 | tf_op jit(solution)/shard_map/ppermute | solution.py:382
  37.9 5.1 %collective-permute-start.6 = (f32[100,128]{1,0:T(8,128)S(1)}, f32[100,128]{1,0:T(8,128)S(1)}, u32[]{:S(2)}, u32[]{:S(2)}) collective-permute-start(f32[100,128]{1,0:T(8,128)S(1)} %fusion.1), channel_id=1, source_target_pairs={{0,1},{1,0},{2,3},{3,2},{4,6},{5,7},{6,4},{7,5},{8,9},{9,8},{10,11... | collective-permute-start | bytes 153608 | tf_op jit(solution)/shard_map/ppermute | solution.py:382
  43.0 5.4 %collective-permute-start.8 = (f32[100,256]{1,0:T(8,128)S(1)}, f32[100,256]{1,0:T(8,128)S(1)}, u32[]{:S(2)}, u32[]{:S(2)}) collective-permute-start(f32[100,256]{1,0:T(8,128)S(1)} %pad_maximum_fusion.refs_1_.refs_3_), channel_id=1, source_target_pairs={{0,4},{1,5},{2,6},{3,7},{4,0},{5,1},{6,2},{7,3},{8,12},{9,13},{10,... | collective-permute-start | bytes 307208 | tf_op jit(solution)/shard_map/ppermute | solution.py:382
  46.0 5.4 %collective-permute-start.10 = (f32[100,256]{1,0:T(8,128)S(1)}, f32[100,256]{1,0:T(8,128)S(1)}, u32[]{:S(2)}, u32[]{:S(2)}) collective-permute-start(f32[100,256]{1,0:T(8,128)S(1)} %pad_maximum_fusion.refs_1_.refs_3_), channel_id=1, source_target_pairs={{0,24},{1,25},{2,26},{3,27},{4,28},{5,29},{6,30},{7,31},{8,16},{9,... | collective-permute-start | bytes 307208 | tf_op jit(solution)/shard_map/ppermute | solution.py:382
  48.2 5.4 %collective-permute-start.7 = (f32[100,256]{1,0:T(8,128)S(1)}, f32[100,256]{1,0:T(8,128)S(1)}, u32[]{:S(2)}, u32[]{:S(2)}) collective-permute-start(f32[100,256]{1,0:T(8,128)S(1)} %pad_maximum_fusion.refs_1_.refs_3_), channel_id=1, source_target_pairs={{0,8},{1,9},{2,10},{3,11},{4,20},{5,21},{6,22},{7,23},{8,0},{9,1},... | collective-permute-start | bytes 307208 | tf_op jit(solution)/shard_map/ppermute | solution.py:382
  51.5 2.5 %collective-permute-start.11 = (f32[100,256]{1,0:T(8,128)S(1)}, f32[100,256]{1,0:T(8,128)S(1)}, u32[]{:S(2)}, u32[]{:S(2)}) collective-permute-start(f32[100,256]{1,0:T(8,128)S(1)} %collective-permute-done.10.refs_1_.refs_6_), channel_id=1, source_target_pairs={{0,4},{1,5},{2,6},{3,7},{4,0},{5,1},{6,2},{7,3},{8,12},{9,13},{10,... | collective-permute-start | bytes 307208 | tf_op jit(solution)/shard_map/ppermute | solution.py:382
  52.4 3.9 %collective-permute-start.12 = (f32[100,256]{1,0:T(8,128)S(1)}, f32[100,256]{1,0:T(8,128)S(1)}, u32[]{:S(2)}, u32[]{:S(2)}) collective-permute-start(f32[100,256]{1,0:T(8,128)S(1)} %pad_maximum_fusion.refs_1_.refs_3_), channel_id=1, source_target_pairs={{0,16},{1,17},{2,18},{3,19},{4,12},{5,13},{6,14},{7,15},{8,24},{9,... | collective-permute-start | bytes 307208 | tf_op jit(solution)/shard_map/ppermute | solution.py:382
  53.6 3.5 %collective-permute-start.9 = (f32[100,256]{1,0:T(8,128)S(1)}, f32[100,256]{1,0:T(8,128)S(1)}, u32[]{:S(2)}, u32[]{:S(2)}) collective-permute-start(f32[100,256]{1,0:T(8,128)S(1)} %collective-permute-done.7.refs_1_.refs_5_), channel_id=1, source_target_pairs={{0,4},{1,5},{2,6},{3,7},{4,0},{5,1},{6,2},{7,3},{8,12},{9,13},{10,... | collective-permute-start | bytes 307208 | tf_op jit(solution)/shard_map/ppermute | solution.py:382
  55.8 3.2 %copy-start.2 = (f32[100,8192]{1,0:T(8,128)S(1)}, f32[100,8192]{1,0:T(8,128)}, u32[]{:S(2)}) copy-start(f32[100,8192]{1,0:T(8,128)} %refs_2_.1) | copy-start | bytes 9830404
  56.3 2.7 %collective-permute-start.13 = (f32[100,256]{1,0:T(8,128)S(1)}, f32[100,256]{1,0:T(8,128)S(1)}, u32[]{:S(2)}, u32[]{:S(2)}) collective-permute-start(f32[100,256]{1,0:T(8,128)S(1)} %collective-permute-done.12.refs_4_), channel_id=1, source_target_pairs={{0,4},{1,5},{2,6},{3,7},{4,0},{5,1},{6,2},{7,3},{8,12},{9,13},{10,... | collective-permute-start | bytes 307208 | tf_op jit(solution)/shard_map/ppermute | solution.py:382

commit v4 on v3

--- a/solution.py
+++ b/solution.py
@@ -12,7 +12,6 @@
 STEP_SIZE = 0.5
 RIDGE_TERM = 1.0
 VMEM_LIMIT = 24 * 1024 * 1024
-FIRST_VMEM_LIMIT = 57 * 1024 * 1024
 AXES = ("dp", "leaf")
 IN_VMEM = pl.BlockSpec(memory_space=pltpu.VMEM)
 IN_HBM = pl.BlockSpec(memory_space=pltpu.HBM)
@@ -115,8 +114,25 @@
         out_ref[:, pl.ds((2 * (first + i) + 1) * PAIR, PAIR)] = block[half : half + classes]
 
 
-def first_kernel(plan, slots, half, width, predict_hbm, labels_hbm, ids_hbm, stacked_hbm, out_ref,
-                 predict_ref, labels_ref, ids_ref, stacked_ref, sems, out_sems):
+def add_up(plan, parts, half, width, stacked_ref, ids_ref, out_refs):
+    device = own_device(plan)
+    rows = stacked_ref.shape[1]
+    todo = []
+    for (slots, other), out_ref in zip(parts, out_refs):
+        tree = tree_rows(plan.code(device, other), slots)
+        todo += [(tree[2 * i : 2 * i + 2], out_ref, i) for i in range(len(slots))]
+    for group in groups(todo, 4):
+        tree = [row for item in group for row in item[0]]
+        total = None
+        for first in range(0, rows, width):
+            part = pair_sums(one_hot(ids_ref, tree, first, width), stacked_ref[:, first : first + width])
+            total = part if total is None else total + part
+        for i, (_, out_ref, place) in enumerate(group):
+            write_sums(total[i * PAIR : (i + 1) * PAIR], half, out_ref, place)
+
+
+def first_kernel(plan, slots, half, width, predict_hbm, labels_hbm, ids_hbm, stacked_ref, other_ref,
+                 predict_ref, labels_ref, ids_ref, sems):
     rows = predict_ref.shape[1]
     classes = predict_ref.shape[0]
     count = rows // width
@@ -132,9 +148,7 @@
     for copy in copies[3:]:
         copy.start()
     copies[1].start()
-    tree = tree_rows(plan.code(own_device(plan), True), slots)
     copies[0].wait()
-    writes = []
     for i in range(count):
         copies[2 + i].wait()
         predict = predict_ref[:, i * width : (i + 1) * width]
@@ -147,53 +161,12 @@
         stacked_ref[:, i * width : (i + 1) * width] = jnp.concatenate(
             [gradient, filler, probability * (1.0 - probability), filler], axis=0
         ).astype(jnp.bfloat16)
-        part = pl.ds(i * width, width)
-        writes.append(pltpu.make_async_copy(stacked_ref.at[:, part], stacked_hbm.at[:, part], out_sems.at[i]))
-        writes[-1].start()
     copies[1].wait()
-    total = None
-    for i in range(count):
-        part = pair_sums(one_hot(ids_ref, tree, i * width, width), stacked_ref[:, i * width : (i + 1) * width])
-        total = part if total is None else total + part
-    write_sums(total, half, out_ref, 0)
-    for write in writes:
-        write.wait()
-
-
-def second_kernel(plan, slots, half, width, stacked_hbm, ids_hbm, out_ref, stacked_ref, ids_ref, sems):
-    rows = stacked_ref.shape[1]
-    count = rows // width
-    copies = [pltpu.make_async_copy(ids_hbm, ids_ref, sems.at[0])]
-    for i in range(count):
-        part = pl.ds(i * width, width)
-        copies.append(pltpu.make_async_copy(stacked_hbm.at[:, part], stacked_ref.at[:, part], sems.at[1 + i]))
-    for copy in copies:
-        copy.start()
-    tree = tree_rows(plan.code(own_device(plan), False), slots)
-    copies[0].wait()
-    total = None
-    for i in range(count):
-        copies[1 + i].wait()
-        part = pair_sums(one_hot(ids_ref, tree, i * width, width), stacked_ref[:, i * width : (i + 1) * width])
-        total = part if total is None else total + part
-    write_sums(total, half, out_ref, 0)
-
-
-def sums_kernel(plan, parts, half, width, stacked_ref, ids_ref, *out_refs):
-    device = own_device(plan)
-    rows = stacked_ref.shape[1]
-    todo = []
-    for (slots, other), out_ref in zip(parts, out_refs):
-        tree = tree_rows(plan.code(device, other), slots)
-        todo += [(tree[2 * i : 2 * i + 2], out_ref, i) for i in range(len(slots))]
-    for group in groups(todo, 4):
-        tree = [row for item in group for row in item[0]]
-        total = None
-        for first in range(0, rows, width):
-            part = pair_sums(one_hot(ids_ref, tree, first, width), stacked_ref[:, first : first + width])
-            total = part if total is None else total + part
-        for i, (_, out_ref, place) in enumerate(group):
-            write_sums(total[i * PAIR : (i + 1) * PAIR], half, out_ref, place)
+    add_up(plan, [(slots, True)], half, width, stacked_ref, ids_ref, (other_ref,))
+
+
+def sums_kernel(plan, parts, half, width, stacked_ref, ids_ref, _, *out_refs):
+    add_up(plan, parts, half, width, stacked_ref, ids_ref, out_refs)
 
 
 def sums_cost(count, half, rows):
@@ -208,55 +181,34 @@
     return pl.pallas_call(
         functools.partial(first_kernel, plan, slots, half, width),
         in_specs=[IN_HBM, IN_HBM, IN_HBM],
-        out_specs=[IN_HBM, IN_VMEM],
+        out_specs=[IN_VMEM, IN_VMEM],
         out_shape=[
-            jax.ShapeDtypeStruct((2 * half, rows), jnp.bfloat16),
-            jax.ShapeDtypeStruct((classes, 2 * PAIR * len(slots)), jnp.float32),
+            pltpu.VMEM((2 * half, rows), jnp.bfloat16),
+            pltpu.VMEM((classes, 2 * PAIR * len(slots)), jnp.float32),
         ],
         scratch_shapes=[
             pltpu.VMEM((classes, rows), jnp.float32),
             pltpu.VMEM((1, rows), jnp.int32),
             pltpu.VMEM(leaf_ids.shape, jnp.int32),
-            pltpu.VMEM((2 * half, rows), jnp.bfloat16),
             pltpu.SemaphoreType.DMA((2 + rows // width,)),
-            pltpu.SemaphoreType.DMA((rows // width,)),
         ],
-        compiler_params=pltpu.CompilerParams(vmem_limit_bytes=FIRST_VMEM_LIMIT),
+        compiler_params=pltpu.CompilerParams(vmem_limit_bytes=VMEM_LIMIT),
         cost_estimate=sums_cost(len(slots), half, rows),
         name="gradients_and_sums",
-    )(predict, labels.reshape(1, rows), leaf_ids)
-
-
-def second_sums(plan, stacked, leaf_ids, classes, slots):
-    height, rows = stacked.shape
-    width = chunk(rows, 2048)
-    return pl.pallas_call(
-        functools.partial(second_kernel, plan, slots, height // 2, width),
-        in_specs=[IN_HBM, IN_HBM],
-        out_specs=IN_VMEM,
-        out_shape=jax.ShapeDtypeStruct((classes, 2 * PAIR * len(slots)), jnp.float32),
-        scratch_shapes=[
-            pltpu.VMEM(stacked.shape, stacked.dtype),
-            pltpu.VMEM(leaf_ids.shape, jnp.int32),
-            pltpu.SemaphoreType.DMA((1 + rows // width,)),
-        ],
-        compiler_params=pltpu.CompilerParams(vmem_limit_bytes=FIRST_VMEM_LIMIT),
-        cost_estimate=sums_cost(len(slots), height // 2, rows),
-        name="second_sums",
-    )(stacked, leaf_ids)
-
-
-def more_sums(plan, stacked, leaf_ids, classes, parts):
+    )(*(pltpu.with_memory_space_constraint(x, pltpu.HBM) for x in (predict, labels.reshape(1, rows), leaf_ids)))
+
+
+def more_sums(plan, stacked, leaf_ids, classes, parts, earlier):
     height, rows = stacked.shape
     return pl.pallas_call(
         functools.partial(sums_kernel, plan, parts, height // 2, chunk(rows, 1024)),
-        in_specs=[IN_VMEM, IN_VMEM],
+        in_specs=[IN_VMEM, IN_VMEM, pl.BlockSpec(memory_space=pl.ANY)],
         out_specs=[IN_VMEM] * len(parts),
         out_shape=[jax.ShapeDtypeStruct((classes, 2 * PAIR * len(slots)), jnp.float32) for slots, _ in parts],
         compiler_params=pltpu.CompilerParams(vmem_limit_bytes=VMEM_LIMIT),
         cost_estimate=sums_cost(sum(len(slots) for slots, _ in parts), height // 2, rows),
         name="leaf_sums",
-    )(stacked, leaf_ids)
+    )(stacked, leaf_ids, earlier)
 
 
 def looked_up(plan, parts, value_refs, ids_ref, first, width):
@@ -368,10 +320,6 @@
     return values[0] if len(values) == 1 else jnp.concatenate(values, axis=1)
 
 
-def after(value, *earlier):
-    return lax.optimization_barrier((value, *earlier))[0]
-
-
 def solution(mesh):
     def shards(predict, labels, leaf_ids):
         classes = predict.shape[0]
@@ -387,18 +335,17 @@
         near = list(range(h // 4))
 
         stacked, far_other = first_sums(plan, predict, labels, leaf_ids, far, half)
-        far_core = exchange(far_other, 0)
-        far_own = second_sums(plan, stacked, leaf_ids, classes, far)
-        far_sums = far_own + far_core
+        (far_own,) = more_sums(plan, stacked, leaf_ids, classes, [(far, False)], far_other)
+        far_sums = far_own + exchange(far_other, 0)
         far_moved = exchange(far_sums, 1)
         other, middle_own = more_sums(
-            plan, after(stacked, far_sums), leaf_ids, classes, [(near + middle, True), (middle, False)]
+            plan, stacked, leaf_ids, classes, [(near + middle, True), (middle, False)], far_sums
         )
         rest = exchange(other, 0)
         cut = 2 * PAIR * len(near)
         middle_sums = middle_own + rest[:, cut:] + far_moved[:, cut:]
         middle_moved = exchange(middle_sums, 2)
-        (near_own,) = more_sums(plan, after(stacked, middle_sums), leaf_ids, classes, [(near, False)])
+        (near_own,) = more_sums(plan, stacked, leaf_ids, classes, [(near, False)], middle_sums)
         held = near_own + rest[:, :cut] + far_moved[:, :cut] + middle_moved
         for step in range(3, plan.steps):
             if step < plan.halvings:
@@ -421,15 +368,17 @@
         first = list(range(h // 2, h // 2 + len(near)))
         both = list(range(h // 2 + len(near), h))
         update = apply([(near, False), (near, True)], [near_values, near_theirs], None)
-        both_theirs = exchange(after(both_values, update), 0)
-        first_theirs = exchange(after(first_values, update), 0)
-        update = apply([(both, False), (both, True)], [both_values, both_theirs], update)
-        second_theirs = exchange(after(second_values, update), 0)
-        update = apply([(first, False), (first, True)], [first_values, first_theirs], update)
+        update, both_values, first_values, second_values = lax.optimization_barrier(
+            (update, both_values, first_values, second_values)
+        )
+        both_theirs = exchange(both_values, 0)
+        first_theirs = exchange(first_values, 0)
+        second_theirs = exchange(second_values, 0)
+        update = apply([(both, False), (first, False)], [both_values, first_values], update)
         pieces = [(slots, other) for other in (False, True) for slots in (near, middle, first, both)]
         values = [near_values, second_values, first_values, both_values]
         values += [near_theirs, second_theirs, first_theirs, both_theirs]
-        last = [(middle, False), (middle, True)]
+        last = [(middle, False), (both, True), (first, True), (middle, True)]
         return tuple(finish(plan, leaf_ids, update, predict, last, pieces, values))
 
     return jax.shard_map(

time: 62.5 us -> 54.9 us (0.88)
  Pallas kernels: 26.3 us -> 19.7 us
  other arithmetic: 1.22 us -> 0.22 us
  starting transfers between devices: 20.9 us -> 19.9 us
  waiting for transfers between devices: 12.4 us -> 13.4 us
    pallas_call x1 -> x0, Pallas kernels: 7.52 us -> none  [second_sums(): pl.pallas_call(functools.partial(second_kernel, plan, slots, height // 2,...]
    pallas_call x2 -> x3, Pallas kernels: 4.9 us -> 7.32 us  [more_sums(): pl.pallas_call(functools.partial(sums_kernel, plan, parts, height // 2, c...]
    pallas_call x3 -> x2, Pallas kernels: 5.26 us -> 3.39 us  [apply_values(): pl.pallas_call(functools.partial(apply_kernel, plan, parts, chunk(rows, 2...]
    pallas_call x1, Pallas kernels: 2.59 us -> 3.77 us  [finish(): pl.pallas_call(functools.partial(last_kernel, plan, parts, pieces, width)...]
    ppermute x14, starting transfers between devices: 20.9 us -> 19.9 us  [exchange(): return lax.ppermute(value, AXES, plan.permutation(*steps))]
    add x1, other arithmetic: 1.06 us -> 0.05 us  [shards(): far_sums = far_own + exchange(far_other, 0)]
    ppermute x14, waiting for transfers between devices: 12.4 us -> 13.4 us  [exchange(): return lax.ppermute(value, AXES, plan.permutation(*steps))]
    pallas_call x1, Pallas kernels: 6.01 us -> 5.24 us  [first_sums(): pl.pallas_call(functools.partial(first_kernel, plan, slots, half, width),...]
  transfers between devices with their start and end apart: 14 -> 14, of which waited for: 7 -> 7; matrix products, arithmetic and copies ran while one was open for 0% -> 0% of each run, Pallas kernels for 29% -> 20%
where the time goes in v4:
time: 54.9 us; the launch traced here: 54.2 us
  starting transfers between devices  19.9 us (36%)
  Pallas kernels  19.7 us (36%)
  waiting for transfers between devices  13.4 us (24%)
  between operations  0.93 us (2%)
    ppermute x14, starting transfers between devices, exchange(): return lax.ppermute(value, AXES, plan.permutation(*steps))  19.9 us
    ppermute x14, waiting for transfers between devices, exchange(): return lax.ppermute(value, AXES, plan.permutation(*steps))  13.4 us
    pallas_call x3, Pallas kernels, more_sums(): pl.pallas_call(functools.partial(sums_kernel, plan, parts, height // 2, c...  7.32 us
    pallas_call x1, Pallas kernels, first_sums(): pl.pallas_call(functools.partial(first_kernel, plan, slots, half, width),...  5.24 us
    pallas_call x1, Pallas kernels, finish(): pl.pallas_call(functools.partial(last_kernel, plan, parts, pieces, width)...  3.77 us
    pallas_call x2, Pallas kernels, apply_values(): pl.pallas_call(functools.partial(apply_kernel, plan, parts, chunk(rows, 2...  3.39 us
  transfers between devices with their start and end apart: 14, of which 7 were waited for; matrix products, arithmetic and copies ran while one was open for 0% of the time, Pallas kernels for 20%

profile of v4, /device:TPU:1, one launch (start us, length us, event | category | flops | bytes accessed | tf_op | source)
XLA Modules:
  0.0 54.2 jit_solution(10350979436213988352)
XLA Ops:
  0.6 0.0 copy-start
  0.6 5.2 %gradients_and_sums.1 = (bf16[224,8192]{1,0:T(8,128)(2,1)S(1)}, f32[100,1024]{1,0:T(8,128)S(1)}) custom-call(f32[100,8192]{1,0:T(8,128)} %refs_2_.1, s32[1,8192]{1,0:T(1,128)} %bitcast.1, s32[32,8192]{1,0:T(8,128)} %refs_0_.5), custom_call_target="tpu_custom_call" | custom-call | flops 1879048192 | bytes 3670016 | tf_op jit(solution)/shard_map/gradients_and_sums/pallas_call | solution.py:181
  5.9 0.1 collective-permute-start
  6.0 0.0 copy-done
  6.0 2.4 %leaf_sums.3 = f32[100,1024]{1,0:T(8,128)S(1)} custom-call(bf16[224,8192]{1,0:T(8,128)(2,1)S(1)} %get-tuple-element.10.stacked_ref, s32[32,8192]{1,0:T(8,128)S(1)} %copy-done, f32[100,1024]{1,0:T(8,128)S(1)} %get-tuple-element.11._), custom_call_target="tpu_custom_call" | custom-call | flops 1879048192 | bytes 3670016 | tf_op jit(solution)/shard_map/leaf_sums/pallas_call | solution.py:203
  8.4 0.0 collective-permute-done
  8.5 2.8 %collective-permute-start.2 = (f32[100,1024]{1,0:T(8,128)S(1)}, f32[100,1024]{1,0:T(8,128)S(1)}, u32[]{:S(2)}, u32[]{:S(2)}) collective-permute-start(f32[100,1024]{1,0:T(8,128)S(1)} %add.30._), channel_id=1, source_target_pairs={{0,8},{1,9},{2,10},{3,11},{4,20},{5,21},{6,22},{7,23},{8,0},{9,1},... | collective-permute-start | bytes 1228808 | tf_op jit(solution)/shard_map/ppermute | solution.py:330
  11.3 3.6 %leaf_sums.4 = (f32[100,1024]{1,0:T(8,128)S(1)}, f32[100,512]{1,0:T(8,128)S(1)}) custom-call(bf16[224,8192]{1,0:T(8,128)(2,1)S(1)} %get-tuple-element.10.stacked_ref, s32[32,8192]{1,0:T(8,128)S(1)} %copy-done, f32[100,1024]{1,0:T(8,128)S(1)} %add.30._), custom_call_target="tpu_custom_call" | custom-call | flops 2818572288 | bytes 3670016 | tf_op jit(solution)/shard_map/leaf_sums/pallas_call | solution.py:203
  14.8 0.3 collective-permute-start.1
  15.2 1.9 %collective-permute-done.2 = f32[100,1024]{1,0:T(8,128)S(1)} collective-permute-done((f32[100,1024]{1,0:T(8,128)S(1)}, f32[100,1024]{1,0:T(8,128)S(1)}, u32[]{:S(2)}, u32[]{:S(2)}) %collective-permute-start.2) | collective-permute-done | bytes 409632 | tf_op jit(solution)/shard_map/ppermute | solution.py:330
  17.1 0.0 collective-permute-done.1
  17.1 1.5 %collective-permute-start.3 = (f32[100,512]{1,0:T(8,128)S(1)}, f32[100,512]{1,0:T(8,128)S(1)}, u32[]{:S(2)}, u32[]{:S(2)}) collective-permute-start(f32[100,512]{1,0:T(8,128)S(1)} %slice_add_fusion.2._), channel_id=1, source_target_pairs={{0,16},{1,17},{2,18},{3,19},{4,12},{5,13},{6,14},{7,15},{8,24},{9,... | collective-permute-start | bytes 614408 | tf_op jit(solution)/shard_map/ppermute | solution.py:330
  18.6 1.3 %leaf_sums.5 = f32[100,512]{1,0:T(8,128)S(1)} custom-call(bf16[224,8192]{1,0:T(8,128)(2,1)S(1)} %get-tuple-element.10.stacked_ref, s32[32,8192]{1,0:T(8,128)S(1)} %copy-done, f32[100,512]{1,0:T(8,128)S(1)} %slice_add_fusion.2._), custom_call_target="tpu_custom_call" | custom-call | flops 939524096 | bytes 3670016 | tf_op jit(solution)/shard_map/leaf_sums/pallas_call | solution.py:203
  20.0 2.2 %collective-permute-done.3 = f32[100,512]{1,0:T(8,128)S(1)} collective-permute-done((f32[100,512]{1,0:T(8,128)S(1)}, f32[100,512]{1,0:T(8,128)S(1)}, u32[]{:S(2)}, u32[]{:S(2)}) %collective-permute-start.3) | collective-permute-done | bytes 204832 | tf_op jit(solution)/shard_map/ppermute | solution.py:330
  22.2 0.1 fusion
  22.3 2.6 %collective-permute-start.4 = (f32[100,256]{1,0:T(8,128)S(1)}, f32[100,256]{1,0:T(8,128)S(1)}, u32[]{:S(2)}, u32[]{:S(2)}) collective-permute-start(f32[100,256]{1,0:T(8,128)S(1)} %slice.37), channel_id=1, source_target_pairs={{0,1},{1,0},{2,3},{3,2},{4,6},{5,7},{6,4},{7,5},{8,9},{9,8},{10,11... | collective-permute-start | bytes 307208 | tf_op jit(solution)/shard_map/ppermute | solution.py:330
  24.9 2.1 %collective-permute-done.4 = f32[100,256]{1,0:T(8,128)S(1)} collective-permute-done((f32[100,256]{1,0:T(8,128)S(1)}, f32[100,256]{1,0:T(8,128)S(1)}, u32[]{:S(2)}, u32[]{:S(2)}) %collective-permute-start.4) | collective-permute-done | bytes 102432 | tf_op jit(solution)/shard_map/ppermute | solution.py:330
  27.0 1.9 %collective-permute-start.5 = (f32[100,256]{1,0:T(8,128)S(1)}, f32[100,256]{1,0:T(8,128)S(1)}, u32[]{:S(2)}, u32[]{:S(2)}) collective-permute-start(f32[100,256]{1,0:T(8,128)S(1)} %slice_add_fusion.4), channel_id=1, source_target_pairs={{0,2},{1,3},{2,0},{3,1},{4,5},{5,4},{6,7},{7,6},{8,10},{9,11},{10,... | collective-permute-start | bytes 307208 | tf_op jit(solution)/shard_map/ppermute | solution.py:330
  28.9 2.1 %collective-permute-done.5 = f32[100,256]{1,0:T(8,128)S(1)} collective-permute-done((f32[100,256]{1,0:T(8,128)S(1)}, f32[100,256]{1,0:T(8,128)S(1)}, u32[]{:S(2)}, u32[]{:S(2)}) %collective-permute-start.5) | collective-permute-done | bytes 102432 | tf_op jit(solution)/shard_map/ppermute | solution.py:330
  31.1 3.0 %collective-permute-start.6 = (f32[100,128]{1,0:T(8,128)S(1)}, f32[100,128]{1,0:T(8,128)S(1)}, u32[]{:S(2)}, u32[]{:S(2)}) collective-permute-start(f32[100,128]{1,0:T(8,128)S(1)} %fusion.1), channel_id=1, source_target_pairs={{0,1},{1,0},{2,3},{3,2},{4,6},{5,7},{6,4},{7,5},{8,9},{9,8},{10,11... | collective-permute-start | bytes 153608 | tf_op jit(solution)/shard_map/ppermute | solution.py:330
  34.0 2.1 %collective-permute-done.6 = f32[100,128]{1,0:T(8,128)S(1)} collective-permute-done((f32[100,128]{1,0:T(8,128)S(1)}, f32[100,128]{1,0:T(8,128)S(1)}, u32[]{:S(2)}, u32[]{:S(2)}) %collective-permute-start.6) | collective-permute-done | bytes 51232 | tf_op jit(solution)/shard_map/ppermute | solution.py:330
  36.1 3.0 %collective-permute-start.7 = (f32[100,256]{1,0:T(8,128)S(1)}, f32[100,256]{1,0:T(8,128)S(1)}, u32[]{:S(2)}, u32[]{:S(2)}) collective-permute-start(f32[100,256]{1,0:T(8,128)S(1)} %pad_maximum_fusion.refs_1_.refs_3_), channel_id=1, source_target_pairs={{0,4},{1,5},{2,6},{3,7},{4,0},{5,1},{6,2},{7,3},{8,12},{9,13},{10,... | collective-permute-start | bytes 307208 | tf_op jit(solution)/shard_map/ppermute | solution.py:330
  39.2 1.2 %collective-permute-start.10 = (f32[100,256]{1,0:T(8,128)S(1)}, f32[100,256]{1,0:T(8,128)S(1)}, u32[]{:S(2)}, u32[]{:S(2)}) collective-permute-start(f32[100,256]{1,0:T(8,128)S(1)} %pad_maximum_fusion.refs_1_.refs_3_), channel_id=1, source_target_pairs={{0,16},{1,17},{2,18},{3,19},{4,12},{5,13},{6,14},{7,15},{8,24},{9,... | collective-permute-start | bytes 307208 | tf_op jit(solution)/shard_map/ppermute | solution.py:330
  40.3 1.2 %collective-permute-start.9 = (f32[100,256]{1,0:T(8,128)S(1)}, f32[100,256]{1,0:T(8,128)S(1)}, u32[]{:S(2)}, u32[]{:S(2)}) collective-permute-start(f32[100,256]{1,0:T(8,128)S(1)} %pad_maximum_fusion.refs_1_.refs_3_), channel_id=1, source_target_pairs={{0,8},{1,9},{2,10},{3,11},{4,20},{5,21},{6,22},{7,23},{8,0},{9,1},... | collective-permute-start | bytes 307208 | tf_op jit(solution)/shard_map/ppermute | solution.py:330
  41.6 0.2 collective-permute-start.8
  41.8 0.0 collective-permute-done.7.refs_2_.refs_7_
  41.8 1.6 %apply_values.2.refs_3_ = f32[100,8192]{1,0:T(8,128)S(1)} custom-call(s32[32,8192]{1,0:T(8,128)S(1)} %copy-done, f32[100,256]{1,0:T(8,128)S(1)} %pad_maximum_fusion.refs_1_.refs_3_, f32[100,256]{1,0:T(8,128)S(1)} %collective-permute-done.7.refs_2_.refs_7_), custom_call_target="tpu_custom_call" | custom-call | flops 1677721600 | bytes 3276800 | tf_op jit(solution)/shard_map/apply_values/pallas_call | solution.py:250
  43.4 0.0 copy-start.1
  43.4 0.0 collective-permute-done.10.refs_4_
  43.4 1.3 %collective-permute-done.9.refs_2_.refs_5_ = f32[100,256]{1,0:T(8,128)S(1)} collective-permute-done((f32[100,256]{1,0:T(8,128)S(1)}, f32[100,256]{1,0:T(8,128)S(1)}, u32[]{:S(2)}, u32[]{:S(2)}) %collective-permute-start.9) | collective-permute-done | bytes 102432 | tf_op jit(solution)/shard_map/ppermute | solution.py:330
  44.7 1.7 %collective-permute-done.8.refs_1_.refs_6_ = f32[100,256]{1,0:T(8,128)S(1)} collective-permute-done((f32[100,256]{1,0:T(8,128)S(1)}, f32[100,256]{1,0:T(8,128)S(1)}, u32[]{:S(2)}, u32[]{:S(2)}) %collective-permute-start.8) | collective-permute-done | bytes 102432 | tf_op jit(solution)/shard_map/ppermute | solution.py:330
  46.3 1.5 %collective-permute-start.11 = (f32[100,256]{1,0:T(8,128)S(1)}, f32[100,256]{1,0:T(8,128)S(1)}, u32[]{:S(2)}, u32[]{:S(2)}) collective-permute-start(f32[100,256]{1,0:T(8,128)S(1)} %collective-permute-done.10.refs_4_), channel_id=1, source_target_pairs={{0,4},{1,5},{2,6},{3,7},{4,0},{5,1},{6,2},{7,3},{8,12},{9,13},{10,... | collective-permute-start | bytes 307208 | tf_op jit(solution)/shard_map/ppermute | solution.py:330
  47.9 0.0 collective-permute-start.13
  47.9 0.5 collective-permute-start.12
  48.4 1.8 %apply_values.3.refs_1_ = f32[100,8192]{1,0:T(8,128)S(1)} custom-call(s32[32,8192]{1,0:T(8,128)S(1)} %copy-done, f32[100,256]{1,0:T(8,128)S(1)} %collective-permute-done.8.refs_1_.refs_6_, f32[100,256]{1,0:T(8,128)S(1)} %collective-permute-done.9.refs_2_.refs_5_, f32[100,8192]{1,0:T(8,128)S(1)} %apply_values.2.refs_3_), custom_call_target="tpu_custom_call", output_to_operand_aliasing={{}: (3, {})} | custom-call | flops 1677721600 | bytes 3276800 | tf_op jit(solution)/shard_map/apply_values/pallas_call | solution.py:250
  50.2 0.0 collective-permute-done.11.refs_8_
  50.2 0.0 collective-permute-done.13.refs_10_
  50.2 0.0 collective-permute-done.12.refs_9_
  50.2 0.0 copy-done.1
  50.2 3.8 %apply_last_values.1 = (f32[100,8192]{1,0:T(8,128)}, f32[100,512]{1,0:T(8,128)}) custom-call(s32[32,8192]{1,0:T(8,128)S(1)} %copy-done, f32[100,8192]{1,0:T(8,128)S(1)} %apply_values.3.refs_1_, f32[100,8192]{1,0:T(8,128)S(1)} %copy-done.1, f32[100,256]{1,0:T(8,128)S(1)} %pad_maximum_fusion.refs_1_.refs_3_, f32[100,256]{1,0:T(8,128)S(1)} %collective-permute-done.10.refs_4_, ...), custom_call_target="tpu_custom_call" | custom-call | flops 3355443200 | bytes 3276800 | tf_op jit(solution)/shard_map/apply_last_values/pallas_call | solution.py:297
  (7 shorter events, 0.2 us)
Async XLA Ops:
  0.6 5.4 %copy-start = (s32[32,8192]{1,0:T(8,128)S(1)}, s32[32,8192]{1,0:T(8,128)}, u32[]{:S(2)}) copy-start(s32[32,8192]{1,0:T(8,128)} %refs_0_.5) | copy-start | bytes 3145732
  5.9 2.6 %collective-permute-start = (f32[100,1024]{1,0:T(8,128)S(1)}, f32[100,1024]{1,0:T(8,128)S(1)}, u32[]{:S(2)}, u32[]{:S(2)}) collective-permute-start(f32[100,1024]{1,0:T(8,128)S(1)} %get-tuple-element.11._), channel_id=1, source_target_pairs={{0,4},{1,5},{2,6},{3,7},{4,0},{5,1},{6,2},{7,3},{8,12},{9,13},{10,... | collective-permute-start | bytes 1228808 | tf_op jit(solution)/shard_map/ppermute | solution.py:330
  8.5 8.6 %collective-permute-start.2 = (f32[100,1024]{1,0:T(8,128)S(1)}, f32[100,1024]{1,0:T(8,128)S(1)}, u32[]{:S(2)}, u32[]{:S(2)}) collective-permute-start(f32[100,1024]{1,0:T(8,128)S(1)} %add.30._), channel_id=1, source_target_pairs={{0,8},{1,9},{2,10},{3,11},{4,20},{5,21},{6,22},{7,23},{8,0},{9,1},... | collective-permute-start | bytes 1228808 | tf_op jit(solution)/shard_map/ppermute | solution.py:330
  14.8 2.2 %collective-permute-start.1 = (f32[100,1024]{1,0:T(8,128)S(1)}, f32[100,1024]{1,0:T(8,128)S(1)}, u32[]{:S(2)}, u32[]{:S(2)}) collective-permute-start(f32[100,1024]{1,0:T(8,128)S(1)} %get-tuple-element.13), channel_id=1, source_target_pairs={{0,4},{1,5},{2,6},{3,7},{4,0},{5,1},{6,2},{7,3},{8,12},{9,13},{10,... | collective-permute-start | bytes 1228808 | tf_op jit(solution)/shard_map/ppermute | solution.py:330
  17.1 5.1 %collective-permute-start.3 = (f32[100,512]{1,0:T(8,128)S(1)}, f32[100,512]{1,0:T(8,128)S(1)}, u32[]{:S(2)}, u32[]{:S(2)}) collective-permute-start(f32[100,512]{1,0:T(8,128)S(1)} %slice_add_fusion.2._), channel_id=1, source_target_pairs={{0,16},{1,17},{2,18},{3,19},{4,12},{5,13},{6,14},{7,15},{8,24},{9,... | collective-permute-start | bytes 614408 | tf_op jit(solution)/shard_map/ppermute | solution.py:330
  22.3 4.7 %collective-permute-start.4 = (f32[100,256]{1,0:T(8,128)S(1)}, f32[100,256]{1,0:T(8,128)S(1)}, u32[]{:S(2)}, u32[]{:S(2)}) collective-permute-start(f32[100,256]{1,0:T(8,128)S(1)} %slice.37), channel_id=1, source_target_pairs={{0,1},{1,0},{2,3},{3,2},{4,6},{5,7},{6,4},{7,5},{8,9},{9,8},{10,11... | collective-permute-start | bytes 307208 | tf_op jit(solution)/shard_map/ppermute | solution.py:330
  27.0 4.0 %collective-permute-start.5 = (f32[100,256]{1,0:T(8,128)S(1)}, f32[100,256]{1,0:T(8,128)S(1)}, u32[]{:S(2)}, u32[]{:S(2)}) collective-permute-start(f32[100,256]{1,0:T(8,128)S(1)} %slice_add_fusion.4), channel_id=1, source_target_pairs={{0,2},{1,3},{2,0},{3,1},{4,5},{5,4},{6,7},{7,6},{8,10},{9,11},{10,... | collective-permute-start | bytes 307208 | tf_op jit(solution)/shard_map/ppermute | solution.py:330
  31.1 5.1 %collective-permute-start.6 = (f32[100,128]{1,0:T(8,128)S(1)}, f32[100,128]{1,0:T(8,128)S(1)}, u32[]{:S(2)}, u32[]{:S(2)}) collective-permute-start(f32[100,128]{1,0:T(8,128)S(1)} %fusion.1), channel_id=1, source_target_pairs={{0,1},{1,0},{2,3},{3,2},{4,6},{5,7},{6,4},{7,5},{8,9},{9,8},{10,11... | collective-permute-start | bytes 153608 | tf_op jit(solution)/shard_map/ppermute | solution.py:330
  36.1 5.7 %collective-permute-start.7 = (f32[100,256]{1,0:T(8,128)S(1)}, f32[100,256]{1,0:T(8,128)S(1)}, u32[]{:S(2)}, u32[]{:S(2)}) collective-permute-start(f32[100,256]{1,0:T(8,128)S(1)} %pad_maximum_fusion.refs_1_.refs_3_), channel_id=1, source_target_pairs={{0,4},{1,5},{2,6},{3,7},{4,0},{5,1},{6,2},{7,3},{8,12},{9,13},{10,... | collective-permute-start | bytes 307208 | tf_op jit(solution)/shard_map/ppermute | solution.py:330
  39.2 4.2 %collective-permute-start.10 = (f32[100,256]{1,0:T(8,128)S(1)}, f32[100,256]{1,0:T(8,128)S(1)}, u32[]{:S(2)}, u32[]{:S(2)}) collective-permute-start(f32[100,256]{1,0:T(8,128)S(1)} %pad_maximum_fusion.refs_1_.refs_3_), channel_id=1, source_target_pairs={{0,16},{1,17},{2,18},{3,19},{4,12},{5,13},{6,14},{7,15},{8,24},{9,... | collective-permute-start | bytes 307208 | tf_op jit(solution)/shard_map/ppermute | solution.py:330
  40.3 4.4 %collective-permute-start.9 = (f32[100,256]{1,0:T(8,128)S(1)}, f32[100,256]{1,0:T(8,128)S(1)}, u32[]{:S(2)}, u32[]{:S(2)}) collective-permute-start(f32[100,256]{1,0:T(8,128)S(1)} %pad_maximum_fusion.refs_1_.refs_3_), channel_id=1, source_target_pairs={{0,8},{1,9},{2,10},{3,11},{4,20},{5,21},{6,22},{7,23},{8,0},{9,1},... | collective-permute-start | bytes 307208 | tf_op jit(solution)/shard_map/ppermute | solution.py:330
  41.6 4.8 %collective-permute-start.8 = (f32[100,256]{1,0:T(8,128)S(1)}, f32[100,256]{1,0:T(8,128)S(1)}, u32[]{:S(2)}, u32[]{:S(2)}) collective-permute-start(f32[100,256]{1,0:T(8,128)S(1)} %pad_maximum_fusion.refs_1_.refs_3_), channel_id=1, source_target_pairs={{0,24},{1,25},{2,26},{3,27},{4,28},{5,29},{6,30},{7,31},{8,16},{9,... | collective-permute-start | bytes 307208 | tf_op jit(solution)/shard_map/ppermute | solution.py:330
  43.4 6.8 %copy-start.1 = (f32[100,8192]{1,0:T(8,128)S(1)}, f32[100,8192]{1,0:T(8,128)}, u32[]{:S(2)}) copy-start(f32[100,8192]{1,0:T(8,128)} %refs_2_.1) | copy-start | bytes 9830404
  46.3 3.8 %collective-permute-start.11 = (f32[100,256]{1,0:T(8,128)S(1)}, f32[100,256]{1,0:T(8,128)S(1)}, u32[]{:S(2)}, u32[]{:S(2)}) collective-permute-start(f32[100,256]{1,0:T(8,128)S(1)} %collective-permute-done.10.refs_4_), channel_id=1, source_target_pairs={{0,4},{1,5},{2,6},{3,7},{4,0},{5,1},{6,2},{7,3},{8,12},{9,13},{10,... | collective-permute-start | bytes 307208 | tf_op jit(solution)/shard_map/ppermute | solution.py:330
  47.9 2.3 %collective-permute-start.13 = (f32[100,256]{1,0:T(8,128)S(1)}, f32[100,256]{1,0:T(8,128)S(1)}, u32[]{:S(2)}, u32[]{:S(2)}) collective-permute-start(f32[100,256]{1,0:T(8,128)S(1)} %collective-permute-done.8.refs_1_.refs_6_), channel_id=1, source_target_pairs={{0,4},{1,5},{2,6},{3,7},{4,0},{5,1},{6,2},{7,3},{8,12},{9,13},{10,... | collective-permute-start | bytes 307208 | tf_op jit(solution)/shard_map/ppermute | solution.py:330
  47.9 2.4 %collective-permute-start.12 = (f32[100,256]{1,0:T(8,128)S(1)}, f32[100,256]{1,0:T(8,128)S(1)}, u32[]{:S(2)}, u32[]{:S(2)}) collective-permute-start(f32[100,256]{1,0:T(8,128)S(1)} %collective-permute-done.9.refs_2_.refs_5_), channel_id=1, source_target_pairs={{0,4},{1,5},{2,6},{3,7},{4,0},{5,1},{6,2},{7,3},{8,12},{9,13},{10,... | collective-permute-start | bytes 307208 | tf_op jit(solution)/shard_map/ppermute | solution.py:330

commit v5 on v4

--- a/solution.py
+++ b/solution.py
@@ -330,56 +330,51 @@
             return lax.ppermute(value, AXES, plan.permutation(*steps))
 
         h = plan.pairs // 2
+        unit = h // 8
         far = list(range(h // 2, h))
-        middle = list(range(h // 4, h // 2))
-        near = list(range(h // 4))
+        near = list(range(h // 2))
+        own, by_3, by_2, by_both = (near[i * unit : (i + 1) * unit] for i in range(4))
 
         stacked, far_other = first_sums(plan, predict, labels, leaf_ids, far, half)
         (far_own,) = more_sums(plan, stacked, leaf_ids, classes, [(far, False)], far_other)
         far_sums = far_own + exchange(far_other, 0)
         far_moved = exchange(far_sums, 1)
-        other, middle_own = more_sums(
-            plan, stacked, leaf_ids, classes, [(near + middle, True), (middle, False)], far_sums
+        near_other, upper_own = more_sums(
+            plan, stacked, leaf_ids, classes, [(near, True), (by_2 + by_both, False)], far_sums
         )
-        rest = exchange(other, 0)
-        cut = 2 * PAIR * len(near)
-        middle_sums = middle_own + rest[:, cut:] + far_moved[:, cut:]
-        middle_moved = exchange(middle_sums, 2)
-        (near_own,) = more_sums(plan, stacked, leaf_ids, classes, [(near, False)], middle_sums)
-        held = near_own + rest[:, :cut] + far_moved[:, :cut] + middle_moved
-        for step in range(3, plan.steps):
+        near_core = exchange(near_other, 0)
+        (lower_own,) = more_sums(plan, stacked, leaf_ids, classes, [(own + by_3, False)], near_other)
+
+        def quarter(i):
+            part = slice(2 * PAIR * unit * i, 2 * PAIR * unit * (i + 1))
+            inner = slice(2 * PAIR * unit * (i % 2), 2 * PAIR * unit * (i % 2 + 1))
+            return (upper_own if i > 1 else lower_own)[:, inner] + near_core[:, part] + far_moved[:, part]
+
+        held = quarter(0)
+        held = held + exchange(quarter(3), 2, 3) + exchange(quarter(1), 3) + exchange(quarter(2), 2)
+        for step in range(4, plan.steps):
             if step < plan.halvings:
                 keep = held.shape[1] // 2
                 held = held[:, :keep] + exchange(held[:, keep:], step)
             else:
                 held = held + exchange(held, step)
-        near_values = newton(held)
-        for step in reversed(range(3, plan.halvings)):
-            near_values = jnp.concatenate([near_values, exchange(near_values, step)], axis=1)
-
+        values = newton(held)
+        for step in reversed(range(4, plan.halvings)):
+            values = jnp.concatenate([values, exchange(values, step)], axis=1)
+
+        moved = [exchange(values, 3), exchange(values, 2), exchange(values, 2, 3)]
+        near_values = jnp.concatenate([values] + moved, axis=1)
+        far_values = exchange(near_values, 1)
         near_theirs = exchange(near_values, 0)
-        both_values = exchange(near_values, 1, 2)
-        first_values = exchange(near_values, 1)
-        second_values = exchange(near_values, 2)
-
-        def apply(parts, values, update):
-            return apply_values(plan, leaf_ids, parts, values, update)
-
-        first = list(range(h // 2, h // 2 + len(near)))
-        both = list(range(h // 2 + len(near), h))
-        update = apply([(near, False), (near, True)], [near_values, near_theirs], None)
-        update, both_values, first_values, second_values = lax.optimization_barrier(
-            (update, both_values, first_values, second_values)
+        update = apply_values(
+            plan, leaf_ids, [(near, False), (near, True)], [near_values, near_theirs], None
         )
-        both_theirs = exchange(both_values, 0)
-        first_theirs = exchange(first_values, 0)
-        second_theirs = exchange(second_values, 0)
-        update = apply([(both, False), (first, False)], [both_values, first_values], update)
-        pieces = [(slots, other) for other in (False, True) for slots in (near, middle, first, both)]
-        values = [near_values, second_values, first_values, both_values]
-        values += [near_theirs, second_theirs, first_theirs, both_theirs]
-        last = [(middle, False), (both, True), (first, True), (middle, True)]
-        return tuple(finish(plan, leaf_ids, update, predict, last, pieces, values))
+        far_values, update = lax.optimization_barrier((far_values, update))
+        far_theirs = exchange(far_values, 0)
+        update = apply_values(plan, leaf_ids, [(far, False)], [far_values], update)
+        pieces = [(near, False), (far, False), (near, True), (far, True)]
+        values = [near_values, far_values, near_theirs, far_theirs]
+        return tuple(finish(plan, leaf_ids, update, predict, [(far, True)], pieces, values))
 
     return jax.shard_map(
         shards,

time: 54.9 us -> 50.9 us (0.927); the launches traced: 54.2 us -> 50.8 us
  starting transfers between devices: 19.9 us -> 18 us
  waiting for transfers between devices: 13.4 us -> 11.9 us
    ppermute x14 -> x13, starting transfers between devices: 19.9 us -> 18 us  [exchange(): return lax.ppermute(value, AXES, plan.permutation(*steps))]
    ppermute x14 -> x13, waiting for transfers between devices: 13.4 us -> 11.9 us  [exchange(): return lax.ppermute(value, AXES, plan.permutation(*steps))]
    pallas_call x1, Pallas kernels: 3.77 us -> 2.59 us  [finish(): pl.pallas_call(functools.partial(last_kernel, plan, parts, pieces, width)...]
    pallas_call x2, Pallas kernels: 3.39 us -> 4.57 us  [apply_values(): pl.pallas_call(functools.partial(apply_kernel, plan, parts, chunk(rows, 2...]
  transfers between devices with their start and end apart: 14 -> 13, of which waited for: 7 -> 8; matrix products, arithmetic and copies ran while one was open for 0% -> 0% of each run, Pallas kernels for 20% -> 23%
where the time goes in v5:
time: 50.9 us; the launch traced here: 50.8 us
  Pallas kernels  19.7 us (39%)
  starting transfers between devices  18 us (35%)
  waiting for transfers between devices  11.9 us (23%)
  between operations  0.9 us (2%)
    ppermute x13, starting transfers between devices, exchange(): return lax.ppermute(value, AXES, plan.permutation(*steps))  18 us
    ppermute x13, waiting for transfers between devices, exchange(): return lax.ppermute(value, AXES, plan.permutation(*steps))  11.9 us
    pallas_call x3, Pallas kernels, more_sums(): pl.pallas_call(functools.partial(sums_kernel, plan, parts, height // 2, c...  7.33 us
    pallas_call x1, Pallas kernels, first_sums(): pl.pallas_call(functools.partial(first_kernel, plan, slots, half, width),...  5.24 us
    pallas_call x2, Pallas kernels, apply_values(): pl.pallas_call(functools.partial(apply_kernel, plan, parts, chunk(rows, 2...  4.57 us
    pallas_call x1, Pallas kernels, finish(): pl.pallas_call(functools.partial(last_kernel, plan, parts, pieces, width)...  2.59 us
  transfers between devices with their start and end apart: 13, of which 8 were waited for; matrix products, arithmetic and copies ran while one was open for 0% of the time, Pallas kernels for 23%

profile of v5, /device:TPU:1, one launch (start us, length us, event | category | flops | bytes accessed | tf_op | source)
XLA Modules:
  0.0 50.8 jit_solution(3652206238721779370)
XLA Ops:
  0.6 0.0 copy-start
  0.6 5.2 %gradients_and_sums.1 = (bf16[224,8192]{1,0:T(8,128)(2,1)S(1)}, f32[100,1024]{1,0:T(8,128)S(1)}) custom-call(f32[100,8192]{1,0:T(8,128)} %refs_2_.1, s32[1,8192]{1,0:T(1,128)} %bitcast.1, s32[32,8192]{1,0:T(8,128)} %refs_0_.5), custom_call_target="tpu_custom_call" | custom-call | flops 1879048192 | bytes 3670016 | tf_op jit(solution)/shard_map/gradients_and_sums/pallas_call | solution.py:181
  5.9 0.1 collective-permute-start
  6.0 0.0 copy-done
  6.0 2.4 %leaf_sums.3 = f32[100,1024]{1,0:T(8,128)S(1)} custom-call(bf16[224,8192]{1,0:T(8,128)(2,1)S(1)} %get-tuple-element.8.stacked_ref, s32[32,8192]{1,0:T(8,128)S(1)} %copy-done, f32[100,1024]{1,0:T(8,128)S(1)} %get-tuple-element.9._), custom_call_target="tpu_custom_call" | custom-call | flops 1879048192 | bytes 3670016 | tf_op jit(solution)/shard_map/leaf_sums/pallas_call | solution.py:203
  8.4 0.0 collective-permute-done
  8.5 2.8 %collective-permute-start.2 = (f32[100,1024]{1,0:T(8,128)S(1)}, f32[100,1024]{1,0:T(8,128)S(1)}, u32[]{:S(2)}, u32[]{:S(2)}) collective-permute-start(f32[100,1024]{1,0:T(8,128)S(1)} %add.45._), channel_id=1, source_target_pairs={{0,8},{1,9},{2,10},{3,11},{4,20},{5,21},{6,22},{7,23},{8,0},{9,1},... | collective-permute-start | bytes 1228808 | tf_op jit(solution)/shard_map/ppermute | solution.py:330
  11.3 3.6 %leaf_sums.4 = (f32[100,1024]{1,0:T(8,128)S(1)}, f32[100,512]{1,0:T(8,128)S(1)}) custom-call(bf16[224,8192]{1,0:T(8,128)(2,1)S(1)} %get-tuple-element.8.stacked_ref, s32[32,8192]{1,0:T(8,128)S(1)} %copy-done, f32[100,1024]{1,0:T(8,128)S(1)} %add.45._), custom_call_target="tpu_custom_call" | custom-call | flops 2818572288 | bytes 3670016 | tf_op jit(solution)/shard_map/leaf_sums/pallas_call | solution.py:203
  14.8 0.3 collective-permute-start.1
  15.2 1.3 %leaf_sums.5 = f32[100,512]{1,0:T(8,128)S(1)} custom-call(bf16[224,8192]{1,0:T(8,128)(2,1)S(1)} %get-tuple-element.8.stacked_ref, s32[32,8192]{1,0:T(8,128)S(1)} %copy-done, f32[100,1024]{1,0:T(8,128)S(1)} %get-tuple-element.10._), custom_call_target="tpu_custom_call" | custom-call | flops 939524096 | bytes 3670016 | tf_op jit(solution)/shard_map/leaf_sums/pallas_call | solution.py:203
  16.5 0.6 %collective-permute-done.2 = f32[100,1024]{1,0:T(8,128)S(1)} collective-permute-done((f32[100,1024]{1,0:T(8,128)S(1)}, f32[100,1024]{1,0:T(8,128)S(1)}, u32[]{:S(2)}, u32[]{:S(2)}) %collective-permute-start.2) | collective-permute-done | bytes 409632 | tf_op jit(solution)/shard_map/ppermute | solution.py:330
  17.1 0.0 collective-permute-done.1
  17.1 0.1 slice_add_fusion.4
  17.2 3.5 %collective-permute-start.3 = (f32[100,256]{1,0:T(8,128)S(1)}, f32[100,256]{1,0:T(8,128)S(1)}, u32[]{:S(2)}, u32[]{:S(2)}) collective-permute-start(f32[100,256]{1,0:T(8,128)S(1)} %get-tuple-element.14), channel_id=1, source_target_pairs={{0,17},{1,16},{2,19},{3,18},{4,14},{5,15},{6,12},{7,13},{8,25},{9,... | collective-permute-start | bytes 307208 | tf_op jit(solution)/shard_map/ppermute | solution.py:330
  20.7 0.3 collective-permute-start.5
  20.9 0.1 collective-permute-start.4
  21.0 2.9 %collective-permute-done.3 = f32[100,256]{1,0:T(8,128)S(1)} collective-permute-done((f32[100,256]{1,0:T(8,128)S(1)}, f32[100,256]{1,0:T(8,128)S(1)}, u32[]{:S(2)}, u32[]{:S(2)}) %collective-permute-start.3) | collective-permute-done | bytes 102432 | tf_op jit(solution)/shard_map/ppermute | solution.py:330
  23.9 0.6 %collective-permute-done.5 = f32[100,256]{1,0:T(8,128)S(1)} collective-permute-done((f32[100,256]{1,0:T(8,128)S(1)}, f32[100,256]{1,0:T(8,128)S(1)}, u32[]{:S(2)}, u32[]{:S(2)}) %collective-permute-start.5) | collective-permute-done | bytes 102432 | tf_op jit(solution)/shard_map/ppermute | solution.py:330
  24.5 1.0 %collective-permute-done.4 = f32[100,256]{1,0:T(8,128)S(1)} collective-permute-done((f32[100,256]{1,0:T(8,128)S(1)}, f32[100,256]{1,0:T(8,128)S(1)}, u32[]{:S(2)}, u32[]{:S(2)}) %collective-permute-start.4) | collective-permute-done | bytes 102432 | tf_op jit(solution)/shard_map/ppermute | solution.py:330
  25.5 0.1 fusion.2
  25.6 1.5 %collective-permute-start.6 = (f32[100,256]{1,0:T(8,128)S(1)}, f32[100,256]{1,0:T(8,128)S(1)}, u32[]{:S(2)}, u32[]{:S(2)}) collective-permute-start(f32[100,256]{1,0:T(8,128)S(1)} %fusion.2), channel_id=1, source_target_pairs={{0,2},{1,3},{2,0},{3,1},{4,5},{5,4},{6,7},{7,6},{8,10},{9,11},{10,... | collective-permute-start | bytes 307208 | tf_op jit(solution)/shard_map/ppermute | solution.py:330
  27.1 2.1 %collective-permute-done.6 = f32[100,256]{1,0:T(8,128)S(1)} collective-permute-done((f32[100,256]{1,0:T(8,128)S(1)}, f32[100,256]{1,0:T(8,128)S(1)}, u32[]{:S(2)}, u32[]{:S(2)}) %collective-permute-start.6) | collective-permute-done | bytes 102432 | tf_op jit(solution)/shard_map/ppermute | solution.py:330
  29.2 2.9 %collective-permute-start.9 = (f32[100,128]{1,0:T(8,128)S(1)}, f32[100,128]{1,0:T(8,128)S(1)}, u32[]{:S(2)}, u32[]{:S(2)}) collective-permute-start(f32[100,128]{1,0:T(8,128)S(1)} %fusion.3), channel_id=1, source_target_pairs={{0,17},{1,16},{2,19},{3,18},{4,14},{5,15},{6,12},{7,13},{8,25},{9,... | collective-permute-start | bytes 153608 | tf_op jit(solution)/shard_map/ppermute | solution.py:330
  32.1 1.2 %collective-permute-start.8 = (f32[100,128]{1,0:T(8,128)S(1)}, f32[100,128]{1,0:T(8,128)S(1)}, u32[]{:S(2)}, u32[]{:S(2)}) collective-permute-start(f32[100,128]{1,0:T(8,128)S(1)} %fusion.3), channel_id=1, source_target_pairs={{0,16},{1,17},{2,18},{3,19},{4,12},{5,13},{6,14},{7,15},{8,24},{9,... | collective-permute-start | bytes 153608 | tf_op jit(solution)/shard_map/ppermute | solution.py:330
  33.4 0.2 collective-permute-start.7
  33.6 1.9 %collective-permute-done.9 = f32[100,128]{1,0:T(8,128)S(1)} collective-permute-done((f32[100,128]{1,0:T(8,128)S(1)}, f32[100,128]{1,0:T(8,128)S(1)}, u32[]{:S(2)}, u32[]{:S(2)}) %collective-permute-start.9) | collective-permute-done | bytes 51232 | tf_op jit(solution)/shard_map/ppermute | solution.py:330
  35.5 0.0 collective-permute-done.8
  35.5 1.8 %collective-permute-done.7 = f32[100,128]{1,0:T(8,128)S(1)} collective-permute-done((f32[100,128]{1,0:T(8,128)S(1)}, f32[100,128]{1,0:T(8,128)S(1)}, u32[]{:S(2)}, u32[]{:S(2)}) %collective-permute-start.7) | collective-permute-done | bytes 51232 | tf_op jit(solution)/shard_map/ppermute | solution.py:330
  37.3 3.0 %collective-permute-start.11 = (f32[100,512]{1,0:T(8,128)S(1)}, f32[100,512]{1,0:T(8,128)S(1)}, u32[]{:S(2)}, u32[]{:S(2)}) collective-permute-start(f32[100,512]{1,0:T(8,128)S(1)} %pad_maximum_fusion.refs_1_.refs_3_), channel_id=1, source_target_pairs={{0,4},{1,5},{2,6},{3,7},{4,0},{5,1},{6,2},{7,3},{8,12},{9,13},{10,... | collective-permute-start | bytes 614408 | tf_op jit(solution)/shard_map/ppermute | solution.py:330
  40.3 1.1 %collective-permute-start.10 = (f32[100,512]{1,0:T(8,128)S(1)}, f32[100,512]{1,0:T(8,128)S(1)}, u32[]{:S(2)}, u32[]{:S(2)}) collective-permute-start(f32[100,512]{1,0:T(8,128)S(1)} %pad_maximum_fusion.refs_1_.refs_3_), channel_id=1, source_target_pairs={{0,8},{1,9},{2,10},{3,11},{4,20},{5,21},{6,22},{7,23},{8,0},{9,1},... | collective-permute-start | bytes 614408 | tf_op jit(solution)/shard_map/ppermute | solution.py:330
  41.4 0.0 collective-permute-done.11.refs_2_.refs_5_
  41.4 2.8 %apply_values.2.refs_2_ = f32[100,8192]{1,0:T(8,128)S(1)} custom-call(s32[32,8192]{1,0:T(8,128)S(1)} %copy-done, f32[100,512]{1,0:T(8,128)S(1)} %pad_maximum_fusion.refs_1_.refs_3_, f32[100,512]{1,0:T(8,128)S(1)} %collective-permute-done.11.refs_2_.refs_5_), custom_call_target="tpu_custom_call" | custom-call | flops 3355443200 | bytes 3276800 | tf_op jit(solution)/shard_map/apply_values/pallas_call | solution.py:250
  44.1 0.0 copy-start.1
  44.1 1.1 %collective-permute-done.10.refs_1_.refs_4_ = f32[100,512]{1,0:T(8,128)S(1)} collective-permute-done((f32[100,512]{1,0:T(8,128)S(1)}, f32[100,512]{1,0:T(8,128)S(1)}, u32[]{:S(2)}, u32[]{:S(2)}) %collective-permute-start.10) | collective-permute-done | bytes 204832 | tf_op jit(solution)/shard_map/ppermute | solution.py:330
  45.2 0.9 %collective-permute-start.12 = (f32[100,512]{1,0:T(8,128)S(1)}, f32[100,512]{1,0:T(8,128)S(1)}, u32[]{:S(2)}, u32[]{:S(2)}) collective-permute-start(f32[100,512]{1,0:T(8,128)S(1)} %collective-permute-done.10.refs_1_.refs_4_), channel_id=1, source_target_pairs={{0,4},{1,5},{2,6},{3,7},{4,0},{5,1},{6,2},{7,3},{8,12},{9,13},{10,... | collective-permute-start | bytes 614408 | tf_op jit(solution)/shard_map/ppermute | solution.py:330
  46.2 1.8 %apply_values.3.refs_1_ = f32[100,8192]{1,0:T(8,128)S(1)} custom-call(s32[32,8192]{1,0:T(8,128)S(1)} %copy-done, f32[100,512]{1,0:T(8,128)S(1)} %collective-permute-done.10.refs_1_.refs_4_, f32[100,8192]{1,0:T(8,128)S(1)} %apply_values.2.refs_2_), custom_call_target="tpu_custom_call", output_to_operand_aliasing={{}: (2, {})} | custom-call | flops 1677721600 | bytes 3276800 | tf_op jit(solution)/shard_map/apply_values/pallas_call | solution.py:250
  48.0 0.0 collective-permute-done.12.refs_6_
  48.0 0.0 copy-done.1
  48.0 2.6 %apply_last_values.1 = (f32[100,8192]{1,0:T(8,128)}, f32[100,512]{1,0:T(8,128)}) custom-call(s32[32,8192]{1,0:T(8,128)S(1)} %copy-done, f32[100,8192]{1,0:T(8,128)S(1)} %apply_values.3.refs_1_, f32[100,8192]{1,0:T(8,128)S(1)} %copy-done.1, f32[100,512]{1,0:T(8,128)S(1)} %pad_maximum_fusion.refs_1_.refs_3_, ...), custom_call_target="tpu_custom_call" | custom-call | flops 1677721600 | bytes 3276800 | tf_op jit(solution)/shard_map/apply_last_values/pallas_call | solution.py:297
  (4 shorter events, 0.1 us)
Async XLA Ops:
  0.6 5.4 %copy-start = (s32[32,8192]{1,0:T(8,128)S(1)}, s32[32,8192]{1,0:T(8,128)}, u32[]{:S(2)}) copy-start(s32[32,8192]{1,0:T(8,128)} %refs_0_.5) | copy-start | bytes 3145732
  5.9 2.6 %collective-permute-start = (f32[100,1024]{1,0:T(8,128)S(1)}, f32[100,1024]{1,0:T(8,128)S(1)}, u32[]{:S(2)}, u32[]{:S(2)}) collective-permute-start(f32[100,1024]{1,0:T(8,128)S(1)} %get-tuple-element.9._), channel_id=1, source_target_pairs={{0,4},{1,5},{2,6},{3,7},{4,0},{5,1},{6,2},{7,3},{8,12},{9,13},{10,... | collective-permute-start | bytes 1228808 | tf_op jit(solution)/shard_map/ppermute | solution.py:330
  8.5 8.6 %collective-permute-start.2 = (f32[100,1024]{1,0:T(8,128)S(1)}, f32[100,1024]{1,0:T(8,128)S(1)}, u32[]{:S(2)}, u32[]{:S(2)}) collective-permute-start(f32[100,1024]{1,0:T(8,128)S(1)} %add.45._), channel_id=1, source_target_pairs={{0,8},{1,9},{2,10},{3,11},{4,20},{5,21},{6,22},{7,23},{8,0},{9,1},... | collective-permute-start | bytes 1228808 | tf_op jit(solution)/shard_map/ppermute | solution.py:330
  14.8 2.2 %collective-permute-start.1 = (f32[100,1024]{1,0:T(8,128)S(1)}, f32[100,1024]{1,0:T(8,128)S(1)}, u32[]{:S(2)}, u32[]{:S(2)}) collective-permute-start(f32[100,1024]{1,0:T(8,128)S(1)} %get-tuple-element.10._), channel_id=1, source_target_pairs={{0,4},{1,5},{2,6},{3,7},{4,0},{5,1},{6,2},{7,3},{8,12},{9,13},{10,... | collective-permute-start | bytes 1228808 | tf_op jit(solution)/shard_map/ppermute | solution.py:330
  17.2 6.8 %collective-permute-start.3 = (f32[100,256]{1,0:T(8,128)S(1)}, f32[100,256]{1,0:T(8,128)S(1)}, u32[]{:S(2)}, u32[]{:S(2)}) collective-permute-start(f32[100,256]{1,0:T(8,128)S(1)} %get-tuple-element.14), channel_id=1, source_target_pairs={{0,17},{1,16},{2,19},{3,18},{4,14},{5,15},{6,12},{7,13},{8,25},{9,... | collective-permute-start | bytes 307208 | tf_op jit(solution)/shard_map/ppermute | solution.py:330
  20.7 3.9 %collective-permute-start.5 = (f32[100,256]{1,0:T(8,128)S(1)}, f32[100,256]{1,0:T(8,128)S(1)}, u32[]{:S(2)}, u32[]{:S(2)}) collective-permute-start(f32[100,256]{1,0:T(8,128)S(1)} %get-tuple-element.15), channel_id=1, source_target_pairs={{0,16},{1,17},{2,18},{3,19},{4,12},{5,13},{6,14},{7,15},{8,24},{9,... | collective-permute-start | bytes 307208 | tf_op jit(solution)/shard_map/ppermute | solution.py:330
  20.9 4.6 %collective-permute-start.4 = (f32[100,256]{1,0:T(8,128)S(1)}, f32[100,256]{1,0:T(8,128)S(1)}, u32[]{:S(2)}, u32[]{:S(2)}) collective-permute-start(f32[100,256]{1,0:T(8,128)S(1)} %get-tuple-element.16), channel_id=1, source_target_pairs={{0,1},{1,0},{2,3},{3,2},{4,6},{5,7},{6,4},{7,5},{8,9},{9,8},{10,11... | collective-permute-start | bytes 307208 | tf_op jit(solution)/shard_map/ppermute | solution.py:330
  25.6 3.6 %collective-permute-start.6 = (f32[100,256]{1,0:T(8,128)S(1)}, f32[100,256]{1,0:T(8,128)S(1)}, u32[]{:S(2)}, u32[]{:S(2)}) collective-permute-start(f32[100,256]{1,0:T(8,128)S(1)} %fusion.2), channel_id=1, source_target_pairs={{0,2},{1,3},{2,0},{3,1},{4,5},{5,4},{6,7},{7,6},{8,10},{9,11},{10,... | collective-permute-start | bytes 307208 | tf_op jit(solution)/shard_map/ppermute | solution.py:330
  29.2 6.2 %collective-permute-start.9 = (f32[100,128]{1,0:T(8,128)S(1)}, f32[100,128]{1,0:T(8,128)S(1)}, u32[]{:S(2)}, u32[]{:S(2)}) collective-permute-start(f32[100,128]{1,0:T(8,128)S(1)} %fusion.3), channel_id=1, source_target_pairs={{0,17},{1,16},{2,19},{3,18},{4,14},{5,15},{6,12},{7,13},{8,25},{9,... | collective-permute-start | bytes 153608 | tf_op jit(solution)/shard_map/ppermute | solution.py:330
  32.1 3.3 %collective-permute-start.8 = (f32[100,128]{1,0:T(8,128)S(1)}, f32[100,128]{1,0:T(8,128)S(1)}, u32[]{:S(2)}, u32[]{:S(2)}) collective-permute-start(f32[100,128]{1,0:T(8,128)S(1)} %fusion.3), channel_id=1, source_target_pairs={{0,16},{1,17},{2,18},{3,19},{4,12},{5,13},{6,14},{7,15},{8,24},{9,... | collective-permute-start | bytes 153608 | tf_op jit(solution)/shard_map/ppermute | solution.py:330
  33.4 3.9 %collective-permute-start.7 = (f32[100,128]{1,0:T(8,128)S(1)}, f32[100,128]{1,0:T(8,128)S(1)}, u32[]{:S(2)}, u32[]{:S(2)}) collective-permute-start(f32[100,128]{1,0:T(8,128)S(1)} %fusion.3), channel_id=1, source_target_pairs={{0,1},{1,0},{2,3},{3,2},{4,6},{5,7},{6,4},{7,5},{8,9},{9,8},{10,11... | collective-permute-start | bytes 153608 | tf_op jit(solution)/shard_map/ppermute | solution.py:330
  37.3 4.1 %collective-permute-start.11 = (f32[100,512]{1,0:T(8,128)S(1)}, f32[100,512]{1,0:T(8,128)S(1)}, u32[]{:S(2)}, u32[]{:S(2)}) collective-permute-start(f32[100,512]{1,0:T(8,128)S(1)} %pad_maximum_fusion.refs_1_.refs_3_), channel_id=1, source_target_pairs={{0,4},{1,5},{2,6},{3,7},{4,0},{5,1},{6,2},{7,3},{8,12},{9,13},{10,... | collective-permute-start | bytes 614408 | tf_op jit(solution)/shard_map/ppermute | solution.py:330
  40.3 5.0 %collective-permute-start.10 = (f32[100,512]{1,0:T(8,128)S(1)}, f32[100,512]{1,0:T(8,128)S(1)}, u32[]{:S(2)}, u32[]{:S(2)}) collective-permute-start(f32[100,512]{1,0:T(8,128)S(1)} %pad_maximum_fusion.refs_1_.refs_3_), channel_id=1, source_target_pairs={{0,8},{1,9},{2,10},{3,11},{4,20},{5,21},{6,22},{7,23},{8,0},{9,1},... | collective-permute-start | bytes 614408 | tf_op jit(solution)/shard_map/ppermute | solution.py:330
  44.1 3.9 %copy-start.1 = (f32[100,8192]{1,0:T(8,128)S(1)}, f32[100,8192]{1,0:T(8,128)}, u32[]{:S(2)}) copy-start(f32[100,8192]{1,0:T(8,128)} %refs_2_.1) | copy-start | bytes 9830404
  45.2 2.8 %collective-permute-start.12 = (f32[100,512]{1,0:T(8,128)S(1)}, f32[100,512]{1,0:T(8,128)S(1)}, u32[]{:S(2)}, u32[]{:S(2)}) collective-permute-start(f32[100,512]{1,0:T(8,128)S(1)} %collective-permute-done.10.refs_1_.refs_4_), channel_id=1, source_target_pairs={{0,4},{1,5},{2,6},{3,7},{4,0},{5,1},{6,2},{7,3},{8,12},{9,13},{10,... | collective-permute-start | bytes 614408 | tf_op jit(solution)/shard_map/ppermute | solution.py:330

commit v6 on v5

--- a/solution.py
+++ b/solution.py
@@ -37,7 +37,7 @@
             even += step
             odd += step[::-1]
         self.core = leaf
-        self.masks = [[leaf] + even + z_bits, [leaf] + odd + z_bits[::-1]]
+        self.masks = [[leaf] + even + z_bits, [leaf] + odd + z_bits]
         self.steps = len(self.masks[0])
         self.halvings = 0
         while self.halvings < self.steps and pairs >> (self.halvings + 1) << (self.halvings + 1) == pairs:
@@ -114,7 +114,7 @@
         out_ref[:, pl.ds((2 * (first + i) + 1) * PAIR, PAIR)] = block[half : half + classes]
 
 
-def add_up(plan, parts, half, width, stacked_ref, ids_ref, out_refs):
+def add_up(plan, parts, half, width, stacked_ref, ids_ref, out_refs, start=0):
     device = own_device(plan)
     rows = stacked_ref.shape[1]
     todo = []
@@ -122,7 +122,7 @@
         tree = tree_rows(plan.code(device, other), slots)
         todo += [(tree[2 * i : 2 * i + 2], out_ref, i) for i in range(len(slots))]
     for group in groups(todo, 4):
-        tree = [row for item in group for row in item[0]]
+        tree = [row - start for item in group for row in item[0]]
         total = None
         for first in range(0, rows, width):
             part = pair_sums(one_hot(ids_ref, tree, first, width), stacked_ref[:, first : first + width])
@@ -136,9 +136,10 @@
     rows = predict_ref.shape[1]
     classes = predict_ref.shape[0]
     count = rows // width
+    group = pl.multiple_of(tree_rows(plan.code(own_device(plan), True), [slots[0]])[0] & -len(slots) * 2, 8)
     copies = [
         pltpu.make_async_copy(labels_hbm, labels_ref, sems.at[0]),
-        pltpu.make_async_copy(ids_hbm, ids_ref, sems.at[1]),
+        pltpu.make_async_copy(ids_hbm.at[pl.ds(group, ids_ref.shape[0]), :], ids_ref, sems.at[1]),
     ]
     for i in range(count):
         part = pl.ds(i * width, width)
@@ -162,7 +163,7 @@
             [gradient, filler, probability * (1.0 - probability), filler], axis=0
         ).astype(jnp.bfloat16)
     copies[1].wait()
-    add_up(plan, [(slots, True)], half, width, stacked_ref, ids_ref, (other_ref,))
+    add_up(plan, [(slots, True)], half, width, stacked_ref, ids_ref, (other_ref,), group)
 
 
 def sums_kernel(plan, parts, half, width, stacked_ref, ids_ref, _, *out_refs):
@@ -189,7 +190,7 @@
         scratch_shapes=[
             pltpu.VMEM((classes, rows), jnp.float32),
             pltpu.VMEM((1, rows), jnp.int32),
-            pltpu.VMEM(leaf_ids.shape, jnp.int32),
+            pltpu.VMEM((2 * len(slots), rows), jnp.int32),
             pltpu.SemaphoreType.DMA((2 + rows // width,)),
         ],
         compiler_params=pltpu.CompilerParams(vmem_limit_bytes=VMEM_LIMIT),
@@ -201,7 +202,7 @@
 def more_sums(plan, stacked, leaf_ids, classes, parts, earlier):
     height, rows = stacked.shape
     return pl.pallas_call(
-        functools.partial(sums_kernel, plan, parts, height // 2, chunk(rows, 1024)),
+        functools.partial(sums_kernel, plan, parts, height // 2, chunk(rows, 2048)),
         in_specs=[IN_VMEM, IN_VMEM, pl.BlockSpec(memory_space=pl.ANY)],
         out_specs=[IN_VMEM] * len(parts),
         out_shape=[jax.ShapeDtypeStruct((classes, 2 * PAIR * len(slots)), jnp.float32) for slots, _ in parts],
@@ -228,13 +229,11 @@
     return total
 
 
-def apply_kernel(plan, parts, width, carried, *refs):
-    ids_ref, refs = refs[0], refs[1:]
-    value_refs, out_ref = refs[: len(parts)], refs[-1]
+def apply_kernel(plan, parts, width, ids_ref, carried_ref, *refs):
+    value_refs, out_ref = refs[:-1], refs[-1]
     for first in range(0, out_ref.shape[1], width):
         part = pl.ds(first, width)
-        total = looked_up(plan, parts, value_refs, ids_ref, first, width)
-        out_ref[:, part] = refs[len(parts)][:, part] + total if carried else total
+        out_ref[:, part] = carried_ref[:, part] + looked_up(plan, parts, value_refs, ids_ref, first, width)
 
 
 def apply_cost(count, classes, rows):
@@ -243,26 +242,23 @@
     )
 
 
-def apply_values(plan, leaf_ids, parts, values, update):
-    classes, rows = values[0].shape[0], leaf_ids.shape[1]
-    carried = update is not None
-    operands = (leaf_ids, *values) + ((update,) if carried else ())
+def apply_values(plan, leaf_ids, parts, values, carried):
+    classes, rows = carried.shape
     return pl.pallas_call(
-        functools.partial(apply_kernel, plan, parts, chunk(rows, 2048), carried),
-        in_specs=[IN_VMEM] * len(operands),
+        functools.partial(apply_kernel, plan, parts, chunk(rows, 2048)),
+        in_specs=[IN_VMEM] * (2 + len(values)),
         out_specs=IN_VMEM,
         out_shape=jax.ShapeDtypeStruct((classes, rows), jnp.float32),
-        input_output_aliases={len(operands) - 1: 0} if carried else {},
         compiler_params=pltpu.CompilerParams(vmem_limit_bytes=VMEM_LIMIT),
         cost_estimate=apply_cost(sum(len(slots) for slots, _ in parts), classes, rows),
         name="apply_values",
-    )(*operands)
+    )(leaf_ids, carried, *values)
 
 
 def last_kernel(plan, parts, pieces, width, *refs):
-    ids_ref, update_ref, predict_ref = refs[:3]
-    value_refs = refs[3 : 3 + len(pieces)]
-    out_hbm, own_hbm, out_ref, own_ref, table_ref, sems = refs[3 + len(pieces) :]
+    ids_ref, carried_ref = refs[:2]
+    value_refs = refs[2 : 2 + len(pieces)]
+    out_hbm, own_hbm, out_ref, own_ref, table_ref, sems = refs[2 + len(pieces) :]
     rows = ids_ref.shape[1]
     count = rows // width
     device = own_device(plan)
@@ -277,26 +273,27 @@
         place = pair ^ mine
         place = jnp.where(place < half, place, (pair ^ theirs) + half)
         own_ref[:, pl.ds(i * PAIR, PAIR)] = table_ref[:, pl.ds(pl.multiple_of(place * PAIR, PAIR), PAIR)]
-    writes = [pltpu.make_async_copy(own_ref, own_hbm, sems.at[count])]
-    writes[0].start()
+    writes = []
     last = [value_refs[pieces.index(piece)] for piece in parts]
     for i in range(count):
         part = pl.ds(i * width, width)
-        total = looked_up(plan, parts, last, ids_ref, i * width, width) + update_ref[:, part]
-        out_ref[:, part] = predict_ref[:, part] + total
+        out_ref[:, part] = carried_ref[:, part] + looked_up(plan, parts, last, ids_ref, i * width, width)
         writes.append(pltpu.make_async_copy(out_ref.at[:, part], out_hbm.at[:, part], sems.at[i]))
         writes[-1].start()
+        if i == 0:
+            writes.append(pltpu.make_async_copy(own_ref, own_hbm, sems.at[count]))
+            writes[-1].start()
     for write in writes:
         write.wait()
 
 
-def finish(plan, leaf_ids, update, predict, parts, pieces, values):
-    classes, rows = predict.shape
-    width = chunk(rows, 2048)
+def finish(plan, leaf_ids, carried, parts, pieces, values):
+    classes, rows = carried.shape
+    width = chunk(rows, 1024)
     own = (classes, plan.pairs // plan.leaf * PAIR)
     return pl.pallas_call(
         functools.partial(last_kernel, plan, parts, pieces, width),
-        in_specs=[IN_VMEM] * (3 + len(values)),
+        in_specs=[IN_VMEM] * (2 + len(values)),
         out_specs=[IN_HBM, IN_HBM],
         out_shape=[jax.ShapeDtypeStruct((classes, rows), jnp.float32), jax.ShapeDtypeStruct(own, jnp.float32)],
         scratch_shapes=[
@@ -308,7 +305,7 @@
         compiler_params=pltpu.CompilerParams(vmem_limit_bytes=VMEM_LIMIT),
         cost_estimate=apply_cost(sum(len(slots) for slots, _ in parts), classes, rows),
         name="apply_last_values",
-    )(leaf_ids, update, predict, *values)
+    )(leaf_ids, carried, *values)
 
 
 def newton(sums):
@@ -367,14 +364,14 @@
         far_values = exchange(near_values, 1)
         near_theirs = exchange(near_values, 0)
         update = apply_values(
-            plan, leaf_ids, [(near, False), (near, True)], [near_values, near_theirs], None
+            plan, leaf_ids, [(near, False), (near, True)], [near_values, near_theirs], predict
         )
         far_values, update = lax.optimization_barrier((far_values, update))
         far_theirs = exchange(far_values, 0)
         update = apply_values(plan, leaf_ids, [(far, False)], [far_values], update)
         pieces = [(near, False), (far, False), (near, True), (far, True)]
         values = [near_values, far_values, near_theirs, far_theirs]
-        return tuple(finish(plan, leaf_ids, update, predict, [(far, True)], pieces, values))
+        return tuple(finish(plan, leaf_ids, update, [(far, True)], pieces, values))
 
     return jax.shard_map(
         shards,

time: 50.9 us -> 49.9 us (0.980)
  Pallas kernels: 19.7 us -> 19.1 us
    ppermute x13, starting transfers between devices: 18 us -> 17.5 us  [exchange(): return lax.ppermute(value, AXES, plan.permutation(*steps))]
where the time goes in v6:
time: 49.9 us; the launch traced here: 49.8 us
  Pallas kernels  19.1 us (38%)
  starting transfers between devices  17.5 us (35%)
  waiting for transfers between devices  12 us (24%)
  between operations  0.9 us (2%)
    ppermute x13, starting transfers between devices, exchange(): return lax.ppermute(value, AXES, plan.permutation(*steps))  17.5 us
    ppermute x13, waiting for transfers between devices, exchange(): return lax.ppermute(value, AXES, plan.permutation(*steps))  12 us
    pallas_call x3, Pallas kernels, more_sums(): pl.pallas_call(functools.partial(sums_kernel, plan, parts, height // 2, c...  7.31 us
    pallas_call x1, Pallas kernels, first_sums(): pl.pallas_call(functools.partial(first_kernel, plan, slots, half, width),...  5.24 us
    pallas_call x2, Pallas kernels, apply_values(): pl.pallas_call(functools.partial(apply_kernel, plan, parts, chunk(rows, 2...  4.18 us
    pallas_call x1, Pallas kernels, finish(): pl.pallas_call(functools.partial(last_kernel, plan, parts, pieces, width)...  2.36 us
  transfers between devices with their start and end apart: 13, of which 8 were waited for; matrix products, arithmetic and copies ran while one was open for 0% of the time, Pallas kernels for 23%

profile of v6, /device:TPU:1, one launch (start us, length us, event | category | flops | bytes accessed | tf_op | source)
XLA Modules:
  0.0 49.8 jit_solution(8625878364755908650)
XLA Ops:
  0.6 0.0 copy-start
  0.6 5.2 %gradients_and_sums.1 = (bf16[224,8192]{1,0:T(8,128)(2,1)S(1)}, f32[100,1024]{1,0:T(8,128)S(1)}) custom-call(f32[100,8192]{1,0:T(8,128)} %carried_ref.1, s32[1,8192]{1,0:T(1,128)} %bitcast.1, s32[32,8192]{1,0:T(8,128)} %refs_0_.1), custom_call_target="tpu_custom_call" | custom-call | flops 1879048192 | bytes 3670016 | tf_op jit(solution)/shard_map/gradients_and_sums/pallas_call | solution.py:182
  5.9 0.1 collective-permute-start
  6.0 0.0 copy-done
  6.0 2.4 %leaf_sums.3 = f32[100,1024]{1,0:T(8,128)S(1)} custom-call(bf16[224,8192]{1,0:T(8,128)(2,1)S(1)} %get-tuple-element.8.stacked_ref, s32[32,8192]{1,0:T(8,128)S(1)} %copy-done, f32[100,1024]{1,0:T(8,128)S(1)} %get-tuple-element.9._), custom_call_target="tpu_custom_call" | custom-call | flops 1879048192 | bytes 3670016 | tf_op jit(solution)/shard_map/leaf_sums/pallas_call | solution.py:204
  8.4 0.0 collective-permute-done
  8.5 2.8 %collective-permute-start.2 = (f32[100,1024]{1,0:T(8,128)S(1)}, f32[100,1024]{1,0:T(8,128)S(1)}, u32[]{:S(2)}, u32[]{:S(2)}) collective-permute-start(f32[100,1024]{1,0:T(8,128)S(1)} %add.45._), channel_id=1, source_target_pairs={{0,8},{1,9},{2,10},{3,11},{4,20},{5,21},{6,22},{7,23},{8,0},{9,1},... | collective-permute-start | bytes 1228808 | tf_op jit(solution)/shard_map/ppermute | solution.py:327
  11.3 3.6 %leaf_sums.4 = (f32[100,1024]{1,0:T(8,128)S(1)}, f32[100,512]{1,0:T(8,128)S(1)}) custom-call(bf16[224,8192]{1,0:T(8,128)(2,1)S(1)} %get-tuple-element.8.stacked_ref, s32[32,8192]{1,0:T(8,128)S(1)} %copy-done, f32[100,1024]{1,0:T(8,128)S(1)} %add.45._), custom_call_target="tpu_custom_call" | custom-call | flops 2818572288 | bytes 3670016 | tf_op jit(solution)/shard_map/leaf_sums/pallas_call | solution.py:204
  14.8 0.0 copy-start.1
  14.8 0.3 collective-permute-start.1
  15.2 1.3 %leaf_sums.5 = f32[100,512]{1,0:T(8,128)S(1)} custom-call(bf16[224,8192]{1,0:T(8,128)(2,1)S(1)} %get-tuple-element.8.stacked_ref, s32[32,8192]{1,0:T(8,128)S(1)} %copy-done, f32[100,1024]{1,0:T(8,128)S(1)} %get-tuple-element.10._), custom_call_target="tpu_custom_call" | custom-call | flops 939524096 | bytes 3670016 | tf_op jit(solution)/shard_map/leaf_sums/pallas_call | solution.py:204
  16.5 0.6 %collective-permute-done.2 = f32[100,1024]{1,0:T(8,128)S(1)} collective-permute-done((f32[100,1024]{1,0:T(8,128)S(1)}, f32[100,1024]{1,0:T(8,128)S(1)}, u32[]{:S(2)}, u32[]{:S(2)}) %collective-permute-start.2) | collective-permute-done | bytes 409632 | tf_op jit(solution)/shard_map/ppermute | solution.py:327
  17.1 0.0 collective-permute-done.1
  17.1 0.1 slice_add_fusion.4
  17.1 2.5 %collective-permute-start.3 = (f32[100,256]{1,0:T(8,128)S(1)}, f32[100,256]{1,0:T(8,128)S(1)}, u32[]{:S(2)}, u32[]{:S(2)}) collective-permute-start(f32[100,256]{1,0:T(8,128)S(1)} %get-tuple-element.14), channel_id=1, source_target_pairs={{0,17},{1,16},{2,19},{3,18},{4,13},{5,12},{6,15},{7,14},{8,25},{9,... | collective-permute-start | bytes 307208 | tf_op jit(solution)/shard_map/ppermute | solution.py:327
  19.7 0.3 collective-permute-start.5
  19.9 0.1 collective-permute-start.4
  20.0 2.0 %collective-permute-done.3 = f32[100,256]{1,0:T(8,128)S(1)} collective-permute-done((f32[100,256]{1,0:T(8,128)S(1)}, f32[100,256]{1,0:T(8,128)S(1)}, u32[]{:S(2)}, u32[]{:S(2)}) %collective-permute-start.3) | collective-permute-done | bytes 102432 | tf_op jit(solution)/shard_map/ppermute | solution.py:327
  22.0 1.5 %collective-permute-done.5 = f32[100,256]{1,0:T(8,128)S(1)} collective-permute-done((f32[100,256]{1,0:T(8,128)S(1)}, f32[100,256]{1,0:T(8,128)S(1)}, u32[]{:S(2)}, u32[]{:S(2)}) %collective-permute-start.5) | collective-permute-done | bytes 102432 | tf_op jit(solution)/shard_map/ppermute | solution.py:327
  23.5 1.4 %collective-permute-done.4 = f32[100,256]{1,0:T(8,128)S(1)} collective-permute-done((f32[100,256]{1,0:T(8,128)S(1)}, f32[100,256]{1,0:T(8,128)S(1)}, u32[]{:S(2)}, u32[]{:S(2)}) %collective-permute-start.4) | collective-permute-done | bytes 102432 | tf_op jit(solution)/shard_map/ppermute | solution.py:327
  24.9 0.1 fusion.2
  25.0 2.4 %collective-permute-start.6 = (f32[100,256]{1,0:T(8,128)S(1)}, f32[100,256]{1,0:T(8,128)S(1)}, u32[]{:S(2)}, u32[]{:S(2)}) collective-permute-start(f32[100,256]{1,0:T(8,128)S(1)} %fusion.2), channel_id=1, source_target_pairs={{0,2},{1,3},{2,0},{3,1},{4,6},{5,7},{6,4},{7,5},{8,10},{9,11},{10,... | collective-permute-start | bytes 307208 | tf_op jit(solution)/shard_map/ppermute | solution.py:327
  27.3 4.0 %collective-permute-done.6 = f32[100,256]{1,0:T(8,128)S(1)} collective-permute-done((f32[100,256]{1,0:T(8,128)S(1)}, f32[100,256]{1,0:T(8,128)S(1)}, u32[]{:S(2)}, u32[]{:S(2)}) %collective-permute-start.6) | collective-permute-done | bytes 102432 | tf_op jit(solution)/shard_map/ppermute | solution.py:327
  31.4 0.1 collective-permute-start.9
  31.4 0.7 %collective-permute-start.8 = (f32[100,128]{1,0:T(8,128)S(1)}, f32[100,128]{1,0:T(8,128)S(1)}, u32[]{:S(2)}, u32[]{:S(2)}) collective-permute-start(f32[100,128]{1,0:T(8,128)S(1)} %fusion.3), channel_id=1, source_target_pairs={{0,16},{1,17},{2,18},{3,19},{4,12},{5,13},{6,14},{7,15},{8,24},{9,... | collective-permute-start | bytes 153608 | tf_op jit(solution)/shard_map/ppermute | solution.py:327
  32.1 2.0 %collective-permute-start.7 = (f32[100,128]{1,0:T(8,128)S(1)}, f32[100,128]{1,0:T(8,128)S(1)}, u32[]{:S(2)}, u32[]{:S(2)}) collective-permute-start(f32[100,128]{1,0:T(8,128)S(1)} %fusion.3), channel_id=1, source_target_pairs={{0,1},{1,0},{2,3},{3,2},{4,5},{5,4},{6,7},{7,6},{8,9},{9,8},{10,11... | collective-permute-start | bytes 153608 | tf_op jit(solution)/shard_map/ppermute | solution.py:327
  34.1 1.2 %collective-permute-done.9 = f32[100,128]{1,0:T(8,128)S(1)} collective-permute-done((f32[100,128]{1,0:T(8,128)S(1)}, f32[100,128]{1,0:T(8,128)S(1)}, u32[]{:S(2)}, u32[]{:S(2)}) %collective-permute-start.9) | collective-permute-done | bytes 51232 | tf_op jit(solution)/shard_map/ppermute | solution.py:327
  35.3 0.0 collective-permute-done.8
  35.3 0.3 collective-permute-done.7
  35.6 4.3 %collective-permute-start.11 = (f32[100,512]{1,0:T(8,128)S(1)}, f32[100,512]{1,0:T(8,128)S(1)}, u32[]{:S(2)}, u32[]{:S(2)}) collective-permute-start(f32[100,512]{1,0:T(8,128)S(1)} %pad_maximum_fusion.refs_0_.refs_2_), channel_id=1, source_target_pairs={{0,4},{1,5},{2,6},{3,7},{4,0},{5,1},{6,2},{7,3},{8,12},{9,13},{10,... | collective-permute-start | bytes 614408 | tf_op jit(solution)/shard_map/ppermute | solution.py:327
  39.9 1.1 %collective-permute-start.10 = (f32[100,512]{1,0:T(8,128)S(1)}, f32[100,512]{1,0:T(8,128)S(1)}, u32[]{:S(2)}, u32[]{:S(2)}) collective-permute-start(f32[100,512]{1,0:T(8,128)S(1)} %pad_maximum_fusion.refs_0_.refs_2_), channel_id=1, source_target_pairs={{0,8},{1,9},{2,10},{3,11},{4,20},{5,21},{6,22},{7,23},{8,0},{9,1},... | collective-permute-start | bytes 614408 | tf_op jit(solution)/shard_map/ppermute | solution.py:327
  41.0 0.0 collective-permute-done.11.refs_1_.refs_4_
  41.0 0.0 copy-done.1
  41.0 2.8 %apply_values.2.carried_ref = f32[100,8192]{1,0:T(8,128)S(1)} custom-call(s32[32,8192]{1,0:T(8,128)S(1)} %copy-done, f32[100,8192]{1,0:T(8,128)S(1)} %copy-done.1, f32[100,512]{1,0:T(8,128)S(1)} %pad_maximum_fusion.refs_0_.refs_2_, f32[100,512]{1,0:T(8,128)S(1)} %collective-permute-done.11.refs_1_.refs_4_), custom_call_target="tpu_custom_call" | custom-call | flops 3355443200 | bytes 3276800 | tf_op jit(solution)/shard_map/apply_values/pallas_call | solution.py:247
  43.8 1.1 %collective-permute-done.10.refs_0_.refs_3_ = f32[100,512]{1,0:T(8,128)S(1)} collective-permute-done((f32[100,512]{1,0:T(8,128)S(1)}, f32[100,512]{1,0:T(8,128)S(1)}, u32[]{:S(2)}, u32[]{:S(2)}) %collective-permute-start.10) | collective-permute-done | bytes 204832 | tf_op jit(solution)/shard_map/ppermute | solution.py:327
  44.9 0.9 %collective-permute-start.12 = (f32[100,512]{1,0:T(8,128)S(1)}, f32[100,512]{1,0:T(8,128)S(1)}, u32[]{:S(2)}, u32[]{:S(2)}) collective-permute-start(f32[100,512]{1,0:T(8,128)S(1)} %collective-permute-done.10.refs_0_.refs_3_), channel_id=1, source_target_pairs={{0,4},{1,5},{2,6},{3,7},{4,0},{5,1},{6,2},{7,3},{8,12},{9,13},{10,... | collective-permute-start | bytes 614408 | tf_op jit(solution)/shard_map/ppermute | solution.py:327
  45.8 1.4 %apply_values.3.refs_1_ = f32[100,8192]{1,0:T(8,128)S(1)} custom-call(s32[32,8192]{1,0:T(8,128)S(1)} %copy-done, f32[100,8192]{1,0:T(8,128)S(1)} %apply_values.2.carried_ref, f32[100,512]{1,0:T(8,128)S(1)} %collective-permute-done.10.refs_0_.refs_3_), custom_call_target="tpu_custom_call" | custom-call | flops 1677721600 | bytes 3276800 | tf_op jit(solution)/shard_map/apply_values/pallas_call | solution.py:247
  47.2 0.0 collective-permute-done.12.refs_5_
  47.2 2.4 %apply_last_values.1 = (f32[100,8192]{1,0:T(8,128)}, f32[100,512]{1,0:T(8,128)}) custom-call(s32[32,8192]{1,0:T(8,128)S(1)} %copy-done, f32[100,8192]{1,0:T(8,128)S(1)} %apply_values.3.refs_1_, f32[100,512]{1,0:T(8,128)S(1)} %pad_maximum_fusion.refs_0_.refs_2_, f32[100,512]{1,0:T(8,128)S(1)} %collective-permute-done.10.refs_0_.refs_3_, ...), custom_call_target="tpu_custom_call" | custom-call | flops 1677721600 | bytes 3276800 | tf_op jit(solution)/shard_map/apply_last_values/pallas_call | solution.py:294
  (4 shorter events, 0.1 us)
Async XLA Ops:
  0.6 5.4 %copy-start = (s32[32,8192]{1,0:T(8,128)S(1)}, s32[32,8192]{1,0:T(8,128)}, u32[]{:S(2)}) copy-start(s32[32,8192]{1,0:T(8,128)} %refs_0_.1) | copy-start | bytes 3145732
  5.9 2.5 %collective-permute-start = (f32[100,1024]{1,0:T(8,128)S(1)}, f32[100,1024]{1,0:T(8,128)S(1)}, u32[]{:S(2)}, u32[]{:S(2)}) collective-permute-start(f32[100,1024]{1,0:T(8,128)S(1)} %get-tuple-element.9._), channel_id=1, source_target_pairs={{0,4},{1,5},{2,6},{3,7},{4,0},{5,1},{6,2},{7,3},{8,12},{9,13},{10,... | collective-permute-start | bytes 1228808 | tf_op jit(solution)/shard_map/ppermute | solution.py:327
  8.5 8.6 %collective-permute-start.2 = (f32[100,1024]{1,0:T(8,128)S(1)}, f32[100,1024]{1,0:T(8,128)S(1)}, u32[]{:S(2)}, u32[]{:S(2)}) collective-permute-start(f32[100,1024]{1,0:T(8,128)S(1)} %add.45._), channel_id=1, source_target_pairs={{0,8},{1,9},{2,10},{3,11},{4,20},{5,21},{6,22},{7,23},{8,0},{9,1},... | collective-permute-start | bytes 1228808 | tf_op jit(solution)/shard_map/ppermute | solution.py:327
  14.8 26.2 %copy-start.1 = (f32[100,8192]{1,0:T(8,128)S(1)}, f32[100,8192]{1,0:T(8,128)}, u32[]{:S(2)}) copy-start(f32[100,8192]{1,0:T(8,128)} %carried_ref.1) | copy-start | bytes 9830404
  14.8 2.2 %collective-permute-start.1 = (f32[100,1024]{1,0:T(8,128)S(1)}, f32[100,1024]{1,0:T(8,128)S(1)}, u32[]{:S(2)}, u32[]{:S(2)}) collective-permute-start(f32[100,1024]{1,0:T(8,128)S(1)} %get-tuple-element.10._), channel_id=1, source_target_pairs={{0,4},{1,5},{2,6},{3,7},{4,0},{5,1},{6,2},{7,3},{8,12},{9,13},{10,... | collective-permute-start | bytes 1228808 | tf_op jit(solution)/shard_map/ppermute | solution.py:327
  17.1 4.9 %collective-permute-start.3 = (f32[100,256]{1,0:T(8,128)S(1)}, f32[100,256]{1,0:T(8,128)S(1)}, u32[]{:S(2)}, u32[]{:S(2)}) collective-permute-start(f32[100,256]{1,0:T(8,128)S(1)} %get-tuple-element.14), channel_id=1, source_target_pairs={{0,17},{1,16},{2,19},{3,18},{4,13},{5,12},{6,15},{7,14},{8,25},{9,... | collective-permute-start | bytes 307208 | tf_op jit(solution)/shard_map/ppermute | solution.py:327
  19.7 3.9 %collective-permute-start.5 = (f32[100,256]{1,0:T(8,128)S(1)}, f32[100,256]{1,0:T(8,128)S(1)}, u32[]{:S(2)}, u32[]{:S(2)}) collective-permute-start(f32[100,256]{1,0:T(8,128)S(1)} %get-tuple-element.15), channel_id=1, source_target_pairs={{0,16},{1,17},{2,18},{3,19},{4,12},{5,13},{6,14},{7,15},{8,24},{9,... | collective-permute-start | bytes 307208 | tf_op jit(solution)/shard_map/ppermute | solution.py:327
  19.9 5.0 %collective-permute-start.4 = (f32[100,256]{1,0:T(8,128)S(1)}, f32[100,256]{1,0:T(8,128)S(1)}, u32[]{:S(2)}, u32[]{:S(2)}) collective-permute-start(f32[100,256]{1,0:T(8,128)S(1)} %get-tuple-element.16), channel_id=1, source_target_pairs={{0,1},{1,0},{2,3},{3,2},{4,5},{5,4},{6,7},{7,6},{8,9},{9,8},{10,11... | collective-permute-start | bytes 307208 | tf_op jit(solution)/shard_map/ppermute | solution.py:327
  25.0 6.4 %collective-permute-start.6 = (f32[100,256]{1,0:T(8,128)S(1)}, f32[100,256]{1,0:T(8,128)S(1)}, u32[]{:S(2)}, u32[]{:S(2)}) collective-permute-start(f32[100,256]{1,0:T(8,128)S(1)} %fusion.2), channel_id=1, source_target_pairs={{0,2},{1,3},{2,0},{3,1},{4,6},{5,7},{6,4},{7,5},{8,10},{9,11},{10,... | collective-permute-start | bytes 307208 | tf_op jit(solution)/shard_map/ppermute | solution.py:327
  31.4 3.9 %collective-permute-start.9 = (f32[100,128]{1,0:T(8,128)S(1)}, f32[100,128]{1,0:T(8,128)S(1)}, u32[]{:S(2)}, u32[]{:S(2)}) collective-permute-start(f32[100,128]{1,0:T(8,128)S(1)} %fusion.3), channel_id=1, source_target_pairs={{0,17},{1,16},{2,19},{3,18},{4,13},{5,12},{6,15},{7,14},{8,25},{9,... | collective-permute-start | bytes 153608 | tf_op jit(solution)/shard_map/ppermute | solution.py:327
  31.4 3.9 %collective-permute-start.8 = (f32[100,128]{1,0:T(8,128)S(1)}, f32[100,128]{1,0:T(8,128)S(1)}, u32[]{:S(2)}, u32[]{:S(2)}) collective-permute-start(f32[100,128]{1,0:T(8,128)S(1)} %fusion.3), channel_id=1, source_target_pairs={{0,16},{1,17},{2,18},{3,19},{4,12},{5,13},{6,14},{7,15},{8,24},{9,... | collective-permute-start | bytes 153608 | tf_op jit(solution)/shard_map/ppermute | solution.py:327
  32.1 3.5 %collective-permute-start.7 = (f32[100,128]{1,0:T(8,128)S(1)}, f32[100,128]{1,0:T(8,128)S(1)}, u32[]{:S(2)}, u32[]{:S(2)}) collective-permute-start(f32[100,128]{1,0:T(8,128)S(1)} %fusion.3), channel_id=1, source_target_pairs={{0,1},{1,0},{2,3},{3,2},{4,5},{5,4},{6,7},{7,6},{8,9},{9,8},{10,11... | collective-permute-start | bytes 153608 | tf_op jit(solution)/shard_map/ppermute | solution.py:327
  35.6 5.4 %collective-permute-start.11 = (f32[100,512]{1,0:T(8,128)S(1)}, f32[100,512]{1,0:T(8,128)S(1)}, u32[]{:S(2)}, u32[]{:S(2)}) collective-permute-start(f32[100,512]{1,0:T(8,128)S(1)} %pad_maximum_fusion.refs_0_.refs_2_), channel_id=1, source_target_pairs={{0,4},{1,5},{2,6},{3,7},{4,0},{5,1},{6,2},{7,3},{8,12},{9,13},{10,... | collective-permute-start | bytes 614408 | tf_op jit(solution)/shard_map/ppermute | solution.py:327
  39.9 5.0 %collective-permute-start.10 = (f32[100,512]{1,0:T(8,128)S(1)}, f32[100,512]{1,0:T(8,128)S(1)}, u32[]{:S(2)}, u32[]{:S(2)}) collective-permute-start(f32[100,512]{1,0:T(8,128)S(1)} %pad_maximum_fusion.refs_0_.refs_2_), channel_id=1, source_target_pairs={{0,8},{1,9},{2,10},{3,11},{4,20},{5,21},{6,22},{7,23},{8,0},{9,1},... | collective-permute-start | bytes 614408 | tf_op jit(solution)/shard_map/ppermute | solution.py:327
  44.9 2.3 %collective-permute-start.12 = (f32[100,512]{1,0:T(8,128)S(1)}, f32[100,512]{1,0:T(8,128)S(1)}, u32[]{:S(2)}, u32[]{:S(2)}) collective-permute-start(f32[100,512]{1,0:T(8,128)S(1)} %collective-permute-done.10.refs_0_.refs_3_), channel_id=1, source_target_pairs={{0,4},{1,5},{2,6},{3,7},{4,0},{5,1},{6,2},{7,3},{8,12},{9,13},{10,... | collective-permute-start | bytes 614408 | tf_op jit(solution)/shard_map/ppermute | solution.py:327

commit v7 on v6

--- a/solution.py
+++ b/solution.py
@@ -105,16 +105,12 @@
     return lax.dot_general(hot, stacked, (((1,), (1,)), ((), ())), preferred_element_type=jnp.float32)
 
 
-def write_sums(sums, half, out_ref, first):
-    classes = out_ref.shape[0]
-    turned = sums.T
-    for i in range(turned.shape[1] // PAIR):
-        block = turned[:, i * PAIR : (i + 1) * PAIR]
-        out_ref[:, pl.ds(2 * (first + i) * PAIR, PAIR)] = block[:classes]
-        out_ref[:, pl.ds((2 * (first + i) + 1) * PAIR, PAIR)] = block[half : half + classes]
-
-
-def add_up(plan, parts, half, width, stacked_ref, ids_ref, out_refs, start=0):
+def write_sums(sums, out_ref, first):
+    turned = sums.T[: out_ref.shape[0]]
+    out_ref[:, pl.ds(first * PAIR, turned.shape[1])] = turned
+
+
+def add_up(plan, parts, width, stacked_ref, ids_ref, out_refs, start=0):
     device = own_device(plan)
     rows = stacked_ref.shape[1]
     todo = []
@@ -128,10 +124,10 @@
             part = pair_sums(one_hot(ids_ref, tree, first, width), stacked_ref[:, first : first + width])
             total = part if total is None else total + part
         for i, (_, out_ref, place) in enumerate(group):
-            write_sums(total[i * PAIR : (i + 1) * PAIR], half, out_ref, place)
-
-
-def first_kernel(plan, slots, half, width, predict_hbm, labels_hbm, ids_hbm, stacked_ref, other_ref,
+            write_sums(total[i * PAIR : (i + 1) * PAIR], out_ref, place)
+
+
+def first_kernel(plan, slots, width, predict_hbm, labels_hbm, ids_hbm, stacked_ref, other_ref,
                  predict_ref, labels_ref, ids_ref, sems):
     rows = predict_ref.shape[1]
     classes = predict_ref.shape[0]
@@ -158,34 +154,35 @@
         probability = exponent * (1.0 / jnp.sum(exponent, axis=0, keepdims=True))
         index = lax.broadcasted_iota(jnp.int32, predict.shape, 0)
         gradient = jnp.where(index == labels_ref[:, i * width : (i + 1) * width], probability - 1.0, probability)
-        filler = jnp.zeros((half - classes, width), jnp.float32)
+        filler = jnp.zeros((stacked_ref.shape[0] - 2 * classes, width), jnp.float32)
         stacked_ref[:, i * width : (i + 1) * width] = jnp.concatenate(
-            [gradient, filler, probability * (1.0 - probability), filler], axis=0
+            [gradient, probability * (1.0 - probability), filler], axis=0
         ).astype(jnp.bfloat16)
     copies[1].wait()
-    add_up(plan, [(slots, True)], half, width, stacked_ref, ids_ref, (other_ref,), group)
-
-
-def sums_kernel(plan, parts, half, width, stacked_ref, ids_ref, _, *out_refs):
-    add_up(plan, parts, half, width, stacked_ref, ids_ref, out_refs)
-
-
-def sums_cost(count, half, rows):
+    add_up(plan, [(slots, True)], width, stacked_ref, ids_ref, (other_ref,), group)
+
+
+def sums_kernel(plan, parts, width, stacked_ref, ids_ref, _, *out_refs):
+    add_up(plan, parts, width, stacked_ref, ids_ref, out_refs)
+
+
+def sums_cost(count, height, rows):
     return pl.CostEstimate(
-        flops=2 * count * PAIR * rows * 2 * half, bytes_accessed=2 * half * rows * 2, transcendentals=0
+        flops=2 * count * PAIR * rows * height, bytes_accessed=2 * height * rows, transcendentals=0
     )
 
 
-def first_sums(plan, predict, labels, leaf_ids, slots, half):
+def first_sums(plan, predict, labels, leaf_ids, slots):
     classes, rows = predict.shape
+    height = round_up(2 * classes, 16)
     width = chunk(rows, 1024)
     return pl.pallas_call(
-        functools.partial(first_kernel, plan, slots, half, width),
+        functools.partial(first_kernel, plan, slots, width),
         in_specs=[IN_HBM, IN_HBM, IN_HBM],
         out_specs=[IN_VMEM, IN_VMEM],
         out_shape=[
-            pltpu.VMEM((2 * half, rows), jnp.bfloat16),
-            pltpu.VMEM((classes, 2 * PAIR * len(slots)), jnp.float32),
+            pltpu.VMEM((height, rows), jnp.bfloat16),
+            pltpu.VMEM((2 * classes, PAIR * len(slots)), jnp.float32),
         ],
         scratch_shapes=[
             pltpu.VMEM((classes, rows), jnp.float32),
@@ -194,7 +191,7 @@
             pltpu.SemaphoreType.DMA((2 + rows // width,)),
         ],
         compiler_params=pltpu.CompilerParams(vmem_limit_bytes=VMEM_LIMIT),
-        cost_estimate=sums_cost(len(slots), half, rows),
+        cost_estimate=sums_cost(len(slots), height, rows),
         name="gradients_and_sums",
     )(*(pltpu.with_memory_space_constraint(x, pltpu.HBM) for x in (predict, labels.reshape(1, rows), leaf_ids)))
 
@@ -202,12 +199,12 @@
 def more_sums(plan, stacked, leaf_ids, classes, parts, earlier):
     height, rows = stacked.shape
     return pl.pallas_call(
-        functools.partial(sums_kernel, plan, parts, height // 2, chunk(rows, 2048)),
+        functools.partial(sums_kernel, plan, parts, chunk(rows, 2048)),
         in_specs=[IN_VMEM, IN_VMEM, pl.BlockSpec(memory_space=pl.ANY)],
         out_specs=[IN_VMEM] * len(parts),
-        out_shape=[jax.ShapeDtypeStruct((classes, 2 * PAIR * len(slots)), jnp.float32) for slots, _ in parts],
+        out_shape=[jax.ShapeDtypeStruct((2 * classes, PAIR * len(slots)), jnp.float32) for slots, _ in parts],
         compiler_params=pltpu.CompilerParams(vmem_limit_bytes=VMEM_LIMIT),
-        cost_estimate=sums_cost(sum(len(slots) for slots, _ in parts), height // 2, rows),
+        cost_estimate=sums_cost(sum(len(slots) for slots, _ in parts), height, rows),
         name="leaf_sums",
     )(stacked, leaf_ids, earlier)
 
@@ -309,19 +306,14 @@
 
 
 def newton(sums):
-    values = []
-    for i in range(sums.shape[1] // (2 * PAIR)):
-        gradient = sums[:, 2 * i * PAIR : (2 * i + 1) * PAIR]
-        hessian = sums[:, (2 * i + 1) * PAIR : (2 * i + 2) * PAIR]
-        values.append(-STEP_SIZE * gradient / (hessian + RIDGE_TERM))
-    return values[0] if len(values) == 1 else jnp.concatenate(values, axis=1)
+    classes = sums.shape[0] // 2
+    return -STEP_SIZE * sums[:classes] / (sums[classes:] + RIDGE_TERM)
 
 
 def solution(mesh):
     def shards(predict, labels, leaf_ids):
         classes = predict.shape[0]
         plan = Plan(mesh, leaf_ids.shape[0] // 2)
-        half = round_up(classes, 16)
 
         def exchange(value, *steps):
             return lax.ppermute(value, AXES, plan.permutation(*steps))
@@ -332,7 +324,7 @@
         near = list(range(h // 2))
         own, by_3, by_2, by_both = (near[i * unit : (i + 1) * unit] for i in range(4))
 
-        stacked, far_other = first_sums(plan, predict, labels, leaf_ids, far, half)
+        stacked, far_other = first_sums(plan, predict, labels, leaf_ids, far)
         (far_own,) = more_sums(plan, stacked, leaf_ids, classes, [(far, False)], far_other)
         far_sums = far_own + exchange(far_other, 0)
         far_moved = exchange(far_sums, 1)
@@ -343,8 +335,8 @@
         (lower_own,) = more_sums(plan, stacked, leaf_ids, classes, [(own + by_3, False)], near_other)
 
         def quarter(i):
-            part = slice(2 * PAIR * unit * i, 2 * PAIR * unit * (i + 1))
-            inner = slice(2 * PAIR * unit * (i % 2), 2 * PAIR * unit * (i % 2 + 1))
+            part = slice(PAIR * unit * i, PAIR * unit * (i + 1))
+            inner = slice(PAIR * unit * (i % 2), PAIR * unit * (i % 2 + 1))
             return (upper_own if i > 1 else lower_own)[:, inner] + near_core[:, part] + far_moved[:, part]
 
         held = quarter(0)

time: 49.9 us -> 49.6 us (level)
  waiting for transfers between devices: 12 us -> 11.4 us
    ppermute x13, waiting for transfers between devices: 12 us -> 11.4 us  [exchange(): return lax.ppermute(value, AXES, plan.permutation(*steps))]
where the time goes in v7:
time: 49.6 us; the launch traced here: 49.4 us
  Pallas kernels  19.3 us (39%)
  starting transfers between devices  17.7 us (36%)
  waiting for transfers between devices  11.4 us (23%)
  between operations  0.89 us (2%)
    ppermute x13, starting transfers between devices, exchange(): return lax.ppermute(value, AXES, plan.permutation(*steps))  17.7 us
    ppermute x13, waiting for transfers between devices, exchange(): return lax.ppermute(value, AXES, plan.permutation(*steps))  11.4 us
    pallas_call x3, Pallas kernels, more_sums(): pl.pallas_call(functools.partial(sums_kernel, plan, parts, chunk(rows, 20...  7.32 us
    pallas_call x1, Pallas kernels, first_sums(): pl.pallas_call(functools.partial(first_kernel, plan, slots, width), in_sp...  5.44 us
    pallas_call x2, Pallas kernels, apply_values(): pl.pallas_call(functools.partial(apply_kernel, plan, parts, chunk(rows, 2...  4.17 us
    pallas_call x1, Pallas kernels, finish(): pl.pallas_call(functools.partial(last_kernel, plan, parts, pieces, width)...  2.36 us
  transfers between devices with their start and end apart: 13, of which 8 were waited for; matrix products, arithmetic and copies ran while one was open for 0% of the time, Pallas kernels for 23%

profile of v7, /device:TPU:1, one launch (start us, length us, event | category | flops | bytes accessed | tf_op | source)
XLA Modules:
  0.0 49.4 jit_solution(7683249266057354379)
XLA Ops:
  0.6 0.0 copy-start
  0.6 5.4 %gradients_and_sums.1 = (bf16[208,8192]{1,0:T(8,128)(2,1)S(1)}, f32[200,512]{1,0:T(8,128)S(1)}) custom-call(f32[100,8192]{1,0:T(8,128)} %carried_ref.1, s32[1,8192]{1,0:T(1,128)} %bitcast.1, s32[32,8192]{1,0:T(8,128)} %refs_0_.1), custom_call_target="tpu_custom_call" | custom-call | flops 1744830464 | bytes 3407872 | tf_op jit(solution)/shard_map/gradients_and_sums/pallas_call | solution.py:179
  6.1 0.1 collective-permute-start
  6.2 0.0 copy-done
  6.2 2.4 %leaf_sums.3 = f32[200,512]{1,0:T(8,128)S(1)} custom-call(bf16[208,8192]{1,0:T(8,128)(2,1)S(1)} %get-tuple-element.8.stacked_ref, s32[32,8192]{1,0:T(8,128)S(1)} %copy-done, f32[200,512]{1,0:T(8,128)S(1)} %get-tuple-element.9._), custom_call_target="tpu_custom_call" | custom-call | flops 1744830464 | bytes 3407872 | tf_op jit(solution)/shard_map/leaf_sums/pallas_call | solution.py:201
  8.6 0.0 collective-permute-done
  8.7 0.1 add.45._
  8.7 2.8 %collective-permute-start.2 = (f32[200,512]{1,0:T(8,128)S(1)}, f32[200,512]{1,0:T(8,128)S(1)}, u32[]{:S(2)}, u32[]{:S(2)}) collective-permute-start(f32[200,512]{1,0:T(8,128)S(1)} %add.45._), channel_id=1, source_target_pairs={{0,8},{1,9},{2,10},{3,11},{4,20},{5,21},{6,22},{7,23},{8,0},{9,1},... | collective-permute-start | bytes 1228808 | tf_op jit(solution)/shard_map/ppermute | solution.py:319
  11.5 3.6 %leaf_sums.4 = (f32[200,512]{1,0:T(8,128)S(1)}, f32[200,256]{1,0:T(8,128)S(1)}) custom-call(bf16[208,8192]{1,0:T(8,128)(2,1)S(1)} %get-tuple-element.8.stacked_ref, s32[32,8192]{1,0:T(8,128)S(1)} %copy-done, f32[200,512]{1,0:T(8,128)S(1)} %add.45._), custom_call_target="tpu_custom_call" | custom-call | flops 2617245696 | bytes 3407872 | tf_op jit(solution)/shard_map/leaf_sums/pallas_call | solution.py:201
  15.0 0.0 copy-start.1
  15.0 0.3 collective-permute-start.1
  15.4 1.3 %leaf_sums.5 = f32[200,256]{1,0:T(8,128)S(1)} custom-call(bf16[208,8192]{1,0:T(8,128)(2,1)S(1)} %get-tuple-element.8.stacked_ref, s32[32,8192]{1,0:T(8,128)S(1)} %copy-done, f32[200,512]{1,0:T(8,128)S(1)} %get-tuple-element.10._), custom_call_target="tpu_custom_call" | custom-call | flops 872415232 | bytes 3407872 | tf_op jit(solution)/shard_map/leaf_sums/pallas_call | solution.py:201
  16.7 0.4 collective-permute-done.2
  17.1 0.0 collective-permute-done.1
  17.1 0.1 slice_add_fusion.4
  17.2 2.5 %collective-permute-start.3 = (f32[200,128]{1,0:T(8,128)S(1)}, f32[200,128]{1,0:T(8,128)S(1)}, u32[]{:S(2)}, u32[]{:S(2)}) collective-permute-start(f32[200,128]{1,0:T(8,128)S(1)} %get-tuple-element.14), channel_id=1, source_target_pairs={{0,17},{1,16},{2,19},{3,18},{4,13},{5,12},{6,15},{7,14},{8,25},{9,... | collective-permute-start | bytes 307208 | tf_op jit(solution)/shard_map/ppermute | solution.py:319
  19.7 0.3 collective-permute-start.5
  19.9 0.1 collective-permute-start.4
  20.0 2.0 %collective-permute-done.3 = f32[200,128]{1,0:T(8,128)S(1)} collective-permute-done((f32[200,128]{1,0:T(8,128)S(1)}, f32[200,128]{1,0:T(8,128)S(1)}, u32[]{:S(2)}, u32[]{:S(2)}) %collective-permute-start.3) | collective-permute-done | bytes 102432 | tf_op jit(solution)/shard_map/ppermute | solution.py:319
  22.0 1.5 %collective-permute-done.5 = f32[200,128]{1,0:T(8,128)S(1)} collective-permute-done((f32[200,128]{1,0:T(8,128)S(1)}, f32[200,128]{1,0:T(8,128)S(1)}, u32[]{:S(2)}, u32[]{:S(2)}) %collective-permute-start.5) | collective-permute-done | bytes 102432 | tf_op jit(solution)/shard_map/ppermute | solution.py:319
  23.5 1.2 %collective-permute-done.4 = f32[200,128]{1,0:T(8,128)S(1)} collective-permute-done((f32[200,128]{1,0:T(8,128)S(1)}, f32[200,128]{1,0:T(8,128)S(1)}, u32[]{:S(2)}, u32[]{:S(2)}) %collective-permute-start.4) | collective-permute-done | bytes 102432 | tf_op jit(solution)/shard_map/ppermute | solution.py:319
  24.7 0.1 fusion.2
  24.7 2.4 %collective-permute-start.6 = (f32[200,128]{1,0:T(8,128)S(1)}, f32[200,128]{1,0:T(8,128)S(1)}, u32[]{:S(2)}, u32[]{:S(2)}) collective-permute-start(f32[200,128]{1,0:T(8,128)S(1)} %fusion.2), channel_id=1, source_target_pairs={{0,2},{1,3},{2,0},{3,1},{4,6},{5,7},{6,4},{7,5},{8,10},{9,11},{10,... | collective-permute-start | bytes 307208 | tf_op jit(solution)/shard_map/ppermute | solution.py:319
  27.1 3.7 %collective-permute-done.6 = f32[200,128]{1,0:T(8,128)S(1)} collective-permute-done((f32[200,128]{1,0:T(8,128)S(1)}, f32[200,128]{1,0:T(8,128)S(1)}, u32[]{:S(2)}, u32[]{:S(2)}) %collective-permute-start.6) | collective-permute-done | bytes 102432 | tf_op jit(solution)/shard_map/ppermute | solution.py:319
  30.9 0.1 collective-permute-start.9
  31.0 0.9 %collective-permute-start.8 = (f32[100,128]{1,0:T(8,128)S(1)}, f32[100,128]{1,0:T(8,128)S(1)}, u32[]{:S(2)}, u32[]{:S(2)}) collective-permute-start(f32[100,128]{1,0:T(8,128)S(1)} %fusion.3), channel_id=1, source_target_pairs={{0,16},{1,17},{2,18},{3,19},{4,12},{5,13},{6,14},{7,15},{8,24},{9,... | collective-permute-start | bytes 153608 | tf_op jit(solution)/shard_map/ppermute | solution.py:319
  31.9 1.7 %collective-permute-start.7 = (f32[100,128]{1,0:T(8,128)S(1)}, f32[100,128]{1,0:T(8,128)S(1)}, u32[]{:S(2)}, u32[]{:S(2)}) collective-permute-start(f32[100,128]{1,0:T(8,128)S(1)} %fusion.3), channel_id=1, source_target_pairs={{0,1},{1,0},{2,3},{3,2},{4,5},{5,4},{6,7},{7,6},{8,9},{9,8},{10,11... | collective-permute-start | bytes 153608 | tf_op jit(solution)/shard_map/ppermute | solution.py:319
  33.6 1.2 %collective-permute-done.9 = f32[100,128]{1,0:T(8,128)S(1)} collective-permute-done((f32[100,128]{1,0:T(8,128)S(1)}, f32[100,128]{1,0:T(8,128)S(1)}, u32[]{:S(2)}, u32[]{:S(2)}) %collective-permute-start.9) | collective-permute-done | bytes 51232 | tf_op jit(solution)/shard_map/ppermute | solution.py:319
  34.8 0.0 collective-permute-done.8
  34.8 0.3 collective-permute-done.7
  35.1 4.5 %collective-permute-start.11 = (f32[100,512]{1,0:T(8,128)S(1)}, f32[100,512]{1,0:T(8,128)S(1)}, u32[]{:S(2)}, u32[]{:S(2)}) collective-permute-start(f32[100,512]{1,0:T(8,128)S(1)} %pad_maximum_fusion.refs_0_.refs_2_), channel_id=1, source_target_pairs={{0,4},{1,5},{2,6},{3,7},{4,0},{5,1},{6,2},{7,3},{8,12},{9,13},{10,... | collective-permute-start | bytes 614408 | tf_op jit(solution)/shard_map/ppermute | solution.py:319
  39.6 1.1 %collective-permute-start.10 = (f32[100,512]{1,0:T(8,128)S(1)}, f32[100,512]{1,0:T(8,128)S(1)}, u32[]{:S(2)}, u32[]{:S(2)}) collective-permute-start(f32[100,512]{1,0:T(8,128)S(1)} %pad_maximum_fusion.refs_0_.refs_2_), channel_id=1, source_target_pairs={{0,8},{1,9},{2,10},{3,11},{4,20},{5,21},{6,22},{7,23},{8,0},{9,1},... | collective-permute-start | bytes 614408 | tf_op jit(solution)/shard_map/ppermute | solution.py:319
  40.7 0.0 collective-permute-done.11.refs_1_.refs_4_
  40.7 0.0 copy-done.1
  40.7 2.8 %apply_values.2.carried_ref = f32[100,8192]{1,0:T(8,128)S(1)} custom-call(s32[32,8192]{1,0:T(8,128)S(1)} %copy-done, f32[100,8192]{1,0:T(8,128)S(1)} %copy-done.1, f32[100,512]{1,0:T(8,128)S(1)} %pad_maximum_fusion.refs_0_.refs_2_, f32[100,512]{1,0:T(8,128)S(1)} %collective-permute-done.11.refs_1_.refs_4_), custom_call_target="tpu_custom_call" | custom-call | flops 3355443200 | bytes 3276800 | tf_op jit(solution)/shard_map/apply_values/pallas_call | solution.py:244
  43.5 1.1 %collective-permute-done.10.refs_0_.refs_3_ = f32[100,512]{1,0:T(8,128)S(1)} collective-permute-done((f32[100,512]{1,0:T(8,128)S(1)}, f32[100,512]{1,0:T(8,128)S(1)}, u32[]{:S(2)}, u32[]{:S(2)}) %collective-permute-start.10) | collective-permute-done | bytes 204832 | tf_op jit(solution)/shard_map/ppermute | solution.py:319
  44.6 0.9 %collective-permute-start.12 = (f32[100,512]{1,0:T(8,128)S(1)}, f32[100,512]{1,0:T(8,128)S(1)}, u32[]{:S(2)}, u32[]{:S(2)}) collective-permute-start(f32[100,512]{1,0:T(8,128)S(1)} %collective-permute-done.10.refs_0_.refs_3_), channel_id=1, source_target_pairs={{0,4},{1,5},{2,6},{3,7},{4,0},{5,1},{6,2},{7,3},{8,12},{9,13},{10,... | collective-permute-start | bytes 614408 | tf_op jit(solution)/shard_map/ppermute | solution.py:319
  45.5 1.4 %apply_values.3.refs_1_ = f32[100,8192]{1,0:T(8,128)S(1)} custom-call(s32[32,8192]{1,0:T(8,128)S(1)} %copy-done, f32[100,8192]{1,0:T(8,128)S(1)} %apply_values.2.carried_ref, f32[100,512]{1,0:T(8,128)S(1)} %collective-permute-done.10.refs_0_.refs_3_), custom_call_target="tpu_custom_call" | custom-call | flops 1677721600 | bytes 3276800 | tf_op jit(solution)/shard_map/apply_values/pallas_call | solution.py:244
  46.9 0.0 collective-permute-done.12.refs_5_
  46.9 2.4 %apply_last_values.1 = (f32[100,8192]{1,0:T(8,128)}, f32[100,512]{1,0:T(8,128)}) custom-call(s32[32,8192]{1,0:T(8,128)S(1)} %copy-done, f32[100,8192]{1,0:T(8,128)S(1)} %apply_values.3.refs_1_, f32[100,512]{1,0:T(8,128)S(1)} %pad_maximum_fusion.refs_0_.refs_2_, f32[100,512]{1,0:T(8,128)S(1)} %collective-permute-done.10.refs_0_.refs_3_, ...), custom_call_target="tpu_custom_call" | custom-call | flops 1677721600 | bytes 3276800 | tf_op jit(solution)/shard_map/apply_last_values/pallas_call | solution.py:291
  (3 shorter events, 0.1 us)
Async XLA Ops:
  0.6 5.6 %copy-start = (s32[32,8192]{1,0:T(8,128)S(1)}, s32[32,8192]{1,0:T(8,128)}, u32[]{:S(2)}) copy-start(s32[32,8192]{1,0:T(8,128)} %refs_0_.1) | copy-start | bytes 3145732
  6.1 2.6 %collective-permute-start = (f32[200,512]{1,0:T(8,128)S(1)}, f32[200,512]{1,0:T(8,128)S(1)}, u32[]{:S(2)}, u32[]{:S(2)}) collective-permute-start(f32[200,512]{1,0:T(8,128)S(1)} %get-tuple-element.9._), channel_id=1, source_target_pairs={{0,4},{1,5},{2,6},{3,7},{4,0},{5,1},{6,2},{7,3},{8,12},{9,13},{10,... | collective-permute-start | bytes 1228808 | tf_op jit(solution)/shard_map/ppermute | solution.py:319
  8.7 8.4 %collective-permute-start.2 = (f32[200,512]{1,0:T(8,128)S(1)}, f32[200,512]{1,0:T(8,128)S(1)}, u32[]{:S(2)}, u32[]{:S(2)}) collective-permute-start(f32[200,512]{1,0:T(8,128)S(1)} %add.45._), channel_id=1, source_target_pairs={{0,8},{1,9},{2,10},{3,11},{4,20},{5,21},{6,22},{7,23},{8,0},{9,1},... | collective-permute-start | bytes 1228808 | tf_op jit(solution)/shard_map/ppermute | solution.py:319
  15.0 25.7 %copy-start.1 = (f32[100,8192]{1,0:T(8,128)S(1)}, f32[100,8192]{1,0:T(8,128)}, u32[]{:S(2)}) copy-start(f32[100,8192]{1,0:T(8,128)} %carried_ref.1) | copy-start | bytes 9830404
  15.0 2.1 %collective-permute-start.1 = (f32[200,512]{1,0:T(8,128)S(1)}, f32[200,512]{1,0:T(8,128)S(1)}, u32[]{:S(2)}, u32[]{:S(2)}) collective-permute-start(f32[200,512]{1,0:T(8,128)S(1)} %get-tuple-element.10._), channel_id=1, source_target_pairs={{0,4},{1,5},{2,6},{3,7},{4,0},{5,1},{6,2},{7,3},{8,12},{9,13},{10,... | collective-permute-start | bytes 1228808 | tf_op jit(solution)/shard_map/ppermute | solution.py:319
  17.2 4.9 %collective-permute-start.3 = (f32[200,128]{1,0:T(8,128)S(1)}, f32[200,128]{1,0:T(8,128)S(1)}, u32[]{:S(2)}, u32[]{:S(2)}) collective-permute-start(f32[200,128]{1,0:T(8,128)S(1)} %get-tuple-element.14), channel_id=1, source_target_pairs={{0,17},{1,16},{2,19},{3,18},{4,13},{5,12},{6,15},{7,14},{8,25},{9,... | collective-permute-start | bytes 307208 | tf_op jit(solution)/shard_map/ppermute | solution.py:319
  19.7 3.8 %collective-permute-start.5 = (f32[200,128]{1,0:T(8,128)S(1)}, f32[200,128]{1,0:T(8,128)S(1)}, u32[]{:S(2)}, u32[]{:S(2)}) collective-permute-start(f32[200,128]{1,0:T(8,128)S(1)} %get-tuple-element.15), channel_id=1, source_target_pairs={{0,16},{1,17},{2,18},{3,19},{4,12},{5,13},{6,14},{7,15},{8,24},{9,... | collective-permute-start | bytes 307208 | tf_op jit(solution)/shard_map/ppermute | solution.py:319
  19.9 4.7 %collective-permute-start.4 = (f32[200,128]{1,0:T(8,128)S(1)}, f32[200,128]{1,0:T(8,128)S(1)}, u32[]{:S(2)}, u32[]{:S(2)}) collective-permute-start(f32[200,128]{1,0:T(8,128)S(1)} %get-tuple-element.16), channel_id=1, source_target_pairs={{0,1},{1,0},{2,3},{3,2},{4,5},{5,4},{6,7},{7,6},{8,9},{9,8},{10,11... | collective-permute-start | bytes 307208 | tf_op jit(solution)/shard_map/ppermute | solution.py:319
  24.7 6.1 %collective-permute-start.6 = (f32[200,128]{1,0:T(8,128)S(1)}, f32[200,128]{1,0:T(8,128)S(1)}, u32[]{:S(2)}, u32[]{:S(2)}) collective-permute-start(f32[200,128]{1,0:T(8,128)S(1)} %fusion.2), channel_id=1, source_target_pairs={{0,2},{1,3},{2,0},{3,1},{4,6},{5,7},{6,4},{7,5},{8,10},{9,11},{10,... | collective-permute-start | bytes 307208 | tf_op jit(solution)/shard_map/ppermute | solution.py:319
  30.9 3.9 %collective-permute-start.9 = (f32[100,128]{1,0:T(8,128)S(1)}, f32[100,128]{1,0:T(8,128)S(1)}, u32[]{:S(2)}, u32[]{:S(2)}) collective-permute-start(f32[100,128]{1,0:T(8,128)S(1)} %fusion.3), channel_id=1, source_target_pairs={{0,17},{1,16},{2,19},{3,18},{4,13},{5,12},{6,15},{7,14},{8,25},{9,... | collective-permute-start | bytes 153608 | tf_op jit(solution)/shard_map/ppermute | solution.py:319
  31.0 3.9 %collective-permute-start.8 = (f32[100,128]{1,0:T(8,128)S(1)}, f32[100,128]{1,0:T(8,128)S(1)}, u32[]{:S(2)}, u32[]{:S(2)}) collective-permute-start(f32[100,128]{1,0:T(8,128)S(1)} %fusion.3), channel_id=1, source_target_pairs={{0,16},{1,17},{2,18},{3,19},{4,12},{5,13},{6,14},{7,15},{8,24},{9,... | collective-permute-start | bytes 153608 | tf_op jit(solution)/shard_map/ppermute | solution.py:319
  31.9 3.2 %collective-permute-start.7 = (f32[100,128]{1,0:T(8,128)S(1)}, f32[100,128]{1,0:T(8,128)S(1)}, u32[]{:S(2)}, u32[]{:S(2)}) collective-permute-start(f32[100,128]{1,0:T(8,128)S(1)} %fusion.3), channel_id=1, source_target_pairs={{0,1},{1,0},{2,3},{3,2},{4,5},{5,4},{6,7},{7,6},{8,9},{9,8},{10,11... | collective-permute-start | bytes 153608 | tf_op jit(solution)/shard_map/ppermute | solution.py:319
  35.1 5.6 %collective-permute-start.11 = (f32[100,512]{1,0:T(8,128)S(1)}, f32[100,512]{1,0:T(8,128)S(1)}, u32[]{:S(2)}, u32[]{:S(2)}) collective-permute-start(f32[100,512]{1,0:T(8,128)S(1)} %pad_maximum_fusion.refs_0_.refs_2_), channel_id=1, source_target_pairs={{0,4},{1,5},{2,6},{3,7},{4,0},{5,1},{6,2},{7,3},{8,12},{9,13},{10,... | collective-permute-start | bytes 614408 | tf_op jit(solution)/shard_map/ppermute | solution.py:319
  39.6 5.0 %collective-permute-start.10 = (f32[100,512]{1,0:T(8,128)S(1)}, f32[100,512]{1,0:T(8,128)S(1)}, u32[]{:S(2)}, u32[]{:S(2)}) collective-permute-start(f32[100,512]{1,0:T(8,128)S(1)} %pad_maximum_fusion.refs_0_.refs_2_), channel_id=1, source_target_pairs={{0,8},{1,9},{2,10},{3,11},{4,20},{5,21},{6,22},{7,23},{8,0},{9,1},... | collective-permute-start | bytes 614408 | tf_op jit(solution)/shard_map/ppermute | solution.py:319
  44.6 2.3 %collective-permute-start.12 = (f32[100,512]{1,0:T(8,128)S(1)}, f32[100,512]{1,0:T(8,128)S(1)}, u32[]{:S(2)}, u32[]{:S(2)}) collective-permute-start(f32[100,512]{1,0:T(8,128)S(1)} %collective-permute-done.10.refs_0_.refs_3_), channel_id=1, source_target_pairs={{0,4},{1,5},{2,6},{3,7},{4,0},{5,1},{6,2},{7,3},{8,12},{9,13},{10,... | collective-permute-start | bytes 614408 | tf_op jit(solution)/shard_map/ppermute | solution.py:319

commit v8 on v7

--- a/solution.py
+++ b/solution.py
@@ -106,11 +106,14 @@
 
 
 def write_sums(sums, out_ref, first):
-    turned = sums.T[: out_ref.shape[0]]
-    out_ref[:, pl.ds(first * PAIR, turned.shape[1])] = turned
-
-
-def add_up(plan, parts, width, stacked_ref, ids_ref, out_refs, start=0):
+    classes, half = out_ref.shape[0] // 2, sums.shape[1] // 2
+    turned = sums.T
+    part = pl.ds(first * PAIR, turned.shape[1])
+    out_ref[pl.ds(0, classes), part] = turned[:classes]
+    out_ref[pl.ds(classes, classes), part] = turned[half : half + classes]
+
+
+def add_up(plan, parts, width, stacked_ref, ids_ref, out_refs):
     device = own_device(plan)
     rows = stacked_ref.shape[1]
     todo = []
@@ -118,7 +121,7 @@
         tree = tree_rows(plan.code(device, other), slots)
         todo += [(tree[2 * i : 2 * i + 2], out_ref, i) for i in range(len(slots))]
     for group in groups(todo, 4):
-        tree = [row - start for item in group for row in item[0]]
+        tree = [row for item in group for row in item[0]]
         total = None
         for first in range(0, rows, width):
             part = pair_sums(one_hot(ids_ref, tree, first, width), stacked_ref[:, first : first + width])
@@ -127,39 +130,42 @@
             write_sums(total[i * PAIR : (i + 1) * PAIR], out_ref, place)
 
 
-def first_kernel(plan, slots, width, predict_hbm, labels_hbm, ids_hbm, stacked_ref, other_ref,
-                 predict_ref, labels_ref, ids_ref, sems):
+def first_kernel(plan, slots, width, predict_hbm, labels_hbm, ids_hbm, stacked_ref, other_ref, ids_ref,
+                 predict_ref, labels_ref, sems, ids_sems):
     rows = predict_ref.shape[1]
     classes = predict_ref.shape[0]
     count = rows // width
-    group = pl.multiple_of(tree_rows(plan.code(own_device(plan), True), [slots[0]])[0] & -len(slots) * 2, 8)
-    copies = [
-        pltpu.make_async_copy(labels_hbm, labels_ref, sems.at[0]),
-        pltpu.make_async_copy(ids_hbm.at[pl.ds(group, ids_ref.shape[0]), :], ids_ref, sems.at[1]),
-    ]
+    size = 2 * len(slots)
+    group = tree_rows(plan.code(own_device(plan), True), [slots[0]])[0] & -size
+    ids_copies = []
+    for i in range(ids_ref.shape[0] // size):
+        part = pl.ds(pl.multiple_of(lax.rem(group + i * size, ids_ref.shape[0]), size), size)
+        ids_copies.append(pltpu.make_async_copy(ids_hbm.at[part, :], ids_ref.at[part, :], ids_sems.at[i]))
+    copies = [pltpu.make_async_copy(labels_hbm, labels_ref, sems.at[0])]
     for i in range(count):
         part = pl.ds(i * width, width)
-        copies.append(pltpu.make_async_copy(predict_hbm.at[:, part], predict_ref.at[:, part], sems.at[2 + i]))
-    copies[2].start()
+        copies.append(pltpu.make_async_copy(predict_hbm.at[:, part], predict_ref.at[:, part], sems.at[1 + i]))
+    copies[1].start()
     copies[0].start()
-    for copy in copies[3:]:
+    for copy in copies[2:] + ids_copies:
         copy.start()
-    copies[1].start()
     copies[0].wait()
     for i in range(count):
-        copies[2 + i].wait()
+        copies[1 + i].wait()
         predict = predict_ref[:, i * width : (i + 1) * width]
         row_max = jnp.max(predict, axis=0, keepdims=True)
         exponent = jnp.exp(predict - row_max)
         probability = exponent * (1.0 / jnp.sum(exponent, axis=0, keepdims=True))
         index = lax.broadcasted_iota(jnp.int32, predict.shape, 0)
         gradient = jnp.where(index == labels_ref[:, i * width : (i + 1) * width], probability - 1.0, probability)
-        filler = jnp.zeros((stacked_ref.shape[0] - 2 * classes, width), jnp.float32)
+        filler = jnp.zeros((stacked_ref.shape[0] // 2 - classes, width), jnp.float32)
         stacked_ref[:, i * width : (i + 1) * width] = jnp.concatenate(
-            [gradient, probability * (1.0 - probability), filler], axis=0
+            [gradient, filler, probability * (1.0 - probability), filler], axis=0
         ).astype(jnp.bfloat16)
-    copies[1].wait()
-    add_up(plan, [(slots, True)], width, stacked_ref, ids_ref, (other_ref,), group)
+    ids_copies[0].wait()
+    add_up(plan, [(slots, True)], width, stacked_ref, ids_ref, (other_ref,))
+    for copy in ids_copies[1:]:
+        copy.wait()
 
 
 def sums_kernel(plan, parts, width, stacked_ref, ids_ref, _, *out_refs):
@@ -174,21 +180,22 @@
 
 def first_sums(plan, predict, labels, leaf_ids, slots):
     classes, rows = predict.shape
-    height = round_up(2 * classes, 16)
+    height = 2 * round_up(classes, 16)
     width = chunk(rows, 1024)
     return pl.pallas_call(
         functools.partial(first_kernel, plan, slots, width),
         in_specs=[IN_HBM, IN_HBM, IN_HBM],
-        out_specs=[IN_VMEM, IN_VMEM],
+        out_specs=[IN_VMEM, IN_VMEM, IN_VMEM],
         out_shape=[
             pltpu.VMEM((height, rows), jnp.bfloat16),
             pltpu.VMEM((2 * classes, PAIR * len(slots)), jnp.float32),
+            pltpu.VMEM(leaf_ids.shape, jnp.int32),
         ],
         scratch_shapes=[
             pltpu.VMEM((classes, rows), jnp.float32),
             pltpu.VMEM((1, rows), jnp.int32),
-            pltpu.VMEM((2 * len(slots), rows), jnp.int32),
-            pltpu.SemaphoreType.DMA((2 + rows // width,)),
+            pltpu.SemaphoreType.DMA((1 + rows // width,)),
+            pltpu.SemaphoreType.DMA((leaf_ids.shape[0] // (2 * len(slots)),)),
         ],
         compiler_params=pltpu.CompilerParams(vmem_limit_bytes=VMEM_LIMIT),
         cost_estimate=sums_cost(len(slots), height, rows),
@@ -324,7 +331,7 @@
         near = list(range(h // 2))
         own, by_3, by_2, by_both = (near[i * unit : (i + 1) * unit] for i in range(4))
 
-        stacked, far_other = first_sums(plan, predict, labels, leaf_ids, far)
+        stacked, far_other, leaf_ids = first_sums(plan, predict, labels, leaf_ids, far)
         (far_own,) = more_sums(plan, stacked, leaf_ids, classes, [(far, False)], far_other)
         far_sums = far_own + exchange(far_other, 0)
         far_moved = exchange(far_sums, 1)

time: 49.6 us -> 49.2 us (level)
  no operation moved by 1% of the time
where the time goes in v8:
time: 49.2 us; the launch traced here: 49.1 us
  Pallas kernels  19 us (39%)
  starting transfers between devices  17.6 us (36%)
  waiting for transfers between devices  11.3 us (23%)
  between operations  0.89 us (2%)
    ppermute x13, starting transfers between devices, exchange(): return lax.ppermute(value, AXES, plan.permutation(*steps))  17.6 us
    ppermute x13, waiting for transfers between devices, exchange(): return lax.ppermute(value, AXES, plan.permutation(*steps))  11.3 us
    pallas_call x3, Pallas kernels, more_sums(): pl.pallas_call(functools.partial(sums_kernel, plan, parts, chunk(rows, 20...  7.32 us
    pallas_call x1, Pallas kernels, first_sums(): pl.pallas_call(functools.partial(first_kernel, plan, slots, width), in_sp...  5.18 us
    pallas_call x2, Pallas kernels, apply_values(): pl.pallas_call(functools.partial(apply_kernel, plan, parts, chunk(rows, 2...  4.18 us
    pallas_call x1, Pallas kernels, finish(): pl.pallas_call(functools.partial(last_kernel, plan, parts, pieces, width)...  2.36 us
  transfers between devices with their start and end apart: 13, of which 8 were waited for; matrix products, arithmetic and copies ran while one was open for 0% of the time, Pallas kernels for 23%

profile of v8, /device:TPU:1, one launch (start us, length us, event | category | flops | bytes accessed | tf_op | source)
XLA Modules:
  0.0 49.1 jit_solution(11237694932835567078)
XLA Ops:
  0.6 5.2 %gradients_and_sums.1 = (bf16[224,8192]{1,0:T(8,128)(2,1)S(1)}, f32[200,512]{1,0:T(8,128)S(1)}, s32[32,8192]{1,0:T(8,128)S(1)}) custom-call(f32[100,8192]{1,0:T(8,128)} %carried_ref.1, s32[1,8192]{1,0:T(1,128)} %bitcast.1, s32[32,8192]{1,0:T(8,128)} %ids_hbm.1), custom_call_target="tpu_custom_call" | custom-call | flops 1879048192 | bytes 3670016 | tf_op jit(solution)/shard_map/gradients_and_sums/pallas_call | solution.py:185
  5.8 0.1 collective-permute-start
  5.9 2.4 %leaf_sums.3 = f32[200,512]{1,0:T(8,128)S(1)} custom-call(bf16[224,8192]{1,0:T(8,128)(2,1)S(1)} %get-tuple-element.10.stacked_ref, s32[32,8192]{1,0:T(8,128)S(1)} %get-tuple-element.9.ids_ref.refs_0_, f32[200,512]{1,0:T(8,128)S(1)} %get-tuple-element.11._), custom_call_target="tpu_custom_call" | custom-call | flops 1879048192 | bytes 3670016 | tf_op jit(solution)/shard_map/leaf_sums/pallas_call | solution.py:208
  8.4 0.0 collective-permute-done
  8.4 0.1 add.45._
  8.4 2.8 %collective-permute-start.2 = (f32[200,512]{1,0:T(8,128)S(1)}, f32[200,512]{1,0:T(8,128)S(1)}, u32[]{:S(2)}, u32[]{:S(2)}) collective-permute-start(f32[200,512]{1,0:T(8,128)S(1)} %add.45._), channel_id=1, source_target_pairs={{0,8},{1,9},{2,10},{3,11},{4,20},{5,21},{6,22},{7,23},{8,0},{9,1},... | collective-permute-start | bytes 1228808 | tf_op jit(solution)/shard_map/ppermute | solution.py:326
  11.2 3.6 %leaf_sums.4 = (f32[200,512]{1,0:T(8,128)S(1)}, f32[200,256]{1,0:T(8,128)S(1)}) custom-call(bf16[224,8192]{1,0:T(8,128)(2,1)S(1)} %get-tuple-element.10.stacked_ref, s32[32,8192]{1,0:T(8,128)S(1)} %get-tuple-element.9.ids_ref.refs_0_, f32[200,512]{1,0:T(8,128)S(1)} %add.45._), custom_call_target="tpu_custom_call" | custom-call | flops 2818572288 | bytes 3670016 | tf_op jit(solution)/shard_map/leaf_sums/pallas_call | solution.py:208
  14.8 0.0 copy-start
  14.8 0.3 collective-permute-start.1
  15.1 1.3 %leaf_sums.5 = f32[200,256]{1,0:T(8,128)S(1)} custom-call(bf16[224,8192]{1,0:T(8,128)(2,1)S(1)} %get-tuple-element.10.stacked_ref, s32[32,8192]{1,0:T(8,128)S(1)} %get-tuple-element.9.ids_ref.refs_0_, f32[200,512]{1,0:T(8,128)S(1)} %get-tuple-element.12._), custom_call_target="tpu_custom_call" | custom-call | flops 939524096 | bytes 3670016 | tf_op jit(solution)/shard_map/leaf_sums/pallas_call | solution.py:208
  16.5 0.4 collective-permute-done.2
  16.8 0.0 collective-permute-done.1
  16.8 0.1 slice_add_fusion.4
  16.9 2.5 %collective-permute-start.3 = (f32[200,128]{1,0:T(8,128)S(1)}, f32[200,128]{1,0:T(8,128)S(1)}, u32[]{:S(2)}, u32[]{:S(2)}) collective-permute-start(f32[200,128]{1,0:T(8,128)S(1)} %get-tuple-element.16), channel_id=1, source_target_pairs={{0,17},{1,16},{2,19},{3,18},{4,13},{5,12},{6,15},{7,14},{8,25},{9,... | collective-permute-start | bytes 307208 | tf_op jit(solution)/shard_map/ppermute | solution.py:326
  19.4 0.3 collective-permute-start.5
  19.7 0.1 collective-permute-start.4
  19.8 2.0 %collective-permute-done.3 = f32[200,128]{1,0:T(8,128)S(1)} collective-permute-done((f32[200,128]{1,0:T(8,128)S(1)}, f32[200,128]{1,0:T(8,128)S(1)}, u32[]{:S(2)}, u32[]{:S(2)}) %collective-permute-start.3) | collective-permute-done | bytes 102432 | tf_op jit(solution)/shard_map/ppermute | solution.py:326
  21.7 1.5 %collective-permute-done.5 = f32[200,128]{1,0:T(8,128)S(1)} collective-permute-done((f32[200,128]{1,0:T(8,128)S(1)}, f32[200,128]{1,0:T(8,128)S(1)}, u32[]{:S(2)}, u32[]{:S(2)}) %collective-permute-start.5) | collective-permute-done | bytes 102432 | tf_op jit(solution)/shard_map/ppermute | solution.py:326
  23.2 1.2 %collective-permute-done.4 = f32[200,128]{1,0:T(8,128)S(1)} collective-permute-done((f32[200,128]{1,0:T(8,128)S(1)}, f32[200,128]{1,0:T(8,128)S(1)}, u32[]{:S(2)}, u32[]{:S(2)}) %collective-permute-start.4) | collective-permute-done | bytes 102432 | tf_op jit(solution)/shard_map/ppermute | solution.py:326
  24.4 0.1 fusion.2
  24.5 2.4 %collective-permute-start.6 = (f32[200,128]{1,0:T(8,128)S(1)}, f32[200,128]{1,0:T(8,128)S(1)}, u32[]{:S(2)}, u32[]{:S(2)}) collective-permute-start(f32[200,128]{1,0:T(8,128)S(1)} %fusion.2), channel_id=1, source_target_pairs={{0,2},{1,3},{2,0},{3,1},{4,6},{5,7},{6,4},{7,5},{8,10},{9,11},{10,... | collective-permute-start | bytes 307208 | tf_op jit(solution)/shard_map/ppermute | solution.py:326
  26.9 3.7 %collective-permute-done.6 = f32[200,128]{1,0:T(8,128)S(1)} collective-permute-done((f32[200,128]{1,0:T(8,128)S(1)}, f32[200,128]{1,0:T(8,128)S(1)}, u32[]{:S(2)}, u32[]{:S(2)}) %collective-permute-start.6) | collective-permute-done | bytes 102432 | tf_op jit(solution)/shard_map/ppermute | solution.py:326
  30.6 0.1 collective-permute-start.9
  30.7 0.9 %collective-permute-start.8 = (f32[100,128]{1,0:T(8,128)S(1)}, f32[100,128]{1,0:T(8,128)S(1)}, u32[]{:S(2)}, u32[]{:S(2)}) collective-permute-start(f32[100,128]{1,0:T(8,128)S(1)} %fusion.3), channel_id=1, source_target_pairs={{0,16},{1,17},{2,18},{3,19},{4,12},{5,13},{6,14},{7,15},{8,24},{9,... | collective-permute-start | bytes 153608 | tf_op jit(solution)/shard_map/ppermute | solution.py:326
  31.6 1.7 %collective-permute-start.7 = (f32[100,128]{1,0:T(8,128)S(1)}, f32[100,128]{1,0:T(8,128)S(1)}, u32[]{:S(2)}, u32[]{:S(2)}) collective-permute-start(f32[100,128]{1,0:T(8,128)S(1)} %fusion.3), channel_id=1, source_target_pairs={{0,1},{1,0},{2,3},{3,2},{4,5},{5,4},{6,7},{7,6},{8,9},{9,8},{10,11... | collective-permute-start | bytes 153608 | tf_op jit(solution)/shard_map/ppermute | solution.py:326
  33.3 1.2 %collective-permute-done.9 = f32[100,128]{1,0:T(8,128)S(1)} collective-permute-done((f32[100,128]{1,0:T(8,128)S(1)}, f32[100,128]{1,0:T(8,128)S(1)}, u32[]{:S(2)}, u32[]{:S(2)}) %collective-permute-start.9) | collective-permute-done | bytes 51232 | tf_op jit(solution)/shard_map/ppermute | solution.py:326
  34.5 0.0 collective-permute-done.8
  34.5 0.3 collective-permute-done.7
  34.9 4.4 %collective-permute-start.11 = (f32[100,512]{1,0:T(8,128)S(1)}, f32[100,512]{1,0:T(8,128)S(1)}, u32[]{:S(2)}, u32[]{:S(2)}) collective-permute-start(f32[100,512]{1,0:T(8,128)S(1)} %pad_maximum_fusion.refs_0_.refs_2_), channel_id=1, source_target_pairs={{0,4},{1,5},{2,6},{3,7},{4,0},{5,1},{6,2},{7,3},{8,12},{9,13},{10,... | collective-permute-start | bytes 614408 | tf_op jit(solution)/shard_map/ppermute | solution.py:326
  39.2 1.1 %collective-permute-start.10 = (f32[100,512]{1,0:T(8,128)S(1)}, f32[100,512]{1,0:T(8,128)S(1)}, u32[]{:S(2)}, u32[]{:S(2)}) collective-permute-start(f32[100,512]{1,0:T(8,128)S(1)} %pad_maximum_fusion.refs_0_.refs_2_), channel_id=1, source_target_pairs={{0,8},{1,9},{2,10},{3,11},{4,20},{5,21},{6,22},{7,23},{8,0},{9,1},... | collective-permute-start | bytes 614408 | tf_op jit(solution)/shard_map/ppermute | solution.py:326
  40.3 0.0 collective-permute-done.11.refs_1_.refs_4_
  40.3 0.0 copy-done
  40.3 2.8 %apply_values.2.carried_ref = f32[100,8192]{1,0:T(8,128)S(1)} custom-call(s32[32,8192]{1,0:T(8,128)S(1)} %get-tuple-element.9.ids_ref.refs_0_, f32[100,8192]{1,0:T(8,128)S(1)} %copy-done, f32[100,512]{1,0:T(8,128)S(1)} %pad_maximum_fusion.refs_0_.refs_2_, f32[100,512]{1,0:T(8,128)S(1)} %collective-permute-done.11.refs_1_.refs_4_), custom_call_target="tpu_custom_call" | custom-call | flops 3355443200 | bytes 3276800 | tf_op jit(solution)/shard_map/apply_values/pallas_call | solution.py:251
  43.1 1.1 %collective-permute-done.10.refs_0_.refs_3_ = f32[100,512]{1,0:T(8,128)S(1)} collective-permute-done((f32[100,512]{1,0:T(8,128)S(1)}, f32[100,512]{1,0:T(8,128)S(1)}, u32[]{:S(2)}, u32[]{:S(2)}) %collective-permute-start.10) | collective-permute-done | bytes 204832 | tf_op jit(solution)/shard_map/ppermute | solution.py:326
  44.2 0.9 %collective-permute-start.12 = (f32[100,512]{1,0:T(8,128)S(1)}, f32[100,512]{1,0:T(8,128)S(1)}, u32[]{:S(2)}, u32[]{:S(2)}) collective-permute-start(f32[100,512]{1,0:T(8,128)S(1)} %collective-permute-done.10.refs_0_.refs_3_), channel_id=1, source_target_pairs={{0,4},{1,5},{2,6},{3,7},{4,0},{5,1},{6,2},{7,3},{8,12},{9,13},{10,... | collective-permute-start | bytes 614408 | tf_op jit(solution)/shard_map/ppermute | solution.py:326
  45.2 1.4 %apply_values.3.refs_1_ = f32[100,8192]{1,0:T(8,128)S(1)} custom-call(s32[32,8192]{1,0:T(8,128)S(1)} %get-tuple-element.9.ids_ref.refs_0_, f32[100,8192]{1,0:T(8,128)S(1)} %apply_values.2.carried_ref, f32[100,512]{1,0:T(8,128)S(1)} %collective-permute-done.10.refs_0_.refs_3_), custom_call_target="tpu_custom_call" | custom-call | flops 1677721600 | bytes 3276800 | tf_op jit(solution)/shard_map/apply_values/pallas_call | solution.py:251
  46.5 0.0 collective-permute-done.12.refs_5_
  46.6 2.4 %apply_last_values.1 = (f32[100,8192]{1,0:T(8,128)}, f32[100,512]{1,0:T(8,128)}) custom-call(s32[32,8192]{1,0:T(8,128)S(1)} %get-tuple-element.9.ids_ref.refs_0_, f32[100,8192]{1,0:T(8,128)S(1)} %apply_values.3.refs_1_, f32[100,512]{1,0:T(8,128)S(1)} %pad_maximum_fusion.refs_0_.refs_2_, f32[100,512]{1,0:T(8,128)S(1)} %collective-permute-done.10.refs_0_.refs_3_, ...), custom_call_target="tpu_custom_call" | custom-call | flops 1677721600 | bytes 3276800 | tf_op jit(solution)/shard_map/apply_last_values/pallas_call | solution.py:298
  (3 shorter events, 0.1 us)
Async XLA Ops:
  5.8 2.5 %collective-permute-start = (f32[200,512]{1,0:T(8,128)S(1)}, f32[200,512]{1,0:T(8,128)S(1)}, u32[]{:S(2)}, u32[]{:S(2)}) collective-permute-start(f32[200,512]{1,0:T(8,128)S(1)} %get-tuple-element.11._), channel_id=1, source_target_pairs={{0,4},{1,5},{2,6},{3,7},{4,0},{5,1},{6,2},{7,3},{8,12},{9,13},{10,... | collective-permute-start | bytes 1228808 | tf_op jit(solution)/shard_map/ppermute | solution.py:326
  8.4 8.4 %collective-permute-start.2 = (f32[200,512]{1,0:T(8,128)S(1)}, f32[200,512]{1,0:T(8,128)S(1)}, u32[]{:S(2)}, u32[]{:S(2)}) collective-permute-start(f32[200,512]{1,0:T(8,128)S(1)} %add.45._), channel_id=1, source_target_pairs={{0,8},{1,9},{2,10},{3,11},{4,20},{5,21},{6,22},{7,23},{8,0},{9,1},... | collective-permute-start | bytes 1228808 | tf_op jit(solution)/shard_map/ppermute | solution.py:326
  14.8 25.6 %copy-start = (f32[100,8192]{1,0:T(8,128)S(1)}, f32[100,8192]{1,0:T(8,128)}, u32[]{:S(2)}) copy-start(f32[100,8192]{1,0:T(8,128)} %carried_ref.1) | copy-start | bytes 9830404
  14.8 2.1 %collective-permute-start.1 = (f32[200,512]{1,0:T(8,128)S(1)}, f32[200,512]{1,0:T(8,128)S(1)}, u32[]{:S(2)}, u32[]{:S(2)}) collective-permute-start(f32[200,512]{1,0:T(8,128)S(1)} %get-tuple-element.12._), channel_id=1, source_target_pairs={{0,4},{1,5},{2,6},{3,7},{4,0},{5,1},{6,2},{7,3},{8,12},{9,13},{10,... | collective-permute-start | bytes 1228808 | tf_op jit(solution)/shard_map/ppermute | solution.py:326
  16.9 4.9 %collective-permute-start.3 = (f32[200,128]{1,0:T(8,128)S(1)}, f32[200,128]{1,0:T(8,128)S(1)}, u32[]{:S(2)}, u32[]{:S(2)}) collective-permute-start(f32[200,128]{1,0:T(8,128)S(1)} %get-tuple-element.16), channel_id=1, source_target_pairs={{0,17},{1,16},{2,19},{3,18},{4,13},{5,12},{6,15},{7,14},{8,25},{9,... | collective-permute-start | bytes 307208 | tf_op jit(solution)/shard_map/ppermute | solution.py:326
  19.4 3.8 %collective-permute-start.5 = (f32[200,128]{1,0:T(8,128)S(1)}, f32[200,128]{1,0:T(8,128)S(1)}, u32[]{:S(2)}, u32[]{:S(2)}) collective-permute-start(f32[200,128]{1,0:T(8,128)S(1)} %get-tuple-element.17), channel_id=1, source_target_pairs={{0,16},{1,17},{2,18},{3,19},{4,12},{5,13},{6,14},{7,15},{8,24},{9,... | collective-permute-start | bytes 307208 | tf_op jit(solution)/shard_map/ppermute | solution.py:326
  19.7 4.7 %collective-permute-start.4 = (f32[200,128]{1,0:T(8,128)S(1)}, f32[200,128]{1,0:T(8,128)S(1)}, u32[]{:S(2)}, u32[]{:S(2)}) collective-permute-start(f32[200,128]{1,0:T(8,128)S(1)} %get-tuple-element.18), channel_id=1, source_target_pairs={{0,1},{1,0},{2,3},{3,2},{4,5},{5,4},{6,7},{7,6},{8,9},{9,8},{10,11... | collective-permute-start | bytes 307208 | tf_op jit(solution)/shard_map/ppermute | solution.py:326
  24.5 6.1 %collective-permute-start.6 = (f32[200,128]{1,0:T(8,128)S(1)}, f32[200,128]{1,0:T(8,128)S(1)}, u32[]{:S(2)}, u32[]{:S(2)}) collective-permute-start(f32[200,128]{1,0:T(8,128)S(1)} %fusion.2), channel_id=1, source_target_pairs={{0,2},{1,3},{2,0},{3,1},{4,6},{5,7},{6,4},{7,5},{8,10},{9,11},{10,... | collective-permute-start | bytes 307208 | tf_op jit(solution)/shard_map/ppermute | solution.py:326
  30.6 3.9 %collective-permute-start.9 = (f32[100,128]{1,0:T(8,128)S(1)}, f32[100,128]{1,0:T(8,128)S(1)}, u32[]{:S(2)}, u32[]{:S(2)}) collective-permute-start(f32[100,128]{1,0:T(8,128)S(1)} %fusion.3), channel_id=1, source_target_pairs={{0,17},{1,16},{2,19},{3,18},{4,13},{5,12},{6,15},{7,14},{8,25},{9,... | collective-permute-start | bytes 153608 | tf_op jit(solution)/shard_map/ppermute | solution.py:326
  30.7 3.9 %collective-permute-start.8 = (f32[100,128]{1,0:T(8,128)S(1)}, f32[100,128]{1,0:T(8,128)S(1)}, u32[]{:S(2)}, u32[]{:S(2)}) collective-permute-start(f32[100,128]{1,0:T(8,128)S(1)} %fusion.3), channel_id=1, source_target_pairs={{0,16},{1,17},{2,18},{3,19},{4,12},{5,13},{6,14},{7,15},{8,24},{9,... | collective-permute-start | bytes 153608 | tf_op jit(solution)/shard_map/ppermute | solution.py:326
  31.6 3.2 %collective-permute-start.7 = (f32[100,128]{1,0:T(8,128)S(1)}, f32[100,128]{1,0:T(8,128)S(1)}, u32[]{:S(2)}, u32[]{:S(2)}) collective-permute-start(f32[100,128]{1,0:T(8,128)S(1)} %fusion.3), channel_id=1, source_target_pairs={{0,1},{1,0},{2,3},{3,2},{4,5},{5,4},{6,7},{7,6},{8,9},{9,8},{10,11... | collective-permute-start | bytes 153608 | tf_op jit(solution)/shard_map/ppermute | solution.py:326
  34.9 5.5 %collective-permute-start.11 = (f32[100,512]{1,0:T(8,128)S(1)}, f32[100,512]{1,0:T(8,128)S(1)}, u32[]{:S(2)}, u32[]{:S(2)}) collective-permute-start(f32[100,512]{1,0:T(8,128)S(1)} %pad_maximum_fusion.refs_0_.refs_2_), channel_id=1, source_target_pairs={{0,4},{1,5},{2,6},{3,7},{4,0},{5,1},{6,2},{7,3},{8,12},{9,13},{10,... | collective-permute-start | bytes 614408 | tf_op jit(solution)/shard_map/ppermute | solution.py:326
  39.2 5.0 %collective-permute-start.10 = (f32[100,512]{1,0:T(8,128)S(1)}, f32[100,512]{1,0:T(8,128)S(1)}, u32[]{:S(2)}, u32[]{:S(2)}) collective-permute-start(f32[100,512]{1,0:T(8,128)S(1)} %pad_maximum_fusion.refs_0_.refs_2_), channel_id=1, source_target_pairs={{0,8},{1,9},{2,10},{3,11},{4,20},{5,21},{6,22},{7,23},{8,0},{9,1},... | collective-permute-start | bytes 614408 | tf_op jit(solution)/shard_map/ppermute | solution.py:326
  44.2 2.3 %collective-permute-start.12 = (f32[100,512]{1,0:T(8,128)S(1)}, f32[100,512]{1,0:T(8,128)S(1)}, u32[]{:S(2)}, u32[]{:S(2)}) collective-permute-start(f32[100,512]{1,0:T(8,128)S(1)} %collective-permute-done.10.refs_0_.refs_3_), channel_id=1, source_target_pairs={{0,4},{1,5},{2,6},{3,7},{4,0},{5,1},{6,2},{7,3},{8,12},{9,13},{10,... | collective-permute-start | bytes 614408 | tf_op jit(solution)/shard_map/ppermute | solution.py:326

commit v9 on v8

--- a/solution.py
+++ b/solution.py
@@ -262,21 +262,24 @@
 def last_kernel(plan, parts, pieces, width, *refs):
     ids_ref, carried_ref = refs[:2]
     value_refs = refs[2 : 2 + len(pieces)]
-    out_hbm, own_hbm, out_ref, own_ref, table_ref, sems = refs[2 + len(pieces) :]
+    out_hbm, own_hbm, out_ref, own_ref, sems = refs[2 + len(pieces) :]
     rows = ids_ref.shape[1]
     count = rows // width
     device = own_device(plan)
     half = plan.pairs // 2
-    for (slots, other), value_ref in zip(pieces, value_refs):
-        first = slots[0] + (half if other else 0)
-        table_ref[:, pl.ds(first * PAIR, len(slots) * PAIR)] = value_ref[...]
     mine, theirs = plan.code(device, False), plan.code(device, True)
     per_leaf = plan.pairs // plan.leaf
     for i in range(per_leaf):
         pair = lax.axis_index("leaf").astype(jnp.int32) * per_leaf + i
         place = pair ^ mine
         place = jnp.where(place < half, place, (pair ^ theirs) + half)
-        own_ref[:, pl.ds(i * PAIR, PAIR)] = table_ref[:, pl.ds(pl.multiple_of(place * PAIR, PAIR), PAIR)]
+        picked = None
+        for (slots, other), value_ref in zip(pieces, value_refs):
+            offset = place - (slots[0] + (half if other else 0))
+            inside = jnp.clip(offset, 0, len(slots) - 1)
+            block = value_ref[:, pl.ds(pl.multiple_of(inside * PAIR, PAIR), PAIR)]
+            picked = block if picked is None else jnp.where(offset == inside, block, picked)
+        own_ref[:, pl.ds(i * PAIR, PAIR)] = picked
     writes = []
     last = [value_refs[pieces.index(piece)] for piece in parts]
     for i in range(count):
@@ -303,7 +306,6 @@
         scratch_shapes=[
             pltpu.VMEM((classes, rows), jnp.float32),
             pltpu.VMEM(own, jnp.float32),
-            pltpu.VMEM((classes, plan.pairs * PAIR), jnp.float32),
             pltpu.SemaphoreType.DMA((rows // width + 1,)),
         ],
         compiler_params=pltpu.CompilerParams(vmem_limit_bytes=VMEM_LIMIT),

time: 49.2 us -> 49.2 us (level)
  no operation moved by 1% of the time
where the time goes in v9:
time: 49.2 us; the launch traced here: 49.1 us
  Pallas kernels  19 us (39%)
  starting transfers between devices  17.6 us (36%)
  waiting for transfers between devices  11.3 us (23%)
  between operations  0.89 us (2%)
    ppermute x13, starting transfers between devices, exchange(): return lax.ppermute(value, AXES, plan.permutation(*steps))  17.6 us
    ppermute x13, waiting for transfers between devices, exchange(): return lax.ppermute(value, AXES, plan.permutation(*steps))  11.3 us
    pallas_call x3, Pallas kernels, more_sums(): pl.pallas_call(functools.partial(sums_kernel, plan, parts, chunk(rows, 20...  7.32 us
    pallas_call x1, Pallas kernels, first_sums(): pl.pallas_call(functools.partial(first_kernel, plan, slots, width), in_sp...  5.18 us
    pallas_call x2, Pallas kernels, apply_values(): pl.pallas_call(functools.partial(apply_kernel, plan, parts, chunk(rows, 2...  4.18 us
    pallas_call x1, Pallas kernels, finish(): pl.pallas_call(functools.partial(last_kernel, plan, parts, pieces, width)...  2.33 us
  transfers between devices with their start and end apart: 13, of which 8 were waited for; matrix products, arithmetic and copies ran while one was open for 0% of the time, Pallas kernels for 23%

profile of v9, /device:TPU:1, one launch (start us, length us, event | category | flops | bytes accessed | tf_op | source)
XLA Modules:
  0.0 49.1 jit_solution(1115724831882703935)
XLA Ops:
  0.6 5.2 %gradients_and_sums.1 = (bf16[224,8192]{1,0:T(8,128)(2,1)S(1)}, f32[200,512]{1,0:T(8,128)S(1)}, s32[32,8192]{1,0:T(8,128)S(1)}) custom-call(f32[100,8192]{1,0:T(8,128)} %carried_ref.1, s32[1,8192]{1,0:T(1,128)} %bitcast.1, s32[32,8192]{1,0:T(8,128)} %ids_hbm.1), custom_call_target="tpu_custom_call" | custom-call | flops 1879048192 | bytes 3670016 | tf_op jit(solution)/shard_map/gradients_and_sums/pallas_call | solution.py:185
  5.8 0.1 collective-permute-start
  5.9 2.4 %leaf_sums.3 = f32[200,512]{1,0:T(8,128)S(1)} custom-call(bf16[224,8192]{1,0:T(8,128)(2,1)S(1)} %get-tuple-element.10.stacked_ref, s32[32,8192]{1,0:T(8,128)S(1)} %get-tuple-element.9.ids_ref.refs_0_, f32[200,512]{1,0:T(8,128)S(1)} %get-tuple-element.11._), custom_call_target="tpu_custom_call" | custom-call | flops 1879048192 | bytes 3670016 | tf_op jit(solution)/shard_map/leaf_sums/pallas_call | solution.py:208
  8.4 0.0 collective-permute-done
  8.4 0.1 add.45._
  8.4 2.8 %collective-permute-start.2 = (f32[200,512]{1,0:T(8,128)S(1)}, f32[200,512]{1,0:T(8,128)S(1)}, u32[]{:S(2)}, u32[]{:S(2)}) collective-permute-start(f32[200,512]{1,0:T(8,128)S(1)} %add.45._), channel_id=1, source_target_pairs={{0,8},{1,9},{2,10},{3,11},{4,20},{5,21},{6,22},{7,23},{8,0},{9,1},... | collective-permute-start | bytes 1228808 | tf_op jit(solution)/shard_map/ppermute | solution.py:328
  11.2 3.6 %leaf_sums.4 = (f32[200,512]{1,0:T(8,128)S(1)}, f32[200,256]{1,0:T(8,128)S(1)}) custom-call(bf16[224,8192]{1,0:T(8,128)(2,1)S(1)} %get-tuple-element.10.stacked_ref, s32[32,8192]{1,0:T(8,128)S(1)} %get-tuple-element.9.ids_ref.refs_0_, f32[200,512]{1,0:T(8,128)S(1)} %add.45._), custom_call_target="tpu_custom_call" | custom-call | flops 2818572288 | bytes 3670016 | tf_op jit(solution)/shard_map/leaf_sums/pallas_call | solution.py:208
  14.8 0.0 copy-start
  14.8 0.3 collective-permute-start.1
  15.1 1.3 %leaf_sums.5 = f32[200,256]{1,0:T(8,128)S(1)} custom-call(bf16[224,8192]{1,0:T(8,128)(2,1)S(1)} %get-tuple-element.10.stacked_ref, s32[32,8192]{1,0:T(8,128)S(1)} %get-tuple-element.9.ids_ref.refs_0_, f32[200,512]{1,0:T(8,128)S(1)} %get-tuple-element.12._), custom_call_target="tpu_custom_call" | custom-call | flops 939524096 | bytes 3670016 | tf_op jit(solution)/shard_map/leaf_sums/pallas_call | solution.py:208
  16.5 0.4 collective-permute-done.2
  16.8 0.0 collective-permute-done.1
  16.8 0.1 slice_add_fusion.4
  16.9 2.5 %collective-permute-start.3 = (f32[200,128]{1,0:T(8,128)S(1)}, f32[200,128]{1,0:T(8,128)S(1)}, u32[]{:S(2)}, u32[]{:S(2)}) collective-permute-start(f32[200,128]{1,0:T(8,128)S(1)} %get-tuple-element.16), channel_id=1, source_target_pairs={{0,17},{1,16},{2,19},{3,18},{4,13},{5,12},{6,15},{7,14},{8,25},{9,... | collective-permute-start | bytes 307208 | tf_op jit(solution)/shard_map/ppermute | solution.py:328
  19.4 0.3 collective-permute-start.5
  19.7 0.1 collective-permute-start.4
  19.8 2.0 %collective-permute-done.3 = f32[200,128]{1,0:T(8,128)S(1)} collective-permute-done((f32[200,128]{1,0:T(8,128)S(1)}, f32[200,128]{1,0:T(8,128)S(1)}, u32[]{:S(2)}, u32[]{:S(2)}) %collective-permute-start.3) | collective-permute-done | bytes 102432 | tf_op jit(solution)/shard_map/ppermute | solution.py:328
  21.7 1.5 %collective-permute-done.5 = f32[200,128]{1,0:T(8,128)S(1)} collective-permute-done((f32[200,128]{1,0:T(8,128)S(1)}, f32[200,128]{1,0:T(8,128)S(1)}, u32[]{:S(2)}, u32[]{:S(2)}) %collective-permute-start.5) | collective-permute-done | bytes 102432 | tf_op jit(solution)/shard_map/ppermute | solution.py:328
  23.2 1.2 %collective-permute-done.4 = f32[200,128]{1,0:T(8,128)S(1)} collective-permute-done((f32[200,128]{1,0:T(8,128)S(1)}, f32[200,128]{1,0:T(8,128)S(1)}, u32[]{:S(2)}, u32[]{:S(2)}) %collective-permute-start.4) | collective-permute-done | bytes 102432 | tf_op jit(solution)/shard_map/ppermute | solution.py:328
  24.4 0.1 fusion.2
  24.5 2.4 %collective-permute-start.6 = (f32[200,128]{1,0:T(8,128)S(1)}, f32[200,128]{1,0:T(8,128)S(1)}, u32[]{:S(2)}, u32[]{:S(2)}) collective-permute-start(f32[200,128]{1,0:T(8,128)S(1)} %fusion.2), channel_id=1, source_target_pairs={{0,2},{1,3},{2,0},{3,1},{4,6},{5,7},{6,4},{7,5},{8,10},{9,11},{10,... | collective-permute-start | bytes 307208 | tf_op jit(solution)/shard_map/ppermute | solution.py:328
  26.9 3.7 %collective-permute-done.6 = f32[200,128]{1,0:T(8,128)S(1)} collective-permute-done((f32[200,128]{1,0:T(8,128)S(1)}, f32[200,128]{1,0:T(8,128)S(1)}, u32[]{:S(2)}, u32[]{:S(2)}) %collective-permute-start.6) | collective-permute-done | bytes 102432 | tf_op jit(solution)/shard_map/ppermute | solution.py:328
  30.6 0.1 collective-permute-start.9
  30.7 0.9 %collective-permute-start.8 = (f32[100,128]{1,0:T(8,128)S(1)}, f32[100,128]{1,0:T(8,128)S(1)}, u32[]{:S(2)}, u32[]{:S(2)}) collective-permute-start(f32[100,128]{1,0:T(8,128)S(1)} %fusion.3), channel_id=1, source_target_pairs={{0,16},{1,17},{2,18},{3,19},{4,12},{5,13},{6,14},{7,15},{8,24},{9,... | collective-permute-start | bytes 153608 | tf_op jit(solution)/shard_map/ppermute | solution.py:328
  31.6 1.7 %collective-permute-start.7 = (f32[100,128]{1,0:T(8,128)S(1)}, f32[100,128]{1,0:T(8,128)S(1)}, u32[]{:S(2)}, u32[]{:S(2)}) collective-permute-start(f32[100,128]{1,0:T(8,128)S(1)} %fusion.3), channel_id=1, source_target_pairs={{0,1},{1,0},{2,3},{3,2},{4,5},{5,4},{6,7},{7,6},{8,9},{9,8},{10,11... | collective-permute-start | bytes 153608 | tf_op jit(solution)/shard_map/ppermute | solution.py:328
  33.3 1.2 %collective-permute-done.9 = f32[100,128]{1,0:T(8,128)S(1)} collective-permute-done((f32[100,128]{1,0:T(8,128)S(1)}, f32[100,128]{1,0:T(8,128)S(1)}, u32[]{:S(2)}, u32[]{:S(2)}) %collective-permute-start.9) | collective-permute-done | bytes 51232 | tf_op jit(solution)/shard_map/ppermute | solution.py:328
  34.5 0.0 collective-permute-done.8
  34.5 0.3 collective-permute-done.7
  34.9 4.4 %collective-permute-start.11 = (f32[100,512]{1,0:T(8,128)S(1)}, f32[100,512]{1,0:T(8,128)S(1)}, u32[]{:S(2)}, u32[]{:S(2)}) collective-permute-start(f32[100,512]{1,0:T(8,128)S(1)} %pad_maximum_fusion.refs_0_.refs_2_), channel_id=1, source_target_pairs={{0,4},{1,5},{2,6},{3,7},{4,0},{5,1},{6,2},{7,3},{8,12},{9,13},{10,... | collective-permute-start | bytes 614408 | tf_op jit(solution)/shard_map/ppermute | solution.py:328
  39.2 1.1 %collective-permute-start.10 = (f32[100,512]{1,0:T(8,128)S(1)}, f32[100,512]{1,0:T(8,128)S(1)}, u32[]{:S(2)}, u32[]{:S(2)}) collective-permute-start(f32[100,512]{1,0:T(8,128)S(1)} %pad_maximum_fusion.refs_0_.refs_2_), channel_id=1, source_target_pairs={{0,8},{1,9},{2,10},{3,11},{4,20},{5,21},{6,22},{7,23},{8,0},{9,1},... | collective-permute-start | bytes 614408 | tf_op jit(solution)/shard_map/ppermute | solution.py:328
  40.3 0.0 collective-permute-done.11.refs_1_.refs_4_
  40.3 0.0 copy-done
  40.3 2.8 %apply_values.2.carried_ref = f32[100,8192]{1,0:T(8,128)S(1)} custom-call(s32[32,8192]{1,0:T(8,128)S(1)} %get-tuple-element.9.ids_ref.refs_0_, f32[100,8192]{1,0:T(8,128)S(1)} %copy-done, f32[100,512]{1,0:T(8,128)S(1)} %pad_maximum_fusion.refs_0_.refs_2_, f32[100,512]{1,0:T(8,128)S(1)} %collective-permute-done.11.refs_1_.refs_4_), custom_call_target="tpu_custom_call" | custom-call | flops 3355443200 | bytes 3276800 | tf_op jit(solution)/shard_map/apply_values/pallas_call | solution.py:251
  43.1 1.1 %collective-permute-done.10.refs_0_.refs_3_ = f32[100,512]{1,0:T(8,128)S(1)} collective-permute-done((f32[100,512]{1,0:T(8,128)S(1)}, f32[100,512]{1,0:T(8,128)S(1)}, u32[]{:S(2)}, u32[]{:S(2)}) %collective-permute-start.10) | collective-permute-done | bytes 204832 | tf_op jit(solution)/shard_map/ppermute | solution.py:328
  44.2 0.9 %collective-permute-start.12 = (f32[100,512]{1,0:T(8,128)S(1)}, f32[100,512]{1,0:T(8,128)S(1)}, u32[]{:S(2)}, u32[]{:S(2)}) collective-permute-start(f32[100,512]{1,0:T(8,128)S(1)} %collective-permute-done.10.refs_0_.refs_3_), channel_id=1, source_target_pairs={{0,4},{1,5},{2,6},{3,7},{4,0},{5,1},{6,2},{7,3},{8,12},{9,13},{10,... | collective-permute-start | bytes 614408 | tf_op jit(solution)/shard_map/ppermute | solution.py:328
  45.2 1.4 %apply_values.3.refs_1_ = f32[100,8192]{1,0:T(8,128)S(1)} custom-call(s32[32,8192]{1,0:T(8,128)S(1)} %get-tuple-element.9.ids_ref.refs_0_, f32[100,8192]{1,0:T(8,128)S(1)} %apply_values.2.carried_ref, f32[100,512]{1,0:T(8,128)S(1)} %collective-permute-done.10.refs_0_.refs_3_), custom_call_target="tpu_custom_call" | custom-call | flops 1677721600 | bytes 3276800 | tf_op jit(solution)/shard_map/apply_values/pallas_call | solution.py:251
  46.5 0.0 collective-permute-done.12.refs_5_
  46.6 2.3 %apply_last_values.1 = (f32[100,8192]{1,0:T(8,128)}, f32[100,512]{1,0:T(8,128)}) custom-call(s32[32,8192]{1,0:T(8,128)S(1)} %get-tuple-element.9.ids_ref.refs_0_, f32[100,8192]{1,0:T(8,128)S(1)} %apply_values.3.refs_1_, f32[100,512]{1,0:T(8,128)S(1)} %pad_maximum_fusion.refs_0_.refs_2_, f32[100,512]{1,0:T(8,128)S(1)} %collective-permute-done.10.refs_0_.refs_3_, ...), custom_call_target="tpu_custom_call" | custom-call | flops 1677721600 | bytes 3276800 | tf_op jit(solution)/shard_map/apply_last_values/pallas_call | solution.py:301
  (3 shorter events, 0.1 us)
Async XLA Ops:
  5.8 2.5 %collective-permute-start = (f32[200,512]{1,0:T(8,128)S(1)}, f32[200,512]{1,0:T(8,128)S(1)}, u32[]{:S(2)}, u32[]{:S(2)}) collective-permute-start(f32[200,512]{1,0:T(8,128)S(1)} %get-tuple-element.11._), channel_id=1, source_target_pairs={{0,4},{1,5},{2,6},{3,7},{4,0},{5,1},{6,2},{7,3},{8,12},{9,13},{10,... | collective-permute-start | bytes 1228808 | tf_op jit(solution)/shard_map/ppermute | solution.py:328
  8.4 8.4 %collective-permute-start.2 = (f32[200,512]{1,0:T(8,128)S(1)}, f32[200,512]{1,0:T(8,128)S(1)}, u32[]{:S(2)}, u32[]{:S(2)}) collective-permute-start(f32[200,512]{1,0:T(8,128)S(1)} %add.45._), channel_id=1, source_target_pairs={{0,8},{1,9},{2,10},{3,11},{4,20},{5,21},{6,22},{7,23},{8,0},{9,1},... | collective-permute-start | bytes 1228808 | tf_op jit(solution)/shard_map/ppermute | solution.py:328
  14.8 25.6 %copy-start = (f32[100,8192]{1,0:T(8,128)S(1)}, f32[100,8192]{1,0:T(8,128)}, u32[]{:S(2)}) copy-start(f32[100,8192]{1,0:T(8,128)} %carried_ref.1) | copy-start | bytes 9830404
  14.8 2.1 %collective-permute-start.1 = (f32[200,512]{1,0:T(8,128)S(1)}, f32[200,512]{1,0:T(8,128)S(1)}, u32[]{:S(2)}, u32[]{:S(2)}) collective-permute-start(f32[200,512]{1,0:T(8,128)S(1)} %get-tuple-element.12._), channel_id=1, source_target_pairs={{0,4},{1,5},{2,6},{3,7},{4,0},{5,1},{6,2},{7,3},{8,12},{9,13},{10,... | collective-permute-start | bytes 1228808 | tf_op jit(solution)/shard_map/ppermute | solution.py:328
  16.9 4.9 %collective-permute-start.3 = (f32[200,128]{1,0:T(8,128)S(1)}, f32[200,128]{1,0:T(8,128)S(1)}, u32[]{:S(2)}, u32[]{:S(2)}) collective-permute-start(f32[200,128]{1,0:T(8,128)S(1)} %get-tuple-element.16), channel_id=1, source_target_pairs={{0,17},{1,16},{2,19},{3,18},{4,13},{5,12},{6,15},{7,14},{8,25},{9,... | collective-permute-start | bytes 307208 | tf_op jit(solution)/shard_map/ppermute | solution.py:328
  19.4 3.8 %collective-permute-start.5 = (f32[200,128]{1,0:T(8,128)S(1)}, f32[200,128]{1,0:T(8,128)S(1)}, u32[]{:S(2)}, u32[]{:S(2)}) collective-permute-start(f32[200,128]{1,0:T(8,128)S(1)} %get-tuple-element.17), channel_id=1, source_target_pairs={{0,16},{1,17},{2,18},{3,19},{4,12},{5,13},{6,14},{7,15},{8,24},{9,... | collective-permute-start | bytes 307208 | tf_op jit(solution)/shard_map/ppermute | solution.py:328
  19.7 4.7 %collective-permute-start.4 = (f32[200,128]{1,0:T(8,128)S(1)}, f32[200,128]{1,0:T(8,128)S(1)}, u32[]{:S(2)}, u32[]{:S(2)}) collective-permute-start(f32[200,128]{1,0:T(8,128)S(1)} %get-tuple-element.18), channel_id=1, source_target_pairs={{0,1},{1,0},{2,3},{3,2},{4,5},{5,4},{6,7},{7,6},{8,9},{9,8},{10,11... | collective-permute-start | bytes 307208 | tf_op jit(solution)/shard_map/ppermute | solution.py:328
  24.5 6.1 %collective-permute-start.6 = (f32[200,128]{1,0:T(8,128)S(1)}, f32[200,128]{1,0:T(8,128)S(1)}, u32[]{:S(2)}, u32[]{:S(2)}) collective-permute-start(f32[200,128]{1,0:T(8,128)S(1)} %fusion.2), channel_id=1, source_target_pairs={{0,2},{1,3},{2,0},{3,1},{4,6},{5,7},{6,4},{7,5},{8,10},{9,11},{10,... | collective-permute-start | bytes 307208 | tf_op jit(solution)/shard_map/ppermute | solution.py:328
  30.6 3.9 %collective-permute-start.9 = (f32[100,128]{1,0:T(8,128)S(1)}, f32[100,128]{1,0:T(8,128)S(1)}, u32[]{:S(2)}, u32[]{:S(2)}) collective-permute-start(f32[100,128]{1,0:T(8,128)S(1)} %fusion.3), channel_id=1, source_target_pairs={{0,17},{1,16},{2,19},{3,18},{4,13},{5,12},{6,15},{7,14},{8,25},{9,... | collective-permute-start | bytes 153608 | tf_op jit(solution)/shard_map/ppermute | solution.py:328
  30.7 3.9 %collective-permute-start.8 = (f32[100,128]{1,0:T(8,128)S(1)}, f32[100,128]{1,0:T(8,128)S(1)}, u32[]{:S(2)}, u32[]{:S(2)}) collective-permute-start(f32[100,128]{1,0:T(8,128)S(1)} %fusion.3), channel_id=1, source_target_pairs={{0,16},{1,17},{2,18},{3,19},{4,12},{5,13},{6,14},{7,15},{8,24},{9,... | collective-permute-start | bytes 153608 | tf_op jit(solution)/shard_map/ppermute | solution.py:328
  31.6 3.2 %collective-permute-start.7 = (f32[100,128]{1,0:T(8,128)S(1)}, f32[100,128]{1,0:T(8,128)S(1)}, u32[]{:S(2)}, u32[]{:S(2)}) collective-permute-start(f32[100,128]{1,0:T(8,128)S(1)} %fusion.3), channel_id=1, source_target_pairs={{0,1},{1,0},{2,3},{3,2},{4,5},{5,4},{6,7},{7,6},{8,9},{9,8},{10,11... | collective-permute-start | bytes 153608 | tf_op jit(solution)/shard_map/ppermute | solution.py:328
  34.9 5.5 %collective-permute-start.11 = (f32[100,512]{1,0:T(8,128)S(1)}, f32[100,512]{1,0:T(8,128)S(1)}, u32[]{:S(2)}, u32[]{:S(2)}) collective-permute-start(f32[100,512]{1,0:T(8,128)S(1)} %pad_maximum_fusion.refs_0_.refs_2_), channel_id=1, source_target_pairs={{0,4},{1,5},{2,6},{3,7},{4,0},{5,1},{6,2},{7,3},{8,12},{9,13},{10,... | collective-permute-start | bytes 614408 | tf_op jit(solution)/shard_map/ppermute | solution.py:328
  39.2 5.0 %collective-permute-start.10 = (f32[100,512]{1,0:T(8,128)S(1)}, f32[100,512]{1,0:T(8,128)S(1)}, u32[]{:S(2)}, u32[]{:S(2)}) collective-permute-start(f32[100,512]{1,0:T(8,128)S(1)} %pad_maximum_fusion.refs_0_.refs_2_), channel_id=1, source_target_pairs={{0,8},{1,9},{2,10},{3,11},{4,20},{5,21},{6,22},{7,23},{8,0},{9,1},... | collective-permute-start | bytes 614408 | tf_op jit(solution)/shard_map/ppermute | solution.py:328
  44.2 2.3 %collective-permute-start.12 = (f32[100,512]{1,0:T(8,128)S(1)}, f32[100,512]{1,0:T(8,128)S(1)}, u32[]{:S(2)}, u32[]{:S(2)}) collective-permute-start(f32[100,512]{1,0:T(8,128)S(1)} %collective-permute-done.10.refs_0_.refs_3_), channel_id=1, source_target_pairs={{0,4},{1,5},{2,6},{3,7},{4,0},{5,1},{6,2},{7,3},{8,12},{9,13},{10,... | collective-permute-start | bytes 614408 | tf_op jit(solution)/shard_map/ppermute | solution.py:328
